TPU v7x, 32 devices: a whole 2x2x4 slice. The times are simulated.
32 devices in a mesh: fsdp: 4 (over z), ctx: 4 (over y, x), tp: 2 (over core).
Axes of the slice: x: 2, y: 2, z: 4, core: 2. Of those that a mesh axis runs over, the one named last changes fastest.
Arguments:
- layer_input: bfloat16 [4, 1024, 896], P('fsdp', 'ctx'), may hold values from -6 to 6
- segments: int32 [4, 1024], P('fsdp', 'ctx'), may hold values from 0 to 2, as said below
- positions: int32 [4, 1024], P('fsdp', 'ctx'), may hold values from 0 to 2046, as said below
- attn_gain: float32 [896], replicated, may hold values from 0.5 to 1.5
- w_q: bfloat16 [896, 896], P(('fsdp', 'ctx'), 'tp'), may hold values from -0.1875 to 0.1875
- b_q: float32 [896], P('tp'), may hold values from -3 to 3
- w_k: bfloat16 [896, 128], P(('fsdp', 'ctx'), 'tp'), may hold values from -0.1875 to 0.1875
- b_k: float32 [128], P('tp'), may hold values from -3 to 3
- w_v: bfloat16 [896, 128], P(('fsdp', 'ctx'), 'tp'), may hold values from -0.1875 to 0.1875
- b_v: float32 [128], P('tp'), may hold values from -3 to 3
- w_o: bfloat16 [896, 896], P('tp', ('fsdp', 'ctx')), may hold values from -6 to 6
- mlp_gain: float32 [896], replicated, may hold values from 0.5 to 1.5
- w_gate: bfloat16 [896, 4864], P(('fsdp', 'ctx'), 'tp'), may hold values from -0.1875 to 0.1875
- w_up: bfloat16 [896, 4864], P(('fsdp', 'ctx'), 'tp'), may hold values from -0.1875 to 0.1875
- w_down: bfloat16 [4864, 896], P('tp', ('fsdp', 'ctx')), may hold values from -0.078125 to 0.078125
- cotangent: bfloat16 [4, 1024, 896], P('fsdp', 'ctx'), may hold values from -6 to 6
Outputs:
- result: bfloat16 [4, 1024, 896], P('fsdp', 'ctx')
- grad_input: bfloat16 [4, 1024, 896], P('fsdp', 'ctx')
- grad_attn_gain: float32 [896], replicated
- grad_w_q: float32 [896, 896], P(('fsdp', 'ctx'), 'tp')
- grad_b_q: float32 [896], P('tp')
- grad_w_k: float32 [896, 128], P(('fsdp', 'ctx'), 'tp')
- grad_b_k: float32 [128], P('tp')
- grad_w_v: float32 [896, 128], P(('fsdp', 'ctx'), 'tp')
- grad_b_v: float32 [128], P('tp')
- grad_w_o: float32 [896, 896], P('tp', ('fsdp', 'ctx'))
- grad_mlp_gain: float32 [896], replicated
- grad_w_gate: float32 [896, 4864], P(('fsdp', 'ctx'), 'tp')
- grad_w_up: float32 [896, 4864], P(('fsdp', 'ctx'), 'tp')
- grad_w_down: float32 [4864, 896], P('tp', ('fsdp', 'ctx'))
Inputs may be any that keep to these rules, and one draw needn't show every extreme that they name: `segments`: in each row the segment numbers are 0, then 1, then 2, never falling; segment 1 begins within the first 256 positions and ends within the last 256 positions. `positions`: A token's place within its segment plus an offset of that segment.
All inputs are finite; a program needn't handle non-finite values.
Results may differ from a plain program's by a relative error of at most 0.04.
Values may be sent and summed in bfloat16 or wider, within the bound.
No kernel may reach another device: no remote copies, remote signals or barrier semaphores. Data moves between devices by JAX's collectives and lax.ppermute only.
A program may use at most 128 MiB of HBM per device.

v0:
```python
import functools
import math

import jax
import jax.numpy as jnp
from jax import lax
from jax.experimental import pallas as pl
from jax.experimental.pallas import tpu as pltpu
from jax.sharding import PartitionSpec as P

HEAD_DIM = 64


EPS = 1e-06
THETA = 1000000.0
NEG = -1e30

LANES = 128
SPLIT = 512
SMALL_ROWS = 16
VMEM_BYTES = 16 * 2**20
FREE = pl.CostEstimate(flops=0, bytes_accessed=0, transcendentals=0)
IN_VMEM = pl.BlockSpec(memory_space=pltpu.VMEM)
IN_SMEM = pl.BlockSpec(memory_space=pltpu.SMEM)
F32 = jnp.float32
BF = jnp.bfloat16


def dot(left, right):
    return jnp.dot(left, right, preferred_element_type=F32)


def dot_rows(left, right):
    return lax.dot_general(left, right, (((1,), (1,)), ((), ())), preferred_element_type=F32)


def turned_dot(left, right):
    return lax.dot_general(left, right, (((0,), (0,)), ((), ())), preferred_element_type=F32)


def rotate(values, cosines, sines):
    halfway = values.shape[-1] // 2
    turned = jnp.concatenate([-values[..., halfway:], values[..., :halfway]], axis=-1)
    return values * cosines + turned * sines


def angles(positions, head_dim):
    even_steps = jnp.arange(0, head_dim, 2).astype(jnp.float32)
    inverse = jnp.exp(-math.log(THETA) * even_steps / head_dim)
    phases = positions.astype(jnp.float32)[..., None] * inverse
    phases = jnp.concatenate([phases, phases], axis=-1)
    return (jnp.cos(phases)[..., None, :], jnp.sin(phases)[..., None, :])


def flips(size, step):
    return [(index, index ^ step) for index in range(size)]


def swap_cores(values):
    return lax.ppermute(values, "tp", flips(lax.axis_size("tp"), 1))


def few():
    return lax.axis_size("ctx") <= 8


def peers():
    size = lax.axis_size("ctx")
    if few():
        return [lax.axis_index("ctx") ^ step for step in range(size)]
    return list(range(size))


def spread(values):
    size = lax.axis_size("ctx")
    if not few():
        return list(lax.all_gather(values, "ctx"))
    return [values] + [lax.ppermute(values, "ctx", flips(size, step)) for step in range(1, size)]


def trade(parts):
    size = lax.axis_size("ctx")
    if not few():
        return list(lax.all_to_all(jnp.stack(parts), "ctx", 0, 0))
    return [parts[0]] + [
        lax.ppermute(parts[step], "ctx", flips(size, step)) for step in range(1, size)
    ]


def untangle(parts):
    if not few():
        return jnp.stack(parts)
    own = lax.axis_index("ctx")
    whole = jnp.stack(parts)
    return jnp.stack(
        [lax.dynamic_index_in_dim(whole, own ^ place, 0, keepdims=False) for place in range(len(parts))]
    )


def choose(whole):
    if not few():
        return list(whole)
    return [lax.dynamic_index_in_dim(whole, peer, 0, keepdims=False) for peer in peers()]


def after(values, *earlier):
    return lax.optimization_barrier((values,) + earlier)[0]


def direct_gather(values):
    size = lax.axis_size("fsdp")
    own = lax.axis_index("fsdp")
    pieces = [values] + [
        lax.ppermute(values, "fsdp", [(index, (index + step) % size) for index in range(size)])
        for step in range(1, size)
    ]
    pieces = pieces[::-1]
    line = jnp.stack(pieces + pieces[:-1])
    return lax.dynamic_slice_in_dim(line, size - 1 - own, size, 0)


def send_up(values, step):
    size = lax.axis_size("fsdp")
    return lax.ppermute(values, "fsdp", [(index, (index + step) % size) for index in range(size)])


def line_steps():
    size = lax.axis_size("fsdp")
    ups = [(index, index + 1) for index in range(size - 1)]
    downs = [(index + 1, index) for index in range(size - 1)]
    return ups, downs


def gather_step(line, step):
    ups, downs = line_steps()
    return (
        [lax.ppermute(line[0], "fsdp", ups[step:])]
        + line
        + [lax.ppermute(line[-1], "fsdp", downs[: len(downs) - step])]
    )


def gather_end(line):
    size = lax.axis_size("fsdp")
    return lax.dynamic_slice_in_dim(
        jnp.stack(line), size - 1 - lax.axis_index("fsdp"), size, 0
    )


def scatter_step(whole, sums, step):
    size = lax.axis_size("fsdp")
    own = lax.axis_index("fsdp")
    ups, downs = line_steps()
    pieces = [
        lax.dynamic_index_in_dim(whole, place, 0, keepdims=False)
        for place in (own + size - step, own - size + step)
    ]
    if sums:
        pieces = [piece + part for piece, part in zip(pieces, sums)]
    return [
        lax.ppermute(pieces[0], "fsdp", ups[:step]),
        lax.ppermute(pieces[1], "fsdp", downs[size - 1 - step :]),
    ]


def scatter_end(whole, sums):
    own = lax.dynamic_index_in_dim(whole, lax.axis_index("fsdp"), 0, keepdims=False)
    return sum(part.astype(F32) for part in [own] + sums)


def gather_half(values):
    half = values.shape[0] // 2
    return jnp.concatenate(
        spread(lax.dynamic_slice_in_dim(values, lax.axis_index("tp") * half, half, 0))
    )


def add_cores(mine, other):
    return (mine.astype(jnp.float32) + swap_cores(other).astype(jnp.float32)).astype(jnp.bfloat16)


def join_tokens(parts):
    own = sum(part.astype(jnp.float32) for part in parts).astype(jnp.bfloat16)
    other = swap_cores(own)
    first = lax.axis_index("tp") == 0
    return jnp.where(
        first, jnp.concatenate([own, other]), jnp.concatenate([other, own])
    ).astype(jnp.float32)


def turn_back(values, cosines, sines, sign):
    half = cosines.shape[0]
    parts = []
    for begin in range(0, values.shape[0], 2 * half):
        first = values[begin : begin + half]
        second = values[begin + half : begin + 2 * half]
        parts += [first * cosines - second * (sign * sines), second * cosines + first * (sign * sines)]
    return jnp.concatenate(parts)


def project_kernel(
    width_q, width_k, input_ref, gain_ref, w_ref, b_ref, cos_ref, sin_ref, seg_ref, q_ref, kv_ref
):
    inputs = input_ref[...].astype(F32)
    scale = lax.rsqrt(jnp.mean(inputs * inputs, -1, keepdims=True) + EPS)
    normed = (inputs * scale * gain_ref[...]).astype(BF)
    projected = dot(normed, w_ref[...]) + b_ref[...]
    rotated = turn_back(projected[:, : width_q + width_k].T, cos_ref[...], sin_ref[...], 1.0).T
    q_ref[...] = rotated[:, :width_q].astype(BF)
    tokens = q_ref.shape[0]
    kv_ref[:tokens, :width_k] = rotated[:, width_q:].astype(BF)
    kv_ref[:tokens, width_k:] = projected[:, width_q + width_k :].astype(BF)
    number = lax.broadcasted_iota(jnp.int32, (SMALL_ROWS, kv_ref.shape[1]), 0)
    counts = jnp.zeros(number.shape, F32)
    for row in range(2):
        below = jnp.sum((seg_ref[...] <= row).astype(F32), -1, keepdims=True)
        counts = jnp.where(number == row, below, counts)
    kv_ref[tokens:, :] = counts.astype(BF)


def project(inputs, gain, weights, biases, cosines, sines, segments, width_q, width_k):
    tokens = inputs.shape[0]
    return pl.pallas_call(
        functools.partial(project_kernel, width_q, width_k),
        out_shape=(
            jax.ShapeDtypeStruct((tokens, width_q), BF),
            jax.ShapeDtypeStruct((tokens + SMALL_ROWS, 2 * width_k), BF),
        ),
        in_specs=[IN_VMEM] * 7,
        out_specs=(IN_VMEM,) * 2,
        compiler_params=pltpu.CompilerParams(vmem_limit_bytes=VMEM_BYTES),
        cost_estimate=FREE,
        name="project",
    )(inputs, gain, weights, biases, cosines, sines, segments)


def key_grads_kernel(count, q_ref, w_ref, cos_ref, sin_ref, *refs):
    parts, qkv_ref, normed_ref = refs[:count], refs[count], refs[count + 1]
    width_q = q_ref.shape[1]
    total = sum(ref[...].astype(F32) for ref in parts)
    width_k = total.shape[1] // 2
    keys = turn_back(total[:, :width_k].T, cos_ref[...], sin_ref[...], -1.0).T
    qkv_ref[:, :width_q] = q_ref[...]
    qkv_ref[:, width_q : width_q + width_k] = keys.astype(BF)
    qkv_ref[:, width_q + width_k :] = total[:, width_k:].astype(BF)
    normed_ref[...] = dot_rows(qkv_ref[...], w_ref[...]).astype(BF)


def key_grads(grad_query, weights, cosines, sines, parts):
    tokens = grad_query.shape[0]
    features, width = weights.shape
    return pl.pallas_call(
        functools.partial(key_grads_kernel, len(parts)),
        out_shape=(
            jax.ShapeDtypeStruct((tokens, width), BF),
            jax.ShapeDtypeStruct((tokens, features), BF),
        ),
        in_specs=[IN_VMEM] * (4 + len(parts)),
        out_specs=(IN_VMEM,) * 2,
        compiler_params=pltpu.CompilerParams(vmem_limit_bytes=VMEM_BYTES),
        cost_estimate=FREE,
        name="key_grads",
    )(grad_query, weights, cosines, sines, *parts)


def masks(start, tokens, own, step):
    peer = own ^ step
    key = peer*tokens + lax.broadcasted_iota(jnp.int32,(tokens,tokens),0)
    query = own*tokens + lax.broadcasted_iota(jnp.int32,(tokens,tokens),1)
    return jnp.where((key>=start)&(key<=query),0.0,NEG).astype(F32)

def fwd_kernel(count, own_ref, q_ref, seg_ref, *refs):
    kv_refs=refs[:count]; att_ref, att_t_ref, lse_ref, start_ref, bias, s_ref = refs[count:]
    own=own_ref[0]
    tokens=q_ref.shape[0]; heads=q_ref.shape[1]//HEAD_DIM
    counts=sum(r[tokens:,:].astype(F32) for r in kv_refs).astype(jnp.int32)
    seg=seg_ref[...]
    start=jnp.where(seg==0,0,jnp.where(seg==1,counts[0:1,0:1],counts[1:2,0:1]))
    start_ref[...]=start
    for step in range(count):
        bias[step*tokens:(step+1)*tokens,:]=masks(start,tokens,own,step)
    q=q_ref[...]*jnp.asarray(HEAD_DIM**-0.5,BF)
    ks=[r[:tokens,:HEAD_DIM] for r in kv_refs]
    vts=[r[:tokens,HEAD_DIM:].astype(F32).T.astype(BF) for r in kv_refs]
    for h in range(heads):
        qh=q[:,h*HEAD_DIM:(h+1)*HEAD_DIM]
        peak=jnp.full((1,tokens),NEG,F32)
        for step in range(count):
            rows=slice(step*tokens,(step+1)*tokens)
            s=dot_rows(ks[step],qh)+bias[rows,:]
            s_ref[h%2,rows,:]=s
            peak=jnp.maximum(peak,jnp.max(s,0,keepdims=True))
        total=jnp.zeros((1,tokens),F32)
        out=jnp.zeros((HEAD_DIM,tokens),F32)
        for step in range(count):
            rows=slice(step*tokens,(step+1)*tokens)
            p=jnp.exp(s_ref[h%2,rows,:]-peak)
            total=total+jnp.sum(p,0,keepdims=True)
            out=out+dot(vts[step],p.astype(BF))
        att_t_ref[h*HEAD_DIM:(h+1)*HEAD_DIM,:]=out/total
        lse_ref[h:h+1,:]=peak+jnp.log(total)
    att_ref[...]=att_t_ref[...].T.astype(BF)

def attend_fwd(own, q, segments, kvs):
    tokens,width=q.shape; heads=width//HEAD_DIM; n=len(kvs)
    return pl.pallas_call(functools.partial(fwd_kernel,n),
        out_shape=(jax.ShapeDtypeStruct((tokens,width),BF),jax.ShapeDtypeStruct((width,tokens),F32),jax.ShapeDtypeStruct((heads,tokens),F32),jax.ShapeDtypeStruct((1,tokens),jnp.int32)),
        in_specs=[IN_SMEM]+[IN_VMEM]*(2+n), out_specs=(IN_VMEM,)*4,
        scratch_shapes=[pltpu.VMEM((n*tokens,tokens),F32),pltpu.VMEM((2,n*tokens,tokens),F32)],
        compiler_params=pltpu.CompilerParams(vmem_limit_bytes=VMEM_BYTES),
        cost_estimate=FREE, name="attend_forward")(own,q,segments,*kvs)

def bwd_kernel(
    count, own_ref, q_ref, start_ref, att_t_ref, lse_ref, gb_ref, wo_ref, cos_ref, sin_ref, *refs
):
    kv_refs=refs[:count]; gq_ref=refs[count]; gkv_refs=refs[count+1:2*count+1]; bias, gqt, dkv = refs[2*count+1:]
    own=own_ref[0]
    tokens=q_ref.shape[0]; heads=q_ref.shape[1]//HEAD_DIM
    start=start_ref[...]
    do=dot(gb_ref[...],wo_ref[...])
    do_low=do.astype(BF)
    do_t=do_low.astype(F32).T
    prod=do_t*att_t_ref[...]
    q=q_ref[...]
    qs=q*jnp.asarray(HEAD_DIM**-0.5,BF)
    ks=[r[:tokens,:HEAD_DIM] for r in kv_refs]
    vs=[r[:tokens,HEAD_DIM:] for r in kv_refs]
    kts=[k.astype(F32).T.astype(BF) for k in ks]
    dot_low=do_t.astype(BF)
    for step in range(count):
        bias[...]=masks(start,tokens,own,step)
        dk=jnp.zeros((tokens,HEAD_DIM),F32); dv=jnp.zeros((tokens,HEAD_DIM),F32)
        for h in range(heads):
            cols=slice(h*HEAD_DIM,(h+1)*HEAD_DIM)
            qh=qs[:,cols]; doh=do_low[:,cols]
            rowdot=jnp.sum(prod[cols,:],0,keepdims=True)
            p=jnp.exp(dot_rows(ks[step],qh)+(bias[...]-lse_ref[h:h+1,:]))
            dp=dot_rows(vs[step],doh)
            ds=(p*(dp-rowdot)).astype(BF)
            dv=dv+dot(p.astype(BF),doh)
            dk=dk+dot(ds,qh)
            dq=dot(kts[step],ds)
            if step==0: gqt[cols,:]=dq
            else: gqt[cols,:]+=dq
        gkv_refs[step][:,:HEAD_DIM]=dk.astype(BF)
        gkv_refs[step][:,HEAD_DIM:]=dv.astype(BF)
    turned=turn_back(gqt[...]*(HEAD_DIM**-0.5),cos_ref[...],sin_ref[...],-1.0)
    gq_ref[...]=turned.T.astype(BF)

def attend_bwd(own,q,start,att_t,lse,gb,wo,cosines,sines,kvs):
    tokens,width=q.shape; n=len(kvs)
    outs=pl.pallas_call(functools.partial(bwd_kernel,n),
        out_shape=(jax.ShapeDtypeStruct((tokens,width),BF),)+(jax.ShapeDtypeStruct((tokens,2*HEAD_DIM),BF),)*n,
        in_specs=[IN_SMEM]+[IN_VMEM]*(8+n), out_specs=(IN_VMEM,)*(n+1),
        scratch_shapes=[pltpu.VMEM((tokens,tokens),F32),pltpu.VMEM((width,tokens),F32),pltpu.VMEM((8,128),F32)],
        compiler_params=pltpu.CompilerParams(vmem_limit_bytes=VMEM_BYTES),
        cost_estimate=FREE, name="attend_backward")(own,q,start,att_t,lse,gb,wo,cosines,sines,*kvs)
    return outs[0],list(outs[1:])


def prepare_kernel(count, chunk, own_ref, gate_ref, up_ref, down_ref, *refs):
    pieces, wide = refs[:count], refs[count]
    rows, hidden = gate_ref.shape
    span = chunk * count
    for number in range(3):
        wide[number, :, :hidden] = (gate_ref, up_ref, down_ref)[number][...]
        if span > hidden:
            wide[number, :, hidden:] = jnp.zeros((rows, span - hidden), BF)
    for step in range(count):
        begin = pl.multiple_of((own_ref[0] ^ step) * chunk, LANES)
        for number in range(3):
            pieces[step][:, number * chunk : (number + 1) * chunk] = wide[
                number, :, pl.ds(begin, chunk)
            ]


def prepare(own, w_gate, w_up, w_down, count, chunk):
    rows = w_gate.shape[0]
    outs = pl.pallas_call(
        functools.partial(prepare_kernel, count, chunk),
        out_shape=(jax.ShapeDtypeStruct((rows, 3 * chunk), BF),) * count,
        in_specs=[IN_SMEM] + [IN_VMEM] * 3,
        out_specs=(IN_VMEM,) * count,
        scratch_shapes=[pltpu.VMEM((3, rows, chunk * count), BF)],
        compiler_params=pltpu.CompilerParams(vmem_limit_bytes=VMEM_BYTES),
        cost_estimate=FREE,
        name="prepare",
    )(own, w_gate, w_up, w_down)
    return list(outs)


def weight_grad_kernel(count, lines, own_ref, left_ref, right_ref, *refs):
    pieces, whole = refs[:count], refs[count]
    whole[...] = turned_dot(left_ref[...], right_ref[...])
    rows = whole.shape[0] // (count * lines)
    for step in range(count):
        peer = own_ref[0] ^ step
        parts = []
        for line in range(lines):
            begin = pl.multiple_of((line * count + peer) * rows, 8)
            parts.append(whole[pl.ds(begin, rows), :])
        pieces[step][...] = jnp.concatenate(parts).astype(BF)


def weight_grad(own, left, right, count, lines):
    height, width = left.shape[1], right.shape[1]
    return list(
        pl.pallas_call(
            functools.partial(weight_grad_kernel, count, lines),
            out_shape=(jax.ShapeDtypeStruct((height // count, width), BF),) * count,
            in_specs=[IN_SMEM] + [IN_VMEM] * 2,
            out_specs=(IN_VMEM,) * count,
            scratch_shapes=[pltpu.VMEM((height, width), F32)],
            compiler_params=pltpu.CompilerParams(vmem_limit_bytes=VMEM_BYTES),
            cost_estimate=FREE,
            name="weight_grad",
        )(own, left, right)
    )


def last_grads_kernel(
    count, lines, own_ref, input_ref, gain_ref, qkv_ref, first_ref, second_ref, middle_ref,
    mlp_ref, out_ref, *refs
):
    pieces, whole, small = refs[:count], refs[count], refs[count + 1]
    features = input_ref.shape[1]
    inputs = input_ref[...].astype(F32)
    scale = lax.rsqrt(jnp.mean(inputs * inputs, -1, keepdims=True) + EPS)
    unit = inputs * scale
    gain = gain_ref[...]
    qkv = qkv_ref[...]
    whole[...] = turned_dot((unit * gain).astype(BF), qkv)
    grad = first_ref[...].astype(F32) + second_ref[...].astype(F32)
    turned = grad * unit
    small[...] = jnp.zeros_like(small)
    small[0:1, :] = jnp.sum(qkv.astype(F32), 0, keepdims=True)
    for row, values in ((1, jnp.sum(turned, 0, keepdims=True)), (3, mlp_ref[...])):
        small[row : row + 1, :SPLIT] = values[:, :SPLIT]
        small[row + 1 : row + 2, : features - SPLIT] = values[:, SPLIT:]
    along = jnp.mean(turned * gain, -1, keepdims=True)
    out_ref[...] = (middle_ref[...] + scale * (grad * gain - unit * along)).astype(BF)
    rows = features // (count * lines)
    for step in range(count):
        peer = own_ref[0] ^ step
        parts = []
        for line in range(lines):
            begin = pl.multiple_of((line * count + peer) * rows, 8)
            parts.append(whole[pl.ds(begin, rows), :])
        pieces[step][...] = jnp.concatenate(parts + [small[...]]).astype(BF)


def last_grads(own, inputs, gain, qkv, first, second, middle, mlp_gain_grad, count, lines):
    tokens, features = inputs.shape
    width = qkv.shape[1]
    outs = pl.pallas_call(
        functools.partial(last_grads_kernel, count, lines),
        out_shape=(jax.ShapeDtypeStruct((tokens, features), BF),)
        + (jax.ShapeDtypeStruct((features // count + SMALL_ROWS, width), BF),) * count,
        in_specs=[IN_SMEM] + [IN_VMEM] * 7,
        out_specs=(IN_VMEM,) * (count + 1),
        scratch_shapes=[pltpu.VMEM((features, width), F32), pltpu.VMEM((SMALL_ROWS, width), F32)],
        compiler_params=pltpu.CompilerParams(vmem_limit_bytes=VMEM_BYTES),
        cost_estimate=FREE,
        name="last_grads",
    )(own, inputs, gain, qkv, first, second, middle, mlp_gain_grad)
    return outs[0], list(outs[1:])


def pack_kernel(count, lines, own_ref, *refs):
    qkv_refs, o_refs = refs[:count], refs[count : 2 * count]
    outs = refs[2 * count : 2 * count + lines]
    qkv_sum, o_sum, block = refs[2 * count + lines :]
    qkv_sum[...] = sum(ref[...].astype(F32) for ref in qkv_refs)
    o_sum[...] = sum(ref[...].astype(F32) for ref in o_refs)
    rows = o_sum.shape[0] // lines
    width = qkv_sum.shape[1]
    block[rows:, :] = jnp.zeros((SMALL_ROWS, block.shape[1]), F32)
    block[rows:, :width] = qkv_sum[lines * rows :, :]
    for step in range(lines):
        begin = pl.multiple_of(lax.rem(own_ref[0] + step, lines) * rows, 8)
        block[:rows, :width] = qkv_sum[pl.ds(begin, rows), :]
        block[:rows, width:] = o_sum[pl.ds(begin, rows), :]
        outs[step][...] = block[...].astype(BF)


def pack(own_line, qkv_parts, o_parts, lines):
    count = len(qkv_parts)
    width, width_o = qkv_parts[0].shape[1], o_parts[0].shape[1]
    rows = o_parts[0].shape[0] // lines
    shape = (rows + SMALL_ROWS, width + width_o)
    return list(
        pl.pallas_call(
            functools.partial(pack_kernel, count, lines),
            out_shape=(jax.ShapeDtypeStruct(shape, BF),) * lines,
            in_specs=[IN_SMEM] + [IN_VMEM] * (2 * count),
            out_specs=(IN_VMEM,) * lines,
            scratch_shapes=[
                pltpu.VMEM(qkv_parts[0].shape, F32),
                pltpu.VMEM(o_parts[0].shape, F32),
                pltpu.VMEM(shape, F32),
            ],
            compiler_params=pltpu.CompilerParams(vmem_limit_bytes=VMEM_BYTES),
            cost_estimate=FREE,
            name="pack",
        )(own_line, *qkv_parts, *o_parts)
    )


def unpack_kernel(lines, widths, *refs):
    parts = refs[:lines]
    q_ref, k_ref, v_ref, o_ref, bq_ref, bk_ref, bv_ref, attn_ref, mlp_ref, total = refs[lines:]
    total[...] = sum(ref[...].astype(F32) for ref in parts)
    rows = q_ref.shape[0]
    first, second = widths[0], widths[0] + widths[1]
    third = second + widths[1]
    q_ref[...] = total[:rows, :first]
    k_ref[...] = total[:rows, first:second]
    v_ref[...] = total[:rows, second:third]
    o_ref[...] = total[:rows, third:]
    bq_ref[...] = total[rows : rows + 1, :first]
    bk_ref[...] = total[rows : rows + 1, first:second]
    bv_ref[...] = total[rows : rows + 1, second:third]
    for row, ref in ((rows + 1, attn_ref), (rows + 3, mlp_ref)):
        ref[:, :SPLIT] = total[row : row + 1, :SPLIT]
        ref[:, SPLIT:] = total[row + 1 : row + 2, : ref.shape[1] - SPLIT]


def unpack(parts, features, width_q, width_k):
    rows, width = parts[0].shape
    rows -= SMALL_ROWS
    width_o = width - width_q - 2 * width_k
    shapes = [
        (rows, width_q), (rows, width_k), (rows, width_k), (rows, width_o),
        (1, width_q), (1, width_k), (1, width_k), (1, features), (1, features),
    ]
    return pl.pallas_call(
        functools.partial(unpack_kernel, len(parts), (width_q, width_k)),
        out_shape=tuple(jax.ShapeDtypeStruct(shape, F32) for shape in shapes),
        in_specs=[IN_VMEM] * len(parts),
        out_specs=(IN_VMEM,) * len(shapes),
        scratch_shapes=[pltpu.VMEM(parts[0].shape, F32)],
        compiler_params=pltpu.CompilerParams(vmem_limit_bytes=VMEM_BYTES),
        cost_estimate=FREE,
        name="unpack",
    )(*parts)


def mlp_out_kernel(count, chunk, own_ref, *refs):
    parts = refs[:count]
    gate_ref, up_ref, down_ref, wide = refs[count:]
    rows, hidden = gate_ref.shape
    for step in range(count):
        begin = pl.multiple_of((own_ref[0] ^ step) * chunk, LANES)
        for number in range(3):
            wide[number, :, pl.ds(begin, chunk)] = parts[step][
                :, number * chunk : (number + 1) * chunk
            ].astype(F32)
    for number, ref in enumerate((gate_ref, up_ref, down_ref)):
        ref[...] = wide[number, :, :hidden]


def mlp_out(own, parts, hidden):
    count = len(parts)
    rows, width = parts[0].shape
    chunk = width // 3
    return pl.pallas_call(
        functools.partial(mlp_out_kernel, count, chunk),
        out_shape=(jax.ShapeDtypeStruct((rows, hidden), F32),) * 3,
        in_specs=[IN_SMEM] + [IN_VMEM] * count,
        out_specs=(IN_VMEM,) * 3,
        scratch_shapes=[pltpu.VMEM((3, rows, chunk * count), F32)],
        compiler_params=pltpu.CompilerParams(vmem_limit_bytes=VMEM_BYTES),
        cost_estimate=FREE,
        name="mlp_out",
    )(own, *parts)


def score_block(query_groups, key_rows, key_index, start, query_index):
    head_dim = query_groups.shape[-1]
    logits = jnp.einsum(
        "qgjd,kgd->gjqk", query_groups, key_rows, preferred_element_type=jnp.float32
    ) * head_dim ** (-0.5)
    allowed = (key_index[None, :] >= start[:, None]) & (key_index[None, :] <= query_index[:, None])
    return jnp.where(allowed, logits, NEG)


def key_window(keyval_all, number, key_block, key_heads):
    window = lax.dynamic_slice_in_dim(keyval_all, number * key_block, key_block, 0)
    width = window.shape[1] // 2
    key_rows = window[:, :width].reshape(key_block, key_heads, width // key_heads)
    value_rows = window[:, width:].reshape(key_block, key_heads, width // key_heads)
    key_index = number * key_block + jnp.arange(key_block, dtype=jnp.int32)
    return key_rows, value_rows, key_index


def repeat(count, step, state):
    if count == 1:
        return step(0, state)
    return lax.fori_loop(0, count, step, state)


def attend(query_rot, keyval_all, start, query_index, key_heads):
    tokens, head_count, head_dim = query_rot.shape
    group_size = head_count // key_heads
    key_block = min(keyval_all.shape[0], 1024)
    query_groups = query_rot.reshape(tokens, key_heads, group_size, head_dim)
    block_count = keyval_all.shape[0] // key_block

    def measure(number, state_pair):
        running_peak, running_total = state_pair
        key_rows, value_rows, key_index = key_window(
            keyval_all, number, key_block, key_heads
        )
        masked = score_block(query_groups, key_rows, key_index, start, query_index)
        fresh = jnp.maximum(running_peak, jnp.max(masked, -1))
        running_total = running_total * jnp.exp(running_peak - fresh) + jnp.sum(
            jnp.exp(masked - fresh[..., None]), -1
        )
        return (fresh, running_total)

    start_state = (
        jnp.full((key_heads, group_size, tokens), NEG, jnp.float32),
        jnp.zeros((key_heads, group_size, tokens), jnp.float32),
    )
    running_peak, running_total = repeat(block_count, measure, start_state)
    log_total = running_peak + jnp.log(running_total)

    def collect(number, summed):
        key_rows, value_rows, key_index = key_window(
            keyval_all, number, key_block, key_heads
        )
        masked = score_block(query_groups, key_rows, key_index, start, query_index)
        chances = jnp.exp(masked - log_total[..., None]).astype(jnp.bfloat16)
        return summed + jnp.einsum(
            "gjqk,kgd->gjqd", chances, value_rows, preferred_element_type=jnp.float32
        )

    summed = repeat(
        block_count, collect, jnp.zeros((key_heads, group_size, tokens, head_dim), jnp.float32)
    )
    return (summed.transpose(2, 0, 1, 3).reshape(tokens, head_count * head_dim), log_total)


def attend_back(
    query_rot,
    keyval_all,
    start,
    query_index,
    key_heads,
    log_total,
    attended,
    grad_attended,
):
    tokens, head_count, head_dim = query_rot.shape
    group_size = head_count // key_heads
    key_block = min(keyval_all.shape[0], 1024)
    query_groups = query_rot.reshape(tokens, key_heads, group_size, head_dim)
    grad_groups = grad_attended.reshape(tokens, key_heads, group_size, head_dim)
    block_count = keyval_all.shape[0] // key_block
    row_dot = jnp.sum(
        (grad_attended.astype(jnp.float32) * attended).reshape(
            tokens, key_heads, group_size, head_dim
        ),
        -1,
    ).transpose(1, 2, 0)
    score_scale = head_dim ** (-0.5)

    def step_back(number, state_pair):
        grad_query, grad_keyval = state_pair
        key_rows, value_rows, key_index = key_window(
            keyval_all, number, key_block, key_heads
        )
        masked = score_block(query_groups, key_rows, key_index, start, query_index)
        chances = jnp.exp(masked - log_total[..., None])
        chances_low = chances.astype(jnp.bfloat16)
        grad_chances = jnp.einsum(
            "qgjd,kgd->gjqk", grad_groups, value_rows, preferred_element_type=jnp.float32
        )
        grad_logits = (chances * (grad_chances - row_dot[..., None])).astype(jnp.bfloat16)
        grad_query = (
            grad_query
            + jnp.einsum(
                "gjqk,kgd->gjqd", grad_logits, key_rows, preferred_element_type=jnp.float32
            )
            * score_scale
        )
        grad_keys = (
            jnp.einsum(
                "gjqk,qgjd->kgd", grad_logits, query_groups, preferred_element_type=jnp.float32
            )
            * score_scale
        )
        grad_values = jnp.einsum(
            "gjqk,qgjd->kgd", chances_low, grad_groups, preferred_element_type=jnp.float32
        )
        grad_piece = jnp.concatenate(
            [
                grad_keys.reshape(key_block, key_heads * head_dim),
                grad_values.reshape(key_block, key_heads * head_dim),
            ],
            axis=-1,
        ).astype(jnp.bfloat16)
        grad_keyval = lax.dynamic_update_slice_in_dim(
            grad_keyval, grad_piece, number * key_block, 0
        )
        return (grad_query, grad_keyval)

    start_state = (
        jnp.zeros((key_heads, group_size, tokens, head_dim), jnp.float32),
        jnp.zeros(keyval_all.shape, jnp.bfloat16),
    )
    grad_query, grad_keyval = repeat(block_count, step_back, start_state)
    return (grad_query.transpose(2, 0, 1, 3).reshape(tokens, head_count, head_dim), grad_keyval)


def body(
    layer_input,
    segments,
    positions,
    attn_gain,
    w_q,
    b_q,
    w_k,
    b_k,
    w_v,
    b_v,
    w_o,
    mlp_gain,
    w_gate,
    w_up,
    w_down,
    cotangent,
):
    key_heads = w_k.shape[1] // HEAD_DIM
    head_count = w_q.shape[1] // HEAD_DIM
    width_q, width_k = w_q.shape[1], w_k.shape[1]
    tokens = layer_input.shape[1]
    ctx_size, fsdp_size = lax.axis_size("ctx"), lax.axis_size("fsdp")
    ctx_own = lax.axis_index("ctx")
    rows, hidden_count = w_gate.shape
    features = layer_input.shape[2]
    chunk = -(-hidden_count // (ctx_size * LANES)) * LANES
    width_qkv = width_q + 2 * width_k
    own = ctx_own.astype(jnp.int32)[None]

    attn_lined = direct_gather(jnp.concatenate([w_q, w_k, w_v, w_o.T], axis=1))

    if few():
        cuts = prepare(own, w_gate, w_up, w_down.T, ctx_size, chunk)
    else:
        tail = ((0, 0), (0, chunk * ctx_size - hidden_count))
        shards = [
            jnp.pad(shard, tail).reshape(rows, ctx_size, chunk) for shard in (w_gate, w_up, w_down.T)
        ]
        cuts = list(jnp.concatenate(shards, axis=-1).transpose(1, 0, 2))
    recut = untangle(trade(cuts)).reshape(ctx_size * rows, 3 * chunk)
    mlp_rows = lax.all_gather(recut, "fsdp", axis=0, tiled=True)

    def ordered(parts):
        pieces = untangle(parts)
        return pieces.transpose(1, 0, 2, 3).reshape(features, pieces.shape[-1])

    full_qkv = ordered(spread(attn_lined[..., :width_qkv]))
    o_pieces = spread(attn_lined[..., width_qkv:])

    inputs = layer_input[0].astype(jnp.float32)
    place = jnp.arange(tokens, dtype=jnp.int32)
    query_index = ctx_own * tokens + place
    grad_top = cotangent[0]
    cosines, sines = angles(positions[0], HEAD_DIM)
    scale_one = lax.rsqrt(jnp.mean(inputs * inputs, -1, keepdims=True) + EPS)
    unit_one = inputs * scale_one
    normed = (unit_one * attn_gain).astype(jnp.bfloat16)
    small_heads = few() and key_heads == 1 and tokens <= 256
    if small_heads:
        half = HEAD_DIM // 2
        cos_turned, sin_turned = cosines[:, 0, :half].T, sines[:, 0, :half].T
        query_flat, keyval = project(
            layer_input[0],
            attn_gain[None],
            full_qkv,
            jnp.concatenate([b_q, b_k, b_v])[None],
            cos_turned,
            sin_turned,
            segments,
            width_q,
            width_k,
        )
    else:
        projected = jnp.dot(normed, full_qkv, preferred_element_type=jnp.float32) + jnp.concatenate(
            [b_q, b_k, b_v]
        )
        queries = projected[:, :width_q]
        keyproj = projected[:, width_q : width_q + width_k]
        valproj = projected[:, width_q + width_k :]
        query_rot = rotate(queries.reshape(tokens, head_count, HEAD_DIM), cosines, sines).astype(
            jnp.bfloat16
        )
        key_rot = rotate(keyproj.reshape(tokens, key_heads, HEAD_DIM), cosines, sines).astype(
            jnp.bfloat16
        )
        keyval = jnp.concatenate(
            [key_rot.reshape(tokens, key_heads * HEAD_DIM), valproj.astype(jnp.bfloat16)], axis=-1
        )
    received = spread(keyval)
    full_o_turned = ordered(o_pieces)
    if small_heads:
        attended_low, attended_turned, log_total, start = attend_fwd(
            own, query_flat, segments, received
        )
    else:
        seg_own = segments[0]
        counts = jnp.stack([jnp.sum((seg_own <= number).astype(jnp.int32)) for number in range(2)])
        counts = lax.psum(counts, "ctx")
        start = jnp.where(seg_own == 0, 0, jnp.where(seg_own == 1, counts[0], counts[1]))
        order = untangle(received).reshape(ctx_size * tokens, 2 * width_k)
        attended, log_total = attend(query_rot, order, start, query_index, key_heads)
        attended_low = attended.astype(jnp.bfloat16)
    attended_low, grad_top_mine = lax.optimization_barrier(
        (attended_low, gather_half(after(grad_top, *received)))
    )
    branch_part = dot_rows(attended_low, full_o_turned).astype(jnp.bfloat16)
    middle = inputs + (
        branch_part.astype(jnp.float32) + swap_cores(branch_part).astype(jnp.float32)
    )
    scale_two = lax.rsqrt(jnp.mean(middle * middle, -1, keepdims=True) + EPS)
    unit_two = middle * scale_two
    normed_two = (unit_two * mlp_gain).astype(jnp.bfloat16)

    normed_mine = gather_half(normed_two)
    halves = [normed_mine, swap_cores(normed_mine)]
    tops = [grad_top_mine, swap_cores(grad_top_mine)]
    fsdp_own = lax.axis_index("fsdp").astype(jnp.int32)[None]

    gate_up, down_turned = mlp_rows[:, : 2 * chunk], mlp_rows[:, 2 * chunk :]
    normed_all, grad_top_all = jnp.concatenate(halves), jnp.concatenate(tops)
    gate_upward = dot(normed_all, gate_up)
    grad_hidden = dot(grad_top_all, down_turned)
    gate_values, upward = gate_upward[:, :chunk], gate_upward[:, chunk:]
    sigmoid_gate = jax.nn.sigmoid(gate_values)
    swish_gate = gate_values * sigmoid_gate
    hidden = (swish_gate * upward).astype(jnp.bfloat16)
    slope = sigmoid_gate + swish_gate * (1.0 - sigmoid_gate)
    grad_both = jnp.concatenate(
        [grad_hidden * upward * slope, grad_hidden * swish_gate], axis=-1
    ).astype(jnp.bfloat16)
    grad_one, grad_two = jnp.split(dot_rows(grad_both, gate_up).astype(jnp.bfloat16), 2)
    grad_normed_sum = add_cores(grad_one, grad_two)
    grad_normed_parts = trade(jnp.split(grad_normed_sum, ctx_size))
    mlp_grad = jnp.concatenate(
        [
            turned_dot(normed_all, grad_both).astype(jnp.bfloat16),
            turned_dot(grad_top_all, hidden).astype(jnp.bfloat16),
        ],
        axis=-1,
    ).reshape(fsdp_size, ctx_size * rows, 3 * chunk)
    mlp_mine = lax.psum_scatter(mlp_grad, "fsdp", scatter_dimension=0, tiled=False)
    branch_two_sum = add_cores(
        *jnp.split(dot_rows(hidden, down_turned).astype(jnp.bfloat16), 2)
    )
    branch_two_sum, *grad_normed_parts = lax.optimization_barrier(
        (branch_two_sum, *grad_normed_parts)
    )
    grad_normed_two = join_tokens(grad_normed_parts)
    branch_two_parts = trade(jnp.split(branch_two_sum, ctx_size))

    grad_mlp_gain = jnp.sum(grad_normed_two * unit_two, 0)
    grad_unit_two = grad_normed_two * mlp_gain
    grad_middle = grad_top.astype(jnp.float32) + scale_two * (
        grad_unit_two - unit_two * jnp.mean(grad_unit_two * unit_two, -1, keepdims=True)
    )
    grad_branch = grad_middle.astype(jnp.bfloat16)
    def owners(left, right):
        if few():
            return weight_grad(own, left, right, ctx_size, fsdp_size)
        grad = turned_dot(left, right).astype(jnp.bfloat16)
        cut = grad.reshape(fsdp_size, ctx_size, rows, right.shape[1]).transpose(1, 0, 2, 3)
        return list(cut.reshape(ctx_size, fsdp_size * rows, right.shape[1]))

    o_parts = trade(owners(grad_branch, attended_low))
    if small_heads:
        grad_query, grad_keyvals = attend_bwd(
            own,
            query_flat,
            start,
            attended_turned,
            log_total,
            grad_branch,
            full_o_turned,
            cos_turned,
            sin_turned,
            received,
        )
    else:
        grad_attended = dot(grad_branch, full_o_turned).astype(jnp.bfloat16)
        grad_query_rot, grad_keyvals = attend_back(
            query_rot,
            order,
            start,
            query_index,
            key_heads,
            log_total,
            attended,
            grad_attended,
        )
        grad_keyvals = choose(grad_keyvals.reshape(ctx_size, tokens, 2 * width_k))
    grad_keyvals[0], branch_two_parts = lax.optimization_barrier(
        (grad_keyvals[0], branch_two_parts)
    )
    grad_keyvals[0], o_parts[1] = lax.optimization_barrier((grad_keyvals[0], o_parts[1]))
    keyval_parts = trade(grad_keyvals)
    keyval_parts[0], o_parts = lax.optimization_barrier((keyval_parts[0], o_parts))
    branch_two = join_tokens(branch_two_parts)
    result = (middle + branch_two).astype(jnp.bfloat16)

    if small_heads:
        grad_qkv, grad_normed_part = key_grads(
            grad_query, full_qkv, cos_turned, sin_turned, keyval_parts
        )
    else:
        grad_keyval = sum(part.astype(F32) for part in keyval_parts)
        grad_query = (
            rotate(grad_query_rot, cosines, -sines)
            .reshape(tokens, head_count * HEAD_DIM)
            .astype(jnp.bfloat16)
        )
        grad_key = (
            rotate(
                grad_keyval[:, : key_heads * HEAD_DIM].reshape(tokens, key_heads, HEAD_DIM),
                cosines,
                -sines,
            )
            .reshape(tokens, key_heads * HEAD_DIM)
            .astype(jnp.bfloat16)
        )
        grad_value = grad_keyval[:, key_heads * HEAD_DIM :].astype(jnp.bfloat16)
        grad_qkv = jnp.concatenate([grad_query, grad_key, grad_value], axis=-1)
        grad_normed_part = dot_rows(grad_qkv, full_qkv).astype(jnp.bfloat16)
    grad_normed_other = swap_cores(grad_normed_part)
    if few():
        grad_inputs, qkv_pieces = last_grads(
            own,
            layer_input[0],
            attn_gain[None],
            grad_qkv,
            grad_normed_part,
            grad_normed_other,
            grad_middle,
            grad_mlp_gain[None],
            ctx_size,
            fsdp_size,
        )
    else:
        grad_normed = grad_normed_part.astype(F32) + grad_normed_other.astype(F32)
        turned = grad_normed * unit_one
        along = jnp.mean(turned * attn_gain, -1, keepdims=True)
        grad_inputs = grad_middle + scale_one * (grad_normed * attn_gain - unit_one * along)
        grad_inputs = grad_inputs.astype(jnp.bfloat16)
        lines = [jnp.sum(grad_qkv.astype(F32), 0)]
        for gains in (jnp.sum(turned, 0), grad_mlp_gain):
            for half in (gains[:SPLIT], gains[SPLIT:]):
                lines.append(jnp.pad(half, (0, width_qkv - half.shape[0])))
        small = jnp.pad(jnp.stack(lines), ((0, SMALL_ROWS - len(lines)), (0, 0)))
        small = small.astype(jnp.bfloat16)
        qkv_pieces = [jnp.concatenate([part, small]) for part in owners(normed, grad_qkv)]
    qkv_parts = trade(qkv_pieces)
    if few():
        packed = pack(fsdp_own, qkv_parts, o_parts, fsdp_size)
    else:
        qkv_sum = sum(part.astype(F32) for part in qkv_parts)
        o_sum = sum(part.astype(F32) for part in o_parts)
        small = jnp.pad(qkv_sum[fsdp_size * rows :], ((0, 0), (0, w_o.shape[0])))
        both = jnp.concatenate([qkv_sum[: fsdp_size * rows], o_sum], axis=-1)
        both = both.reshape(fsdp_size, rows, both.shape[-1])
        packed = [
            jnp.concatenate([both[(fsdp_own[0] + step) % fsdp_size], small]).astype(jnp.bfloat16)
            for step in range(fsdp_size)
        ]
    mlp_mine = mlp_mine.reshape(ctx_size, rows, 3 * chunk)
    packed = packed[:1] + [send_up(packed[step], step) for step in range(1, fsdp_size)]
    mlp_pieces = trade(choose(mlp_mine))
    if few():
        w_grads = unpack(packed, features, width_q, width_k)
        mlp_grads = mlp_out(own, mlp_pieces, hidden_count)
    else:
        total = sum(part.astype(F32) for part in packed)
        tops = [0, width_q, width_q + width_k, width_qkv]
        w_grads = [total[:rows, tops[k] : tops[k + 1]] for k in range(3)]
        w_grads.append(total[:rows, width_qkv:])
        w_grads += [total[rows, tops[k] : tops[k + 1]] for k in range(3)]
        for row in (rows + 1, rows + 3):
            w_grads.append(
                jnp.concatenate([total[row, :SPLIT], total[row + 1, : features - SPLIT]])
            )
        mlp_grads = []
        for number in range(3):
            pieces = untangle(mlp_pieces)[..., number * chunk : (number + 1) * chunk]
            wide = pieces.transpose(1, 0, 2).reshape(rows, chunk * ctx_size)
            mlp_grads.append(wide[:, :hidden_count].astype(F32))
    grad_q, grad_k, grad_v, grad_o = w_grads[:4]
    grad_b_q, grad_b_k, grad_b_v, grad_attn_gain, grad_mlp_gain = [
        values.reshape(-1) for values in w_grads[4:]
    ]
    return (
        result[None],
        grad_inputs[None],
        grad_attn_gain,
        grad_q,
        grad_b_q,
        grad_k,
        grad_b_k,
        grad_v,
        grad_b_v,
        grad_o.T,
        grad_mlp_gain,
        mlp_grads[0],
        mlp_grads[1],
        mlp_grads[2].T,
    )


def solution(mesh):
    placed = (
        P("fsdp", "ctx", None),
        P("fsdp", "ctx"),
        P("fsdp", "ctx"),
        P(),
        P(("fsdp", "ctx"), "tp"),
        P("tp"),
        P(("fsdp", "ctx"), "tp"),
        P("tp"),
        P(("fsdp", "ctx"), "tp"),
        P("tp"),
        P("tp", ("fsdp", "ctx")),
        P(),
        P(("fsdp", "ctx"), "tp"),
        P(("fsdp", "ctx"), "tp"),
        P("tp", ("fsdp", "ctx")),
        P("fsdp", "ctx", None),
    )
    return jax.shard_map(
        body,
        mesh=mesh,
        in_specs=placed,
        out_specs=(
            P("fsdp", "ctx", None),
            P("fsdp", "ctx", None),
            P(),
            P(("fsdp", "ctx"), "tp"),
            P("tp"),
            P(("fsdp", "ctx"), "tp"),
            P("tp"),
            P(("fsdp", "ctx"), "tp"),
            P("tp"),
            P("tp", ("fsdp", "ctx")),
            P(),
            P(("fsdp", "ctx"), "tp"),
            P(("fsdp", "ctx"), "tp"),
            P("tp", ("fsdp", "ctx")),
        ),
        check_vma=False,
    )
```

profile of v0, /device:TPU:0, one launch (start us, length us, event | category | flops | bytes accessed | tf_op | source)
XLA Modules:
  0.0 220.7 jit_solution(12308755262865053978)
XLA Ops:
  8.2 3.1 %collective-permute-start.2 = (bf16[56,1024]{1,0:T(8,128)(2,1)S(1)}, bf16[56,1024]{1,0:T(8,128)(2,1)S(1)}, u32[]{:S(2)}, u32[]{:S(2)}) collective-permute-start(bf16[56,1024]{1,0:T(8,128)(2,1)S(1)} %pad_maximum_fusion.10), channel_id=1, source_target_pairs={{0,8},{8,16},{16,24},{24,0},{1,9},{9,17},{17,25},{25,1},{2,10},{10... | collective-permute-start | bytes 344072 | tf_op jit(solution)/shard_map/ppermute | solution.py:114
  11.3 2.6 %collective-permute-start.1 = (bf16[56,1024]{1,0:T(8,128)(2,1)S(1)}, bf16[56,1024]{1,0:T(8,128)(2,1)S(1)}, u32[]{:S(2)}, u32[]{:S(2)}) collective-permute-start(bf16[56,1024]{1,0:T(8,128)(2,1)S(1)} %pad_maximum_fusion.10), channel_id=1, source_target_pairs={{0,16},{8,24},{16,0},{24,8},{1,17},{9,25},{17,1},{25,9},{2,18},{10... | collective-permute-start | bytes 344072 | tf_op jit(solution)/shard_map/ppermute | solution.py:114
  13.9 1.3 collective-permute-start
  18.3 1.6 collective-permute-start.20
  19.8 1.5 collective-permute-start.21
  24.5 4.9 %collective-permute-done.21 = bf16[56,1920]{1,0:T(8,128)(2,1)S(1)} collective-permute-done((bf16[56,1920]{1,0:T(8,128)(2,1)S(1)}, bf16[56,1920]{1,0:T(8,128)(2,1)S(1)}, u32[]{:S(2)}, u32[]{:S(2)}) %collective-permute-start.21) | collective-permute-done | bytes 215072 | tf_op jit(solution)/shard_map/ppermute | solution.py:86
  29.4 1.2 collective-permute-done.22
  32.0 1.4 collective-permute-start.4
  33.9 1.7 collective-permute-start.5
  35.8 1.4 collective-permute-start.13
  37.8 6.1 %collective-permute-done.4 = bf16[4,56,576]{2,1,0:T(8,128)(2,1)S(1)} collective-permute-done((bf16[4,56,576]{2,1,0:T(8,128)(2,1)S(1)}, bf16[4,56,576]{2,1,0:T(8,128)(2,1)S(1)}, u32[]{:S(2)}, u32[]{:S(2)}) %collective-permute-start.4) | collective-permute-done | bytes 258080 | tf_op jit(solution)/shard_map/ppermute | solution.py:78
  44.0 2.7 %collective-permute-start.14 = (bf16[4,56,448]{2,1,0:T(8,128)(2,1)S(1)}, bf16[4,56,448]{2,1,0:T(8,128)(2,1)S(1)}, u32[]{:S(2)}, u32[]{:S(2)}) collective-permute-start(bf16[4,56,448]{2,1,0:T(8,128)(2,1)S(1)} %constant_dynamic-slice_fusion.14), channel_id=1, source_target_pairs={{0,6},{2,4},{4,2},{6,0},{1,7},{3,5},{5,3},{7,1},{8,14},{10,12},{12... | collective-permute-start | bytes 602120 | tf_op jit(solution)/shard_map/ppermute | solution.py:78
  46.7 2.9 %collective-permute-done.5 = bf16[4,56,576]{2,1,0:T(8,128)(2,1)S(1)} collective-permute-done((bf16[4,56,576]{2,1,0:T(8,128)(2,1)S(1)}, bf16[4,56,576]{2,1,0:T(8,128)(2,1)S(1)}, u32[]{:S(2)}, u32[]{:S(2)}) %collective-permute-start.5) | collective-permute-done | bytes 258080 | tf_op jit(solution)/shard_map/ppermute | solution.py:78
  51.9 1.3 collective-permute-start.8
  53.2 1.2 collective-permute-start.7
  54.3 1.1 collective-permute-start.6
  55.4 1.6 collective-permute-done.14
  59.4 2.9 %collective-permute-start.11 = (bf16[128,896]{1,0:T(8,128)(2,1)S(1)}, bf16[128,896]{1,0:T(8,128)(2,1)S(1)}, u32[]{:S(2)}, u32[]{:S(2)}) collective-permute-start(bf16[128,896]{1,0:T(8,128)(2,1)S(1)} %constant_dynamic-slice_fusion.9), channel_id=1, source_target_pairs={{0,6},{2,4},{4,2},{6,0},{1,7},{3,5},{5,3},{7,1},{8,14},{10,12},{12... | collective-permute-start | bytes 688136 | tf_op jit(solution)/shard_map/ppermute | solution.py:78
  62.3 2.6 %collective-permute-start.10 = (bf16[128,896]{1,0:T(8,128)(2,1)S(1)}, bf16[128,896]{1,0:T(8,128)(2,1)S(1)}, u32[]{:S(2)}, u32[]{:S(2)}) collective-permute-start(bf16[128,896]{1,0:T(8,128)(2,1)S(1)} %constant_dynamic-slice_fusion.9), channel_id=1, source_target_pairs={{0,4},{2,6},{4,0},{6,2},{1,5},{3,7},{5,1},{7,3},{8,12},{10,14},{12... | collective-permute-start | bytes 688136 | tf_op jit(solution)/shard_map/ppermute | solution.py:78
  65.3 4.2 %attend_forward.1 = (bf16[256,448]{1,0:T(8,128)(2,1)S(1)}, f32[448,256]{1,0:T(8,128)S(1)}, f32[7,256]{1,0:T(8,128)S(1)}, s32[1,256]{1,0:T(1,128)S(1)}) custom-call(s32[1]{0:T(128)} %bitcast.1.own_ref, bf16[256,448]{1,0:T(8,128)(2,1)S(1)} %get-tuple-element.76.q_ref, s32[1,256]{1,0:T(1,128)S(1)} %copy-done.6, bf16[272,128]{1,0:T(8,128)(2,1)S(1)} %get-tuple-element.77.refs_0_, ...), custom_call_target="tpu_custom_call" | custom-call | tf_op jit(solution)/shard_map/attend_forward/pallas_call | solution.py:306
  71.6 1.8 collective-permute-done.15
  75.9 1.9 collective-permute-start.18
  79.4 5.9 %collective-permute-done.18 = bf16[128,896]{1,0:T(8,128)(2,1)S(1)} collective-permute-done((bf16[128,896]{1,0:T(8,128)(2,1)S(1)}, bf16[128,896]{1,0:T(8,128)(2,1)S(1)}, u32[]{:S(2)}, u32[]{:S(2)}) %collective-permute-start.18) | collective-permute-done | bytes 229408 | tf_op jit(solution)/shard_map/ppermute | solution.py:78
  85.3 4.1 %collective-permute-done.17 = bf16[128,896]{1,0:T(8,128)(2,1)S(1)} collective-permute-done((bf16[128,896]{1,0:T(8,128)(2,1)S(1)}, bf16[128,896]{1,0:T(8,128)(2,1)S(1)}, u32[]{:S(2)}, u32[]{:S(2)}) %collective-permute-start.17) | collective-permute-done | bytes 229408 | tf_op jit(solution)/shard_map/ppermute | solution.py:78
  92.0 1.3 copy-done.18
  94.2 5.9 %all-gather.2.cloned.1.call-done = bf16[896,1920]{1,0:T(8,128)(2,1)} async-done(((bf16[224,1920]{1,0:T(8,128)(2,1)}), bf16[896,1920]{1,0:T(8,128)(2,1)}) %all-gather.2.cloned.1.call-update) | async-done | bytes 3440656 | tf_op jit(solution)/shard_map/all_gather | solution.py:757
  100.1 5.2 %fusion.2 = f32[1024,1280]{1,0:T(8,128)S(1)} fusion(bf16[1024,896]{1,0:T(8,128)(2,1)} %constant_dynamic-update-slice_fusion, bf16[896,1920]{1,0:T(8,128)(2,1)} %all-gather.2.cloned.1.call-done), kind=kOutput, calls=%fused_computation.10 | convolution fusion | flops 2348810240 | bytes 9371648 | tf_op jit(solution)/shard_map/dot_general | solution.py:30
  105.3 3.8 %multiply_convert_fusion.1 = (bf16[1024,640]{1,0:T(8,128)(2,1)S(1)}, bf16[1024,640]{1,0:T(8,128)(2,1)S(1)}, bf16[1024,640]{1,0:T(8,128)(2,1)S(1)}) fusion(f32[1024,1280]{1,0:T(8,128)S(1)} %fusion.2, bf16[1024,896]{1,0:T(8,128)(2,1)S(1)} %copy-done.19, bf16[896,1920]{1,0:T(8,128)(2,1)} %all-gather.2.cloned.1.call-done), kind=kOutput, calls=%fused_computation.4 | convolution fusion | flops 1183580160 | bytes 12156928 | tf_op jit(solution)/shard_map/dot_general | solution.py:30
  109.2 1.7 convolution_convert_fusion.2
  111.1 4.1 %convolution_convert_fusion = bf16[896,1280]{1,0:T(8,128)(2,1)S(1)} fusion(bf16[1024,896]{1,0:T(8,128)(2,1)} %constant_dynamic-update-slice_fusion, bf16[1024,640]{1,0:T(8,128)(2,1)S(1)} %get-tuple-element.145, bf16[1024,640]{1,0:T(8,128)(2,1)S(1)} %get-tuple-element.144), kind=kOutput, calls=%fused_computation | convolution fusion | flops 2355200000 | bytes 6750208 | tf_op jit(solution)/shard_map/dot_general | solution.py:38
  115.3 2.0 pad_maximum_fusion
  117.3 5.3 %fusion.4 = bf16[1024,896]{1,0:T(8,128)(2,1)S(1)} fusion(bf16[896,1920]{1,0:T(8,128)(2,1)} %all-gather.2.cloned.1.call-done, bf16[1024,640]{1,0:T(8,128)(2,1)} %copy-done.26, bf16[1024,640]{1,0:T(8,128)(2,1)} %copy-done.25), kind=kOutput, calls=%fused_computation.14 | convolution fusion | flops 2354970624 | bytes 6750208 | tf_op jit(solution)/shard_map/dot_general | solution.py:34
  123.7 1.3 copy-done.28
  125.0 3.0 %convolution_convert_fusion.1 = bf16[1024,896]{1,0:T(8,128)(2,1)S(1)} fusion(bf16[1024,640]{1,0:T(8,128)(2,1)S(1)} %copy-done.28, bf16[896,1920]{1,0:T(8,128)(2,1)} %all-gather.2.cloned.1.call-done), kind=kOutput, calls=%fused_computation.15 | convolution fusion | flops 1175322624 | bytes 4292608 | tf_op jit(solution)/shard_map/dot_general | solution.py:34
  128.0 1.2 copy-done.13
  130.2 1.8 add_convert_fusion
  132.1 2.5 %collective-permute-start.28 = (bf16[128,896]{1,0:T(8,128)(2,1)S(1)}, bf16[128,896]{1,0:T(8,128)(2,1)S(1)}, u32[]{:S(2)}, u32[]{:S(2)}) collective-permute-start(bf16[128,896]{1,0:T(8,128)(2,1)S(1)} %get-tuple-element.155), channel_id=1, source_target_pairs={{0,6},{2,4},{4,2},{6,0},{1,7},{3,5},{5,3},{7,1},{8,14},{10,12},{12... | collective-permute-start | bytes 688136 | tf_op jit(solution)/shard_map/ppermute | solution.py:86
  135.7 1.4 add_convert_fusion.1
  137.1 4.4 %collective-permute-done.28 = bf16[128,896]{1,0:T(8,128)(2,1)S(1)} collective-permute-done((bf16[128,896]{1,0:T(8,128)(2,1)S(1)}, bf16[128,896]{1,0:T(8,128)(2,1)S(1)}, u32[]{:S(2)}, u32[]{:S(2)}) %collective-permute-start.28) | collective-permute-done | bytes 229408 | tf_op jit(solution)/shard_map/ppermute | solution.py:86
  141.5 4.5 %collective-permute-done.27 = bf16[128,896]{1,0:T(8,128)(2,1)S(1)} collective-permute-done((bf16[128,896]{1,0:T(8,128)(2,1)S(1)}, bf16[128,896]{1,0:T(8,128)(2,1)S(1)}, u32[]{:S(2)}, u32[]{:S(2)}) %collective-permute-start.27) | collective-permute-done | bytes 229408 | tf_op jit(solution)/shard_map/ppermute | solution.py:86
  146.4 1.7 collective-permute-start.32
  148.1 1.3 collective-permute-start.31
  151.2 1.6 collective-permute-start.34
  153.5 2.4 %collective-permute-done.32 = bf16[128,896]{1,0:T(8,128)(2,1)S(1)} collective-permute-done((bf16[128,896]{1,0:T(8,128)(2,1)S(1)}, bf16[128,896]{1,0:T(8,128)(2,1)S(1)}, u32[]{:S(2)}, u32[]{:S(2)}) %collective-permute-start.32) | collective-permute-done | bytes 229408 | tf_op jit(solution)/shard_map/ppermute | solution.py:86
  155.8 1.6 collective-permute-start.36
  157.4 7.4 %attend_backward.1 = (bf16[256,448]{1,0:T(8,128)(2,1)S(1)}, bf16[256,128]{1,0:T(8,128)(2,1)S(1)}, bf16[256,128]{1,0:T(8,128)(2,1)S(1)}, bf16[256,128]{1,0:T(8,128)(2,1)S(1)}, bf16[256,128]{1,0:T(8,128)(2,1)S(1)}) custom-call(s32[1]{0:T(128)} %bitcast.1.own_ref, bf16[256,448]{1,0:T(8,128)(2,1)S(1)} %get-tuple-element.76.q_ref, ...), custom_call_target="tpu_custom_call" | custom-call | tf_op jit(solution)/shard_map/attend_backward/pallas_call | solution.py:352
  164.8 1.5 collective-permute-start.37
  166.8 1.6 collective-permute-start.39
  168.4 2.2 %collective-permute-done.36.refs_7_ = bf16[224,448]{1,0:T(8,128)(2,1)S(1)} collective-permute-done((bf16[224,448]{1,0:T(8,128)(2,1)S(1)}, bf16[224,448]{1,0:T(8,128)(2,1)S(1)}, u32[]{:S(2)}, u32[]{:S(2)}) %collective-permute-start.36) | collective-permute-done | bytes 200736 | tf_op jit(solution)/shard_map/ppermute | solution.py:86
  170.6 1.5 collective-permute-done.37.refs_1_
  173.9 1.8 collective-permute-done.40.second_ref
  175.7 1.9 last_grads.1
  177.6 1.5 collective-permute-start.41
  179.8 1.3 collective-permute-start.43
  181.2 6.4 %collective-permute-done.41.refs_1_ = bf16[240,576]{1,0:T(8,128)(2,1)S(1)} collective-permute-done((bf16[240,576]{1,0:T(8,128)(2,1)S(1)}, bf16[240,576]{1,0:T(8,128)(2,1)S(1)}, u32[]{:S(2)}, u32[]{:S(2)}) %collective-permute-start.41) | collective-permute-done | bytes 276512 | tf_op jit(solution)/shard_map/ppermute | solution.py:86
  187.7 7.0 %collective-permute-done.42.refs_2_ = bf16[240,576]{1,0:T(8,128)(2,1)S(1)} collective-permute-done((bf16[240,576]{1,0:T(8,128)(2,1)S(1)}, bf16[240,576]{1,0:T(8,128)(2,1)S(1)}, u32[]{:S(2)}, u32[]{:S(2)}) %collective-permute-start.42) | collective-permute-done | bytes 276512 | tf_op jit(solution)/shard_map/ppermute | solution.py:86
  195.3 1.6 collective-permute-start.45
  196.9 2.4 %collective-permute-start.46 = (bf16[72,1024]{1,0:T(8,128)(2,1)S(1)}, bf16[72,1024]{1,0:T(8,128)(2,1)S(1)}, u32[]{:S(2)}, u32[]{:S(2)}) collective-permute-start(bf16[72,1024]{1,0:T(8,128)(2,1)S(1)} %get-tuple-element.125), channel_id=1, source_target_pairs={{0,24},{8,0},{16,8},{24,16},{1,25},{9,1},{17,9},{25,17},{2,26},{10... | collective-permute-start | bytes 442376 | tf_op jit(solution)/shard_map/ppermute | solution.py:124
  199.3 2.1 dynamic-slice_bitcast_fusion
  201.4 1.4 collective-permute-start.49
  204.9 2.1 fusion.16
  207.0 1.3 collective-permute-done.45.refs_2_
  210.3 2.2 %collective-permute-done.48.refs_2_ = bf16[56,1920]{1,0:T(8,128)(2,1)S(1)} collective-permute-done((bf16[56,1920]{1,0:T(8,128)(2,1)}, bf16[56,1920]{1,0:T(8,128)(2,1)S(1)}, u32[]{:S(2)}, u32[]{:S(2)}) %collective-permute-start.48) | collective-permute-done | bytes 215072 | tf_op jit(solution)/shard_map/ppermute | solution.py:86
  212.6 1.3 mlp_out.1
  (177 shorter events, 38.9 us)
Async XLA Ops:
  7.2 17.2 %copy-start.22 = (bf16[56,64]{1,0:T(8,128)(2,1)S(1)}, bf16[56,64]{1,0:T(8,128)(2,1)}, u32[]{:S(2)}) copy-start(bf16[56,64]{1,0:T(8,128)(2,1)} %param.24) | copy-start | bytes 21508
  7.2 17.2 %copy-start.23 = (bf16[56,64]{1,0:T(8,128)(2,1)S(1)}, bf16[56,64]{1,0:T(8,128)(2,1)}, u32[]{:S(2)}) copy-start(bf16[56,64]{1,0:T(8,128)(2,1)} %param.22) | copy-start | bytes 21508
  7.2 17.2 %copy-start.21 = (bf16[56,448]{1,0:T(8,128)(2,1)S(1)}, bf16[56,448]{1,0:T(8,128)(2,1)}, u32[]{:S(2)}) copy-start(bf16[56,448]{1,0:T(8,128)(2,1)} %param.20) | copy-start | bytes 150532
  7.2 17.2 %copy-start.20 = (bf16[448,56]{0,1:T(8,128)(2,1)S(1)}, bf16[448,56]{0,1:T(8,128)(2,1)}, u32[]{:S(2)}) copy-start(bf16[448,56]{0,1:T(8,128)(2,1)} %param.26) | copy-start | bytes 150532
  7.2 92.9 %all-gather.2.cloned.1.call-start = ((), (), s32[]{:S(2)}) async-start(), calls=%async_computation.1 | async-start | bytes 4300800 | tf_op jit(solution)/shard_map/all_gather | solution.py:757
  8.2 16.1 %collective-permute-start.2 = (bf16[56,1024]{1,0:T(8,128)(2,1)S(1)}, bf16[56,1024]{1,0:T(8,128)(2,1)S(1)}, u32[]{:S(2)}, u32[]{:S(2)}) collective-permute-start(bf16[56,1024]{1,0:T(8,128)(2,1)S(1)} %pad_maximum_fusion.10), channel_id=1, source_target_pairs={{0,8},{8,16},{16,24},{24,0},{1,9},{9,17},{17,25},{25,1},{2,10},{10... | collective-permute-start | bytes 344072 | tf_op jit(solution)/shard_map/ppermute | solution.py:114
  11.3 13.0 %collective-permute-start.1 = (bf16[56,1024]{1,0:T(8,128)(2,1)S(1)}, bf16[56,1024]{1,0:T(8,128)(2,1)S(1)}, u32[]{:S(2)}, u32[]{:S(2)}) collective-permute-start(bf16[56,1024]{1,0:T(8,128)(2,1)S(1)} %pad_maximum_fusion.10), channel_id=1, source_target_pairs={{0,16},{8,24},{16,0},{24,8},{1,17},{9,25},{17,1},{25,9},{2,18},{10... | collective-permute-start | bytes 344072 | tf_op jit(solution)/shard_map/ppermute | solution.py:114
  13.9 9.8 %collective-permute-start = (bf16[56,1024]{1,0:T(8,128)(2,1)S(1)}, bf16[56,1024]{1,0:T(8,128)(2,1)S(1)}, u32[]{:S(2)}, u32[]{:S(2)}) collective-permute-start(bf16[56,1024]{1,0:T(8,128)(2,1)S(1)} %pad_maximum_fusion.10), channel_id=1, source_target_pairs={{0,24},{8,0},{16,8},{24,16},{1,25},{9,1},{17,9},{25,17},{2,26},{10... | collective-permute-start | bytes 344072 | tf_op jit(solution)/shard_map/ppermute | solution.py:114
  18.3 6.3 %collective-permute-start.20 = (bf16[56,1920]{1,0:T(8,128)(2,1)S(1)}, bf16[56,1920]{1,0:T(8,128)(2,1)S(1)}, u32[]{:S(2)}, u32[]{:S(2)}) collective-permute-start(bf16[56,1920]{1,0:T(8,128)(2,1)S(1)} %get-tuple-element.85), channel_id=1, source_target_pairs={{0,2},{2,0},{4,6},{6,4},{1,3},{3,1},{5,7},{7,5},{8,10},{10,8},{12,... | collective-permute-start | bytes 645128 | tf_op jit(solution)/shard_map/ppermute | solution.py:86
  19.8 9.6 %collective-permute-start.21 = (bf16[56,1920]{1,0:T(8,128)(2,1)S(1)}, bf16[56,1920]{1,0:T(8,128)(2,1)S(1)}, u32[]{:S(2)}, u32[]{:S(2)}) collective-permute-start(bf16[56,1920]{1,0:T(8,128)(2,1)S(1)} %get-tuple-element.86), channel_id=1, source_target_pairs={{0,4},{2,6},{4,0},{6,2},{1,5},{3,7},{5,1},{7,3},{8,12},{10,14},{12... | collective-permute-start | bytes 645128 | tf_op jit(solution)/shard_map/ppermute | solution.py:86
  23.7 6.8 %collective-permute-start.22 = (bf16[56,1920]{1,0:T(8,128)(2,1)S(1)}, bf16[56,1920]{1,0:T(8,128)(2,1)S(1)}, u32[]{:S(2)}, u32[]{:S(2)}) collective-permute-start(bf16[56,1920]{1,0:T(8,128)(2,1)S(1)} %get-tuple-element.87), channel_id=1, source_target_pairs={{0,6},{2,4},{4,2},{6,0},{1,7},{3,5},{5,3},{7,1},{8,14},{10,12},{12... | collective-permute-start | bytes 645128 | tf_op jit(solution)/shard_map/ppermute | solution.py:86
  31.9 167.4 %reduce-scatter.2.cloned.1.call-start = ((), (), s32[]{:S(2)}) async-start(), calls=%async_computation.2 | async-start | bytes 4300800 | tf_op jit(solution)/shard_map/reduce_scatter | solution.py:857
  32.0 11.9 %collective-permute-start.4 = (bf16[4,56,576]{2,1,0:T(8,128)(2,1)S(1)}, bf16[4,56,576]{2,1,0:T(8,128)(2,1)S(1)}, u32[]{:S(2)}, u32[]{:S(2)}) collective-permute-start(bf16[4,56,576]{2,1,0:T(8,128)(2,1)S(1)} %constant_dynamic-slice_fusion), channel_id=1, source_target_pairs={{0,4},{2,6},{4,0},{6,2},{1,5},{3,7},{5,1},{7,3},{8,12},{10,14},{12... | collective-permute-start | bytes 774152 | tf_op jit(solution)/shard_map/ppermute | solution.py:78
  33.4 13.3 %collective-permute-start.3 = (bf16[4,56,576]{2,1,0:T(8,128)(2,1)S(1)}, bf16[4,56,576]{2,1,0:T(8,128)(2,1)S(1)}, u32[]{:S(2)}, u32[]{:S(2)}) collective-permute-start(bf16[4,56,576]{2,1,0:T(8,128)(2,1)S(1)} %constant_dynamic-slice_fusion), channel_id=1, source_target_pairs={{0,2},{2,0},{4,6},{6,4},{1,3},{3,1},{5,7},{7,5},{8,10},{10,8},{12,... | collective-permute-start | bytes 774152 | tf_op jit(solution)/shard_map/ppermute | solution.py:78
  33.9 15.7 %collective-permute-start.5 = (bf16[4,56,576]{2,1,0:T(8,128)(2,1)S(1)}, bf16[4,56,576]{2,1,0:T(8,128)(2,1)S(1)}, u32[]{:S(2)}, u32[]{:S(2)}) collective-permute-start(bf16[4,56,576]{2,1,0:T(8,128)(2,1)S(1)} %constant_dynamic-slice_fusion), channel_id=1, source_target_pairs={{0,6},{2,4},{4,2},{6,0},{1,7},{3,5},{5,3},{7,1},{8,14},{10,12},{12... | collective-permute-start | bytes 774152 | tf_op jit(solution)/shard_map/ppermute | solution.py:78
  35.8 18.6 %collective-permute-start.13 = (bf16[4,56,448]{2,1,0:T(8,128)(2,1)S(1)}, bf16[4,56,448]{2,1,0:T(8,128)(2,1)S(1)}, u32[]{:S(2)}, u32[]{:S(2)}) collective-permute-start(bf16[4,56,448]{2,1,0:T(8,128)(2,1)S(1)} %constant_dynamic-slice_fusion.14), channel_id=1, source_target_pairs={{0,4},{2,6},{4,0},{6,2},{1,5},{3,7},{5,1},{7,3},{8,12},{10,14},{12... | collective-permute-start | bytes 602120 | tf_op jit(solution)/shard_map/ppermute | solution.py:78
  37.1 18.3 %collective-permute-start.12 = (bf16[4,56,448]{2,1,0:T(8,128)(2,1)S(1)}, bf16[4,56,448]{2,1,0:T(8,128)(2,1)S(1)}, u32[]{:S(2)}, u32[]{:S(2)}) collective-permute-start(bf16[4,56,448]{2,1,0:T(8,128)(2,1)S(1)} %constant_dynamic-slice_fusion.14), channel_id=1, source_target_pairs={{0,2},{2,0},{4,6},{6,4},{1,3},{3,1},{5,7},{7,5},{8,10},{10,8},{12,... | collective-permute-start | bytes 602120 | tf_op jit(solution)/shard_map/ppermute | solution.py:78
  44.0 13.1 %collective-permute-start.14 = (bf16[4,56,448]{2,1,0:T(8,128)(2,1)S(1)}, bf16[4,56,448]{2,1,0:T(8,128)(2,1)S(1)}, u32[]{:S(2)}, u32[]{:S(2)}) collective-permute-start(bf16[4,56,448]{2,1,0:T(8,128)(2,1)S(1)} %constant_dynamic-slice_fusion.14), channel_id=1, source_target_pairs={{0,6},{2,4},{4,2},{6,0},{1,7},{3,5},{5,3},{7,1},{8,14},{10,12},{12... | collective-permute-start | bytes 602120 | tf_op jit(solution)/shard_map/ppermute | solution.py:78
  50.3 9.1 %copy-start.16 = (bf16[1,256,896]{2,1,0:T(8,128)(2,1)S(1)}, bf16[1,256,896]{2,1,0:T(8,128)(2,1)}, u32[]{:S(2)}) copy-start(bf16[1,256,896]{2,1,0:T(8,128)(2,1)} %param.31) | copy-start | bytes 1376260
  51.9 6.0 %collective-permute-start.8 = (bf16[272,128]{1,0:T(8,128)(2,1)S(1)}, bf16[272,128]{1,0:T(8,128)(2,1)S(1)}, u32[]{:S(2)}, u32[]{:S(2)}) collective-permute-start(bf16[272,128]{1,0:T(8,128)(2,1)S(1)} %get-tuple-element.77.refs_0_), channel_id=1, source_target_pairs={{0,6},{2,4},{4,2},{6,0},{1,7},{3,5},{5,3},{7,1},{8,14},{10,12},{12... | collective-permute-start | bytes 208904 | tf_op jit(solution)/shard_map/ppermute | solution.py:78
  53.2 5.6 %collective-permute-start.7 = (bf16[272,128]{1,0:T(8,128)(2,1)S(1)}, bf16[272,128]{1,0:T(8,128)(2,1)S(1)}, u32[]{:S(2)}, u32[]{:S(2)}) collective-permute-start(bf16[272,128]{1,0:T(8,128)(2,1)S(1)} %get-tuple-element.77.refs_0_), channel_id=1, source_target_pairs={{0,4},{2,6},{4,0},{6,2},{1,5},{3,7},{5,1},{7,3},{8,12},{10,14},{12... | collective-permute-start | bytes 208904 | tf_op jit(solution)/shard_map/ppermute | solution.py:78
  54.3 5.1 %collective-permute-start.6 = (bf16[272,128]{1,0:T(8,128)(2,1)S(1)}, bf16[272,128]{1,0:T(8,128)(2,1)S(1)}, u32[]{:S(2)}, u32[]{:S(2)}) collective-permute-start(bf16[272,128]{1,0:T(8,128)(2,1)S(1)} %get-tuple-element.77.refs_0_), channel_id=1, source_target_pairs={{0,2},{2,0},{4,6},{6,4},{1,3},{3,1},{5,7},{7,5},{8,10},{10,8},{12,... | collective-permute-start | bytes 208904 | tf_op jit(solution)/shard_map/ppermute | solution.py:78
  59.4 10.8 %collective-permute-start.11 = (bf16[128,896]{1,0:T(8,128)(2,1)S(1)}, bf16[128,896]{1,0:T(8,128)(2,1)S(1)}, u32[]{:S(2)}, u32[]{:S(2)}) collective-permute-start(bf16[128,896]{1,0:T(8,128)(2,1)S(1)} %constant_dynamic-slice_fusion.9), channel_id=1, source_target_pairs={{0,6},{2,4},{4,2},{6,0},{1,7},{3,5},{5,3},{7,1},{8,14},{10,12},{12... | collective-permute-start | bytes 688136 | tf_op jit(solution)/shard_map/ppermute | solution.py:78
  62.3 7.9 %collective-permute-start.10 = (bf16[128,896]{1,0:T(8,128)(2,1)S(1)}, bf16[128,896]{1,0:T(8,128)(2,1)S(1)}, u32[]{:S(2)}, u32[]{:S(2)}) collective-permute-start(bf16[128,896]{1,0:T(8,128)(2,1)S(1)} %constant_dynamic-slice_fusion.9), channel_id=1, source_target_pairs={{0,4},{2,6},{4,0},{6,2},{1,5},{3,7},{5,1},{7,3},{8,12},{10,14},{12... | collective-permute-start | bytes 688136 | tf_op jit(solution)/shard_map/ppermute | solution.py:78
  64.9 6.0 %collective-permute-start.9 = (bf16[128,896]{1,0:T(8,128)(2,1)S(1)}, bf16[128,896]{1,0:T(8,128)(2,1)S(1)}, u32[]{:S(2)}, u32[]{:S(2)}) collective-permute-start(bf16[128,896]{1,0:T(8,128)(2,1)S(1)} %constant_dynamic-slice_fusion.9), channel_id=1, source_target_pairs={{0,2},{2,0},{4,6},{6,4},{1,3},{3,1},{5,7},{7,5},{8,10},{10,8},{12,... | collective-permute-start | bytes 688136 | tf_op jit(solution)/shard_map/ppermute | solution.py:78
  71.5 1.9 collective-permute-start.15
  75.9 9.4 %collective-permute-start.18 = (bf16[128,896]{1,0:T(8,128)(2,1)S(1)}, bf16[128,896]{1,0:T(8,128)(2,1)S(1)}, u32[]{:S(2)}, u32[]{:S(2)}) collective-permute-start(bf16[128,896]{1,0:T(8,128)(2,1)S(1)} %get-tuple-element.143), channel_id=1, source_target_pairs={{0,6},{2,4},{4,2},{6,0},{1,7},{3,5},{5,3},{7,1},{8,14},{10,12},{12... | collective-permute-start | bytes 688136 | tf_op jit(solution)/shard_map/ppermute | solution.py:78
  77.8 11.5 %collective-permute-start.17 = (bf16[128,896]{1,0:T(8,128)(2,1)S(1)}, bf16[128,896]{1,0:T(8,128)(2,1)S(1)}, u32[]{:S(2)}, u32[]{:S(2)}) collective-permute-start(bf16[128,896]{1,0:T(8,128)(2,1)S(1)} %get-tuple-element.143), channel_id=1, source_target_pairs={{0,4},{2,6},{4,0},{6,2},{1,5},{3,7},{5,1},{7,3},{8,12},{10,14},{12... | collective-permute-start | bytes 688136 | tf_op jit(solution)/shard_map/ppermute | solution.py:78
  78.6 10.7 %collective-permute-start.16 = (bf16[128,896]{1,0:T(8,128)(2,1)S(1)}, bf16[128,896]{1,0:T(8,128)(2,1)S(1)}, u32[]{:S(2)}, u32[]{:S(2)}) collective-permute-start(bf16[128,896]{1,0:T(8,128)(2,1)S(1)} %get-tuple-element.143), channel_id=1, source_target_pairs={{0,2},{2,0},{4,6},{6,4},{1,3},{3,1},{5,7},{7,5},{8,10},{10,8},{12,... | collective-permute-start | bytes 688136 | tf_op jit(solution)/shard_map/ppermute | solution.py:78
  79.4 12.4 %collective-permute-start.24 = (bf16[512,896]{1,0:T(8,128)(2,1)S(1)}, bf16[512,896]{1,0:T(8,128)(2,1)S(1)}, u32[]{:S(2)}, u32[]{:S(2)}) collective-permute-start(bf16[512,896]{1,0:T(8,128)(2,1)S(1)} %pad_maximum_fusion.5), channel_id=1, source_target_pairs={{0,1},{1,0},{2,3},{3,2},{4,5},{5,4},{6,7},{7,6},{8,9},{9,8},{10,11... | collective-permute-start | bytes 2752520 | tf_op jit(solution)/shard_map/ppermute | solution.py:60
  89.4 2.5 %collective-permute-start.19 = (bf16[512,896]{1,0:T(8,128)(2,1)S(1)}, bf16[512,896]{1,0:T(8,128)(2,1)S(1)}, u32[]{:S(2)}, u32[]{:S(2)}) collective-permute-start(bf16[512,896]{1,0:T(8,128)(2,1)S(1)} %pad_maximum_fusion.7), channel_id=1, source_target_pairs={{0,1},{1,0},{2,3},{3,2},{4,5},{5,4},{6,7},{7,6},{8,9},{9,8},{10,11... | collective-permute-start | bytes 2752520 | tf_op jit(solution)/shard_map/ppermute | solution.py:60
  100.1 5.2 %copy-start.19 = (bf16[1024,896]{1,0:T(8,128)(2,1)S(1)}, bf16[1024,896]{1,0:T(8,128)(2,1)}, u32[]{:S(2)}) copy-start(bf16[1024,896]{1,0:T(8,128)(2,1)} %copy-done.18) | copy-start | bytes 5505028
  122.7 5.3 %copy-start.15 = (bf16[1024,896]{1,0:T(8,128)(2,1)}, bf16[1024,896]{1,0:T(8,128)(2,1)S(1)}, u32[]{:S(2)}) copy-start(bf16[1024,896]{1,0:T(8,128)(2,1)S(1)} %fusion.4) | copy-start | bytes 5505028
  123.7 6.5 %collective-permute-start.25 = (bf16[512,896]{1,0:T(8,128)(2,1)}, bf16[512,896]{1,0:T(8,128)(2,1)}, u32[]{:S(2)}, u32[]{:S(2)}) collective-permute-start(bf16[512,896]{1,0:T(8,128)(2,1)} %split.51), channel_id=1, source_target_pairs={{0,1},{1,0},{2,3},{3,2},{4,5},{5,4},{6,7},{7,6},{8,9},{9,8},{10,11... | collective-permute-start | bytes 2752520 | tf_op jit(solution)/shard_map/ppermute | solution.py:60
  130.2 5.5 %collective-permute-start.23 = (bf16[512,896]{1,0:T(8,128)(2,1)}, bf16[512,896]{1,0:T(8,128)(2,1)}, u32[]{:S(2)}, u32[]{:S(2)}) collective-permute-start(bf16[512,896]{1,0:T(8,128)(2,1)} %split.49), channel_id=1, source_target_pairs={{0,1},{1,0},{2,3},{3,2},{4,5},{5,4},{6,7},{7,6},{8,9},{9,8},{10,11... | collective-permute-start | bytes 2752520 | tf_op jit(solution)/shard_map/ppermute | solution.py:60
  130.2 5.5 %copy-start.14 = (bf16[1024,896]{1,0:T(8,128)(2,1)S(1)}, bf16[1024,896]{1,0:T(8,128)(2,1)}, u32[]{:S(2)}) copy-start(bf16[1024,896]{1,0:T(8,128)(2,1)} %copy-done.13) | copy-start | bytes 5505028
  132.1 9.4 %collective-permute-start.28 = (bf16[128,896]{1,0:T(8,128)(2,1)S(1)}, bf16[128,896]{1,0:T(8,128)(2,1)S(1)}, u32[]{:S(2)}, u32[]{:S(2)}) collective-permute-start(bf16[128,896]{1,0:T(8,128)(2,1)S(1)} %get-tuple-element.155), channel_id=1, source_target_pairs={{0,6},{2,4},{4,2},{6,0},{1,7},{3,5},{5,3},{7,1},{8,14},{10,12},{12... | collective-permute-start | bytes 688136 | tf_op jit(solution)/shard_map/ppermute | solution.py:86
  134.6 11.4 %collective-permute-start.27 = (bf16[128,896]{1,0:T(8,128)(2,1)S(1)}, bf16[128,896]{1,0:T(8,128)(2,1)S(1)}, u32[]{:S(2)}, u32[]{:S(2)}) collective-permute-start(bf16[128,896]{1,0:T(8,128)(2,1)S(1)} %get-tuple-element.156), channel_id=1, source_target_pairs={{0,4},{2,6},{4,0},{6,2},{1,5},{3,7},{5,1},{7,3},{8,12},{10,14},{12... | collective-permute-start | bytes 688136 | tf_op jit(solution)/shard_map/ppermute | solution.py:86
  135.1 11.0 %collective-permute-start.26 = (bf16[128,896]{1,0:T(8,128)(2,1)S(1)}, bf16[128,896]{1,0:T(8,128)(2,1)S(1)}, u32[]{:S(2)}, u32[]{:S(2)}) collective-permute-start(bf16[128,896]{1,0:T(8,128)(2,1)S(1)} %get-tuple-element.157), channel_id=1, source_target_pairs={{0,2},{2,0},{4,6},{6,4},{1,3},{3,1},{5,7},{7,5},{8,10},{10,8},{12,... | collective-permute-start | bytes 688136 | tf_op jit(solution)/shard_map/ppermute | solution.py:86
  137.1 12.9 %copy-start.8 = (f32[256,896]{1,0:T(8,128)S(1)}, f32[256,896]{1,0:T(8,128)}, u32[]{:S(2)}) copy-start(f32[256,896]{1,0:T(8,128)} %copy-done.7) | copy-start | bytes 2752516
  146.2 3.8 %collective-permute-start.29 = (bf16[128,896]{1,0:T(8,128)(2,1)S(1)}, bf16[128,896]{1,0:T(8,128)(2,1)S(1)}, u32[]{:S(2)}, u32[]{:S(2)}) collective-permute-start(bf16[128,896]{1,0:T(8,128)(2,1)S(1)} %add_convert_fusion.4), channel_id=1, source_target_pairs={{0,1},{1,0},{2,3},{3,2},{4,5},{5,4},{6,7},{7,6},{8,9},{9,8},{10,11... | collective-permute-start | bytes 688136 | tf_op jit(solution)/shard_map/ppermute | solution.py:60
  146.4 9.4 %collective-permute-start.32 = (bf16[128,896]{1,0:T(8,128)(2,1)S(1)}, bf16[128,896]{1,0:T(8,128)(2,1)S(1)}, u32[]{:S(2)}, u32[]{:S(2)}) collective-permute-start(bf16[128,896]{1,0:T(8,128)(2,1)S(1)} %get-tuple-element.151), channel_id=1, source_target_pairs={{0,6},{2,4},{4,2},{6,0},{1,7},{3,5},{5,3},{7,1},{8,14},{10,12},{12... | collective-permute-start | bytes 688136 | tf_op jit(solution)/shard_map/ppermute | solution.py:86
  148.1 16.7 %collective-permute-start.31 = (bf16[128,896]{1,0:T(8,128)(2,1)S(1)}, bf16[128,896]{1,0:T(8,128)(2,1)S(1)}, u32[]{:S(2)}, u32[]{:S(2)}) collective-permute-start(bf16[128,896]{1,0:T(8,128)(2,1)S(1)} %get-tuple-element.152), channel_id=1, source_target_pairs={{0,4},{2,6},{4,0},{6,2},{1,5},{3,7},{5,1},{7,3},{8,12},{10,14},{12... | collective-permute-start | bytes 688136 | tf_op jit(solution)/shard_map/ppermute | solution.py:86
  149.4 16.9 %collective-permute-start.30 = (bf16[128,896]{1,0:T(8,128)(2,1)S(1)}, bf16[128,896]{1,0:T(8,128)(2,1)S(1)}, u32[]{:S(2)}, u32[]{:S(2)}) collective-permute-start(bf16[128,896]{1,0:T(8,128)(2,1)S(1)} %get-tuple-element.153), channel_id=1, source_target_pairs={{0,2},{2,0},{4,6},{6,4},{1,3},{3,1},{5,7},{7,5},{8,10},{10,8},{12,... | collective-permute-start | bytes 688136 | tf_op jit(solution)/shard_map/ppermute | solution.py:86
  150.3 7.1 %copy-start.2 = (f32[448,256]{1,0:T(8,128)S(1)}, f32[448,256]{1,0:T(8,128)}, u32[]{:S(2)}) copy-start(f32[448,256]{1,0:T(8,128)} %copy-done.1) | copy-start | bytes 1376260
  151.2 15.6 %collective-permute-start.34 = (bf16[224,448]{1,0:T(8,128)(2,1)S(1)}, bf16[224,448]{1,0:T(8,128)(2,1)S(1)}, u32[]{:S(2)}, u32[]{:S(2)}) collective-permute-start(bf16[224,448]{1,0:T(8,128)(2,1)S(1)} %get-tuple-element.101), channel_id=1, source_target_pairs={{0,2},{2,0},{4,6},{6,4},{1,3},{3,1},{5,7},{7,5},{8,10},{10,8},{12,... | collective-permute-start | bytes 602120 | tf_op jit(solution)/shard_map/ppermute | solution.py:86
  152.8 15.6 %collective-permute-start.35 = (bf16[224,448]{1,0:T(8,128)(2,1)S(1)}, bf16[224,448]{1,0:T(8,128)(2,1)S(1)}, u32[]{:S(2)}, u32[]{:S(2)}) collective-permute-start(bf16[224,448]{1,0:T(8,128)(2,1)S(1)} %get-tuple-element.105), channel_id=1, source_target_pairs={{0,4},{2,6},{4,0},{6,2},{1,5},{3,7},{5,1},{7,3},{8,12},{10,14},{12... | collective-permute-start | bytes 602120 | tf_op jit(solution)/shard_map/ppermute | solution.py:86
  155.8 14.8 %collective-permute-start.36 = (bf16[224,448]{1,0:T(8,128)(2,1)S(1)}, bf16[224,448]{1,0:T(8,128)(2,1)S(1)}, u32[]{:S(2)}, u32[]{:S(2)}) collective-permute-start(bf16[224,448]{1,0:T(8,128)(2,1)S(1)} %get-tuple-element.106), channel_id=1, source_target_pairs={{0,6},{2,4},{4,2},{6,0},{1,7},{3,5},{5,3},{7,1},{8,14},{10,12},{12... | collective-permute-start | bytes 602120 | tf_op jit(solution)/shard_map/ppermute | solution.py:86
  164.8 7.3 %collective-permute-start.37 = (bf16[256,128]{1,0:T(8,128)(2,1)S(1)}, bf16[256,128]{1,0:T(8,128)(2,1)S(1)}, u32[]{:S(2)}, u32[]{:S(2)}) collective-permute-start(bf16[256,128]{1,0:T(8,128)(2,1)S(1)} %get-tuple-element.108), channel_id=1, source_target_pairs={{0,2},{2,0},{4,6},{6,4},{1,3},{3,1},{5,7},{7,5},{8,10},{10,8},{12,... | collective-permute-start | bytes 196616 | tf_op jit(solution)/shard_map/ppermute | solution.py:86
  166.3 5.8 %collective-permute-start.38 = (bf16[256,128]{1,0:T(8,128)(2,1)S(1)}, bf16[256,128]{1,0:T(8,128)(2,1)S(1)}, u32[]{:S(2)}, u32[]{:S(2)}) collective-permute-start(bf16[256,128]{1,0:T(8,128)(2,1)S(1)} %get-tuple-element.109), channel_id=1, source_target_pairs={{0,4},{2,6},{4,0},{6,2},{1,5},{3,7},{5,1},{7,3},{8,12},{10,14},{12... | collective-permute-start | bytes 196616 | tf_op jit(solution)/shard_map/ppermute | solution.py:86
  166.8 6.2 %collective-permute-start.39 = (bf16[256,128]{1,0:T(8,128)(2,1)S(1)}, bf16[256,128]{1,0:T(8,128)(2,1)S(1)}, u32[]{:S(2)}, u32[]{:S(2)}) collective-permute-start(bf16[256,128]{1,0:T(8,128)(2,1)S(1)} %get-tuple-element.110), channel_id=1, source_target_pairs={{0,6},{2,4},{4,2},{6,0},{1,7},{3,5},{5,3},{7,1},{8,14},{10,12},{12... | collective-permute-start | bytes 196616 | tf_op jit(solution)/shard_map/ppermute | solution.py:86
  173.8 1.9 collective-permute-start.40
  177.6 10.1 %collective-permute-start.41 = (bf16[240,576]{1,0:T(8,128)(2,1)S(1)}, bf16[240,576]{1,0:T(8,128)(2,1)S(1)}, u32[]{:S(2)}, u32[]{:S(2)}) collective-permute-start(bf16[240,576]{1,0:T(8,128)(2,1)S(1)} %get-tuple-element.115), channel_id=1, source_target_pairs={{0,2},{2,0},{4,6},{6,4},{1,3},{3,1},{5,7},{7,5},{8,10},{10,8},{12,... | collective-permute-start | bytes 829448 | tf_op jit(solution)/shard_map/ppermute | solution.py:86
  179.0 15.6 %collective-permute-start.42 = (bf16[240,576]{1,0:T(8,128)(2,1)S(1)}, bf16[240,576]{1,0:T(8,128)(2,1)S(1)}, u32[]{:S(2)}, u32[]{:S(2)}) collective-permute-start(bf16[240,576]{1,0:T(8,128)(2,1)S(1)} %get-tuple-element.116), channel_id=1, source_target_pairs={{0,4},{2,6},{4,0},{6,2},{1,5},{3,7},{5,1},{7,3},{8,12},{10,14},{12... | collective-permute-start | bytes 829448 | tf_op jit(solution)/shard_map/ppermute | solution.py:86
  179.8 14.9 %collective-permute-start.43 = (bf16[240,576]{1,0:T(8,128)(2,1)S(1)}, bf16[240,576]{1,0:T(8,128)(2,1)S(1)}, u32[]{:S(2)}, u32[]{:S(2)}) collective-permute-start(bf16[240,576]{1,0:T(8,128)(2,1)S(1)} %get-tuple-element.117), channel_id=1, source_target_pairs={{0,6},{2,4},{4,2},{6,0},{1,7},{3,5},{5,3},{7,1},{8,14},{10,12},{12... | collective-permute-start | bytes 829448 | tf_op jit(solution)/shard_map/ppermute | solution.py:86
  181.2 21.6 %collective-permute-start.33 = (bf16[128,896]{1,0:T(8,128)(2,1)S(1)}, bf16[128,896]{1,0:T(8,128)(2,1)}, u32[]{:S(2)}, u32[]{:S(2)}) collective-permute-start(bf16[128,896]{1,0:T(8,128)(2,1)S(1)} %add_convert_fusion.3), channel_id=1, source_target_pairs={{0,1},{1,0},{2,3},{3,2},{4,5},{5,4},{6,7},{7,6},{8,9},{9,8},{10,11... | collective-permute-start | bytes 688136 | tf_op jit(solution)/shard_map/ppermute | solution.py:60
  194.6 10.3 %copy-start.10 = (bf16[256,896]{1,0:T(8,128)(2,1)S(1)}, bf16[256,896]{1,0:T(8,128)(2,1)}, u32[]{:S(2)}) copy-start(bf16[256,896]{1,0:T(8,128)(2,1)} %copy-done.9) | copy-start | bytes 1376260
  194.7 10.3 %copy-start.12 = (bf16[256,896]{1,0:T(8,128)(2,1)S(1)}, bf16[256,896]{1,0:T(8,128)(2,1)}, u32[]{:S(2)}) copy-start(bf16[256,896]{1,0:T(8,128)(2,1)} %copy-done.11) | copy-start | bytes 1376260
  195.2 8.7 %collective-permute-start.44 = (bf16[72,1024]{1,0:T(8,128)(2,1)S(1)}, bf16[72,1024]{1,0:T(8,128)(2,1)S(1)}, u32[]{:S(2)}, u32[]{:S(2)}) collective-permute-start(bf16[72,1024]{1,0:T(8,128)(2,1)S(1)} %get-tuple-element.123), channel_id=1, source_target_pairs={{0,8},{8,16},{16,24},{24,0},{1,9},{9,17},{17,25},{25,1},{2,10},{10... | collective-permute-start | bytes 442376 | tf_op jit(solution)/shard_map/ppermute | solution.py:124
  195.3 13.0 %collective-permute-start.45 = (bf16[72,1024]{1,0:T(8,128)(2,1)S(1)}, bf16[72,1024]{1,0:T(8,128)(2,1)S(1)}, u32[]{:S(2)}, u32[]{:S(2)}) collective-permute-start(bf16[72,1024]{1,0:T(8,128)(2,1)S(1)} %get-tuple-element.124), channel_id=1, source_target_pairs={{0,16},{8,24},{16,0},{24,8},{1,17},{9,25},{17,1},{25,9},{2,18},{10... | collective-permute-start | bytes 442376 | tf_op jit(solution)/shard_map/ppermute | solution.py:124
  196.9 11.4 %collective-permute-start.46 = (bf16[72,1024]{1,0:T(8,128)(2,1)S(1)}, bf16[72,1024]{1,0:T(8,128)(2,1)S(1)}, u32[]{:S(2)}, u32[]{:S(2)}) collective-permute-start(bf16[72,1024]{1,0:T(8,128)(2,1)S(1)} %get-tuple-element.125), channel_id=1, source_target_pairs={{0,24},{8,0},{16,8},{24,16},{1,25},{9,1},{17,9},{25,17},{2,26},{10... | collective-permute-start | bytes 442376 | tf_op jit(solution)/shard_map/ppermute | solution.py:124
  201.4 8.9 %collective-permute-start.49 = (bf16[56,1920]{1,0:T(8,128)(2,1)}, bf16[56,1920]{1,0:T(8,128)(2,1)S(1)}, u32[]{:S(2)}, u32[]{:S(2)}) collective-permute-start(bf16[56,1920]{1,0:T(8,128)(2,1)} %get-tuple-element.163), channel_id=1, source_target_pairs={{0,6},{2,4},{4,2},{6,0},{1,7},{3,5},{5,3},{7,1},{8,14},{10,12},{12... | collective-permute-start | bytes 645128 | tf_op jit(solution)/shard_map/ppermute | solution.py:86
  202.8 9.7 %collective-permute-start.48 = (bf16[56,1920]{1,0:T(8,128)(2,1)}, bf16[56,1920]{1,0:T(8,128)(2,1)S(1)}, u32[]{:S(2)}, u32[]{:S(2)}) collective-permute-start(bf16[56,1920]{1,0:T(8,128)(2,1)} %get-tuple-element.164), channel_id=1, source_target_pairs={{0,4},{2,6},{4,0},{6,2},{1,5},{3,7},{5,1},{7,3},{8,12},{10,14},{12... | collective-permute-start | bytes 645128 | tf_op jit(solution)/shard_map/ppermute | solution.py:86
  203.9 8.7 %collective-permute-start.47 = (bf16[56,1920]{1,0:T(8,128)(2,1)}, bf16[56,1920]{1,0:T(8,128)(2,1)S(1)}, u32[]{:S(2)}, u32[]{:S(2)}) collective-permute-start(bf16[56,1920]{1,0:T(8,128)(2,1)} %get-tuple-element.165), channel_id=1, source_target_pairs={{0,2},{2,0},{4,6},{6,4},{1,3},{3,1},{5,7},{7,5},{8,10},{10,8},{12,... | collective-permute-start | bytes 645128 | tf_op jit(solution)/shard_map/ppermute | solution.py:86
  (17 other events, 27.7 us)
Sparse Core Ops, SparseCore 0:
  32.0 68.0 all-gather.1
  117.4 63.4 reduce-scatter.1
where the time goes:
time: 221 us
  waiting for transfers between devices  72.6 us (33%)
  starting transfers between devices  57.1 us (26%)
  matrix products  23.6 us (11%)
  local copies, waits for them, and re-layouts  18.8 us (9%)
  Pallas kernels  18.4 us (8%)
  other arithmetic  15.6 us (7%)
  between operations  14.7 us (7%)
    ppermute x21, waiting for transfers between devices, trade(): lax.ppermute(parts[step], 'ctx', flips(size, step))  37.7 us
    ppermute x21, starting transfers between devices, trade(): lax.ppermute(parts[step], 'ctx', flips(size, step))  24.6 us
    ppermute x15, waiting for transfers between devices, spread(): lax.ppermute(values, 'ctx', flips(size, step))  23.6 us
    ppermute x15, starting transfers between devices, spread(): lax.ppermute(values, 'ctx', flips(size, step))  20.7 us
    unnamed x67, local copies, waits for them, and re-layouts  11.9 us
    dot_general x2, matrix products, dot(): return jnp.dot(left, right, preferred_element_type=F32)  9 us
    dot_general x3, matrix products, dot_rows(): lax.dot_general(left, right, (((1,), (1,)), ((), ())), preferred_element_...  8.81 us
    pallas_call x1, Pallas kernels, attend_bwd(): pl.pallas_call(functools.partial(bwd_kernel, n), out_shape=(jax.ShapeDtyp...  7.4 us
  transfers between devices with their start and end apart: 52, of which 27 were waited for; matrix products, arithmetic and copies ran while one was open for 13% of the time, Pallas kernels for 8%

commit v1 on v0

--- a/solution.py
+++ b/solution.py
@@ -18,6 +18,8 @@
 LANES = 128
 SPLIT = 512
 SMALL_ROWS = 16
+BLOCK = 512
+MLP_VMEM = 32 * 2**20
 VMEM_BYTES = 16 * 2**20
 FREE = pl.CostEstimate(flops=0, bytes_accessed=0, transcendentals=0)
 IN_VMEM = pl.BlockSpec(memory_space=pltpu.VMEM)
@@ -389,6 +391,45 @@
     return list(outs)
 
 
+def mlp_kernel(chunk, first_ref, second_ref, top_one_ref, top_two_ref, weights, *refs):
+    grad_one_ref, grad_two_ref, hidden_ref, both_ref = refs
+    rows = first_ref.shape[0]
+    block = min(rows, BLOCK)
+    for half, (tokens_ref, top_ref, grad_ref) in enumerate(
+        ((first_ref, top_one_ref, grad_one_ref), (second_ref, top_two_ref, grad_two_ref))
+    ):
+        for begin in range(0, rows, block):
+            here = slice(begin, begin + block)
+            there = slice(half * rows + begin, half * rows + begin + block)
+            gate_up = dot(tokens_ref[here, :], weights[:, : 2 * chunk])
+            grad_hidden = dot(top_ref[here, :], weights[:, 2 * chunk :])
+            gate, upward = gate_up[:, :chunk], gate_up[:, chunk:]
+            sigmoid = jax.nn.sigmoid(gate)
+            swish = gate * sigmoid
+            hidden_ref[there, :] = (swish * upward).astype(BF)
+            slope = sigmoid + swish * (1.0 - sigmoid)
+            both_ref[there, :chunk] = (grad_hidden * upward * slope).astype(BF)
+            both_ref[there, chunk:] = (grad_hidden * swish).astype(BF)
+            grad_ref[here, :] = dot_rows(both_ref[there, :], weights[:, : 2 * chunk]).astype(BF)
+
+
+def mlp(halves, tops, weights, chunk):
+    rows, features = halves[0].shape
+    return pl.pallas_call(
+        functools.partial(mlp_kernel, chunk),
+        out_shape=(jax.ShapeDtypeStruct((rows, features), BF),) * 2
+        + (
+            jax.ShapeDtypeStruct((2 * rows, chunk), BF),
+            jax.ShapeDtypeStruct((2 * rows, 2 * chunk), BF),
+        ),
+        in_specs=[IN_VMEM] * 5,
+        out_specs=(IN_VMEM,) * 4,
+        compiler_params=pltpu.CompilerParams(vmem_limit_bytes=MLP_VMEM),
+        cost_estimate=FREE,
+        name="mlp",
+    )(*halves, *tops, weights)
+
+
 def weight_grad_kernel(count, lines, own_ref, left_ref, right_ref, *refs):
     pieces, whole = refs[:count], refs[count]
     whole[...] = turned_dot(left_ref[...], right_ref[...])
@@ -834,19 +875,23 @@
 
     gate_up, down_turned = mlp_rows[:, : 2 * chunk], mlp_rows[:, 2 * chunk :]
     normed_all, grad_top_all = jnp.concatenate(halves), jnp.concatenate(tops)
-    gate_upward = dot(normed_all, gate_up)
-    grad_hidden = dot(grad_top_all, down_turned)
-    gate_values, upward = gate_upward[:, :chunk], gate_upward[:, chunk:]
-    sigmoid_gate = jax.nn.sigmoid(gate_values)
-    swish_gate = gate_values * sigmoid_gate
-    hidden = (swish_gate * upward).astype(jnp.bfloat16)
-    slope = sigmoid_gate + swish_gate * (1.0 - sigmoid_gate)
-    grad_both = jnp.concatenate(
-        [grad_hidden * upward * slope, grad_hidden * swish_gate], axis=-1
-    ).astype(jnp.bfloat16)
-    grad_one, grad_two = jnp.split(dot_rows(grad_both, gate_up).astype(jnp.bfloat16), 2)
+    if few():
+        grad_one, grad_two, hidden, grad_both = mlp(halves, tops, mlp_rows, chunk)
+    else:
+        gate_upward = dot(normed_all, gate_up)
+        grad_hidden = dot(grad_top_all, down_turned)
+        gate_values, upward = gate_upward[:, :chunk], gate_upward[:, chunk:]
+        sigmoid_gate = jax.nn.sigmoid(gate_values)
+        swish_gate = gate_values * sigmoid_gate
+        hidden = (swish_gate * upward).astype(jnp.bfloat16)
+        slope = sigmoid_gate + swish_gate * (1.0 - sigmoid_gate)
+        grad_both = jnp.concatenate(
+            [grad_hidden * upward * slope, grad_hidden * swish_gate], axis=-1
+        ).astype(jnp.bfloat16)
+        grad_one, grad_two = jnp.split(dot_rows(grad_both, gate_up).astype(jnp.bfloat16), 2)
     grad_normed_sum = add_cores(grad_one, grad_two)
     grad_normed_parts = trade(jnp.split(grad_normed_sum, ctx_size))
+    grad_both, grad_normed_sum = lax.optimization_barrier((grad_both, grad_normed_sum))
     mlp_grad = jnp.concatenate(
         [
             turned_dot(normed_all, grad_both).astype(jnp.bfloat16),
@@ -856,7 +901,7 @@
     ).reshape(fsdp_size, ctx_size * rows, 3 * chunk)
     mlp_mine = lax.psum_scatter(mlp_grad, "fsdp", scatter_dimension=0, tiled=False)
     branch_two_sum = add_cores(
-        *jnp.split(dot_rows(hidden, down_turned).astype(jnp.bfloat16), 2)
+        *jnp.split(dot_rows(after(hidden, grad_normed_sum), down_turned).astype(jnp.bfloat16), 2)
     )
     branch_two_sum, *grad_normed_parts = lax.optimization_barrier(
         (branch_two_sum, *grad_normed_parts)

time: 221 us -> 216 us (0.977)
  matrix products: 23.6 us -> 8.08 us
  Pallas kernels: 18.4 us -> 26.1 us
  waiting for transfers between devices: 72.6 us -> 75.1 us
    dot_general x2 -> x0, matrix products: 9 us -> none  [dot(): return jnp.dot(left, right, preferred_element_type=F32)]
    pallas_call x0 -> x1, Pallas kernels: none -> 7.73 us  [mlp(): pl.pallas_call(functools.partial(mlp_kernel, chunk), out_shape=(jax.Shape...]
    dot_general x3 -> x2, matrix products: 8.81 us -> 3.86 us  [dot_rows(): lax.dot_general(left, right, (((1,), (1,)), ((), ())), preferred_element_...]
    unnamed x67 -> x106, local copies, waits for them, and re-layouts: 11.9 us -> 14.8 us
  transfers between devices with their start and end apart: 52 -> 52, of which waited for: 27 -> 29; matrix products, arithmetic and copies ran while one was open for 13% -> 9% of each run, Pallas kernels for 8% -> 8%
where the time goes in v1:
time: 216 us; the launch traced here: 215 us
  waiting for transfers between devices  75.1 us (35%)
  starting transfers between devices  57.1 us (26%)
  Pallas kernels  26.1 us (12%)
  local copies, waits for them, and re-layouts  19.8 us (9%)
  between operations  14.9 us (7%)
  other arithmetic  14.1 us (7%)
  matrix products  8.08 us (4%)
    ppermute x21, waiting for transfers between devices, trade(): lax.ppermute(parts[step], 'ctx', flips(size, step))  36.9 us
    ppermute x21, starting transfers between devices, trade(): lax.ppermute(parts[step], 'ctx', flips(size, step))  24.6 us
    ppermute x15, waiting for transfers between devices, spread(): lax.ppermute(values, 'ctx', flips(size, step))  23.6 us
    ppermute x15, starting transfers between devices, spread(): lax.ppermute(values, 'ctx', flips(size, step))  20.7 us
    unnamed x106, local copies, waits for them, and re-layouts  14.8 us
    all_gather x1, waiting for transfers between devices, body(): mlp_rows = lax.all_gather(recut, 'fsdp', axis=0, tiled=True)  8.06 us
    pallas_call x1, Pallas kernels, mlp(): pl.pallas_call(functools.partial(mlp_kernel, chunk), out_shape=(jax.Shape...  7.73 us
    pallas_call x1, Pallas kernels, attend_bwd(): pl.pallas_call(functools.partial(bwd_kernel, n), out_shape=(jax.ShapeDtyp...  7.39 us
  transfers between devices with their start and end apart: 52, of which 29 were waited for; matrix products, arithmetic and copies ran while one was open for 9% of the time, Pallas kernels for 8%

profile of v1, /device:TPU:0, one launch (start us, length us, event | category | flops | bytes accessed | tf_op | source)
XLA Modules:
  0.0 215.1 jit_solution(2187378470923904605)
XLA Ops:
  8.2 3.1 %collective-permute-start.2 = (bf16[56,1024]{1,0:T(8,128)(2,1)S(1)}, bf16[56,1024]{1,0:T(8,128)(2,1)S(1)}, u32[]{:S(2)}, u32[]{:S(2)}) collective-permute-start(bf16[56,1024]{1,0:T(8,128)(2,1)S(1)} %pad_maximum_fusion.7), channel_id=1, source_target_pairs={{0,8},{8,16},{16,24},{24,0},{1,9},{9,17},{17,25},{25,1},{2,10},{10... | collective-permute-start | bytes 344072 | tf_op jit(solution)/shard_map/ppermute | solution.py:116
  11.3 2.6 %collective-permute-start.1 = (bf16[56,1024]{1,0:T(8,128)(2,1)S(1)}, bf16[56,1024]{1,0:T(8,128)(2,1)S(1)}, u32[]{:S(2)}, u32[]{:S(2)}) collective-permute-start(bf16[56,1024]{1,0:T(8,128)(2,1)S(1)} %pad_maximum_fusion.7), channel_id=1, source_target_pairs={{0,16},{8,24},{16,0},{24,8},{1,17},{9,25},{17,1},{25,9},{2,18},{10... | collective-permute-start | bytes 344072 | tf_op jit(solution)/shard_map/ppermute | solution.py:116
  13.9 1.3 collective-permute-start
  18.3 1.6 collective-permute-start.21
  19.8 1.5 collective-permute-start.22
  24.5 4.9 %collective-permute-done.22 = bf16[56,1920]{1,0:T(8,128)(2,1)S(1)} collective-permute-done((bf16[56,1920]{1,0:T(8,128)(2,1)S(1)}, bf16[56,1920]{1,0:T(8,128)(2,1)S(1)}, u32[]{:S(2)}, u32[]{:S(2)}) %collective-permute-start.22) | collective-permute-done | bytes 215072 | tf_op jit(solution)/shard_map/ppermute | solution.py:88
  29.4 1.2 collective-permute-done.23
  30.8 1.1 pad_maximum_fusion.6
  32.1 1.4 collective-permute-start.4
  34.0 1.7 collective-permute-start.5
  35.8 1.4 collective-permute-start.13
  37.9 6.1 %collective-permute-done.4 = bf16[4,56,576]{2,1,0:T(8,128)(2,1)S(1)} collective-permute-done((bf16[4,56,576]{2,1,0:T(8,128)(2,1)S(1)}, bf16[4,56,576]{2,1,0:T(8,128)(2,1)S(1)}, u32[]{:S(2)}, u32[]{:S(2)}) %collective-permute-start.4) | collective-permute-done | bytes 258080 | tf_op jit(solution)/shard_map/ppermute | solution.py:80
  44.0 2.7 %collective-permute-start.14 = (bf16[4,56,448]{2,1,0:T(8,128)(2,1)S(1)}, bf16[4,56,448]{2,1,0:T(8,128)(2,1)S(1)}, u32[]{:S(2)}, u32[]{:S(2)}) collective-permute-start(bf16[4,56,448]{2,1,0:T(8,128)(2,1)S(1)} %constant_dynamic-slice_fusion.14), channel_id=1, source_target_pairs={{0,6},{2,4},{4,2},{6,0},{1,7},{3,5},{5,3},{7,1},{8,14},{10,12},{12... | collective-permute-start | bytes 602120 | tf_op jit(solution)/shard_map/ppermute | solution.py:80
  46.7 2.9 %collective-permute-done.5 = bf16[4,56,576]{2,1,0:T(8,128)(2,1)S(1)} collective-permute-done((bf16[4,56,576]{2,1,0:T(8,128)(2,1)S(1)}, bf16[4,56,576]{2,1,0:T(8,128)(2,1)S(1)}, u32[]{:S(2)}, u32[]{:S(2)}) %collective-permute-start.5) | collective-permute-done | bytes 258080 | tf_op jit(solution)/shard_map/ppermute | solution.py:80
  51.9 1.3 collective-permute-start.8
  53.2 1.2 collective-permute-start.7
  54.4 1.1 collective-permute-start.6
  55.5 1.6 collective-permute-done.14
  59.5 2.9 %collective-permute-start.11 = (bf16[128,896]{1,0:T(8,128)(2,1)S(1)}, bf16[128,896]{1,0:T(8,128)(2,1)S(1)}, u32[]{:S(2)}, u32[]{:S(2)}) collective-permute-start(bf16[128,896]{1,0:T(8,128)(2,1)S(1)} %constant_dynamic-slice_fusion.9), channel_id=1, source_target_pairs={{0,6},{2,4},{4,2},{6,0},{1,7},{3,5},{5,3},{7,1},{8,14},{10,12},{12... | collective-permute-start | bytes 688136 | tf_op jit(solution)/shard_map/ppermute | solution.py:80
  62.3 2.6 %collective-permute-start.10 = (bf16[128,896]{1,0:T(8,128)(2,1)S(1)}, bf16[128,896]{1,0:T(8,128)(2,1)S(1)}, u32[]{:S(2)}, u32[]{:S(2)}) collective-permute-start(bf16[128,896]{1,0:T(8,128)(2,1)S(1)} %constant_dynamic-slice_fusion.9), channel_id=1, source_target_pairs={{0,4},{2,6},{4,0},{6,2},{1,5},{3,7},{5,1},{7,3},{8,12},{10,14},{12... | collective-permute-start | bytes 688136 | tf_op jit(solution)/shard_map/ppermute | solution.py:80
  65.3 4.2 %attend_forward.1 = (bf16[256,448]{1,0:T(8,128)(2,1)S(1)}, f32[448,256]{1,0:T(8,128)S(1)}, f32[7,256]{1,0:T(8,128)S(1)}, s32[1,256]{1,0:T(1,128)S(1)}) custom-call(s32[1]{0:T(128)} %bitcast.1.own_ref, bf16[256,448]{1,0:T(8,128)(2,1)S(1)} %get-tuple-element.81.q_ref, s32[1,256]{1,0:T(1,128)S(1)} %copy-done.25, ...), custom_call_target="tpu_custom_call" | custom-call | tf_op jit(solution)/shard_map/attend_forward/pallas_call | solution.py:308
  71.6 1.8 collective-permute-done.15
  75.0 1.9 collective-permute-start.18
  78.5 5.9 %collective-permute-done.18 = bf16[128,896]{1,0:T(8,128)(2,1)S(1)} collective-permute-done((bf16[128,896]{1,0:T(8,128)(2,1)S(1)}, bf16[128,896]{1,0:T(8,128)(2,1)S(1)}, u32[]{:S(2)}, u32[]{:S(2)}) %collective-permute-start.18) | collective-permute-done | bytes 229408 | tf_op jit(solution)/shard_map/ppermute | solution.py:80
  84.4 4.1 %collective-permute-done.17 = bf16[128,896]{1,0:T(8,128)(2,1)S(1)} collective-permute-done((bf16[128,896]{1,0:T(8,128)(2,1)S(1)}, bf16[128,896]{1,0:T(8,128)(2,1)S(1)}, u32[]{:S(2)}, u32[]{:S(2)}) %collective-permute-start.17) | collective-permute-done | bytes 229408 | tf_op jit(solution)/shard_map/ppermute | solution.py:80
  92.0 8.1 %all-gather.2.cloned.1.call-done.weights = bf16[896,1920]{1,0:T(8,128)(2,1)} async-done(((bf16[224,1920]{1,0:T(8,128)(2,1)}), bf16[896,1920]{1,0:T(8,128)(2,1)}) %all-gather.2.cloned.1.call-update) | async-done | bytes 3440656 | tf_op jit(solution)/shard_map/all_gather | solution.py:798
  100.1 1.2 copy-done.2
  101.3 1.2 copy-done.4
  102.5 2.0 copy-done.5
  104.4 1.2 copy-done.11
  105.6 7.7 %mlp.1 = (bf16[512,896]{1,0:T(8,128)(2,1)S(1)}, bf16[512,896]{1,0:T(8,128)(2,1)S(1)}, bf16[1024,640]{1,0:T(8,128)(2,1)S(1)}, bf16[1024,1280]{1,0:T(8,128)(2,1)S(1)}) custom-call(bf16[512,896]{1,0:T(8,128)(2,1)S(1)} %copy-done.4, bf16[512,896]{1,0:T(8,128)(2,1)S(1)} %copy-done.2, bf16[512,896]{1,0:T(8,128)(2,1)S(1)} %pad_maximum_fusion.2.top_one_ref, ...), custom_call_target="tpu_custom_call" | custom-call | tf_op jit(solution)/shard_map/mlp/pallas_call | solution.py:418
  113.7 1.6 fusion.4
  116.1 2.6 %convolution_convert_fusion = bf16[896,1280]{1,0:T(8,128)(2,1)S(1)} fusion(bf16[1024,896]{1,0:T(8,128)(2,1)S(1)} %constant_dynamic-update-slice_fusion, bf16[1024,1280]{1,0:T(8,128)(2,1)S(1)} %get-tuple-element.144), kind=kOutput, calls=%fused_computation | convolution fusion | flops 2349957120 | bytes 6750208 | tf_op jit(solution)/shard_map/dot_general | solution.py:40
  118.7 2.0 pad_maximum_fusion
  120.8 3.4 %convolution_convert_fusion.1 = bf16[1024,896]{1,0:T(8,128)(2,1)S(1)} fusion(bf16[1024,640]{1,0:T(8,128)(2,1)} %copy-done.26, bf16[896,1920]{1,0:T(8,128)(2,1)} %all-gather.2.cloned.1.call-done.weights), kind=kOutput, calls=%fused_computation.8 | convolution fusion | flops 1175322624 | bytes 4292608 | tf_op jit(solution)/shard_map/dot_general | solution.py:36
  124.2 1.2 copy-done.33
  126.7 2.5 %collective-permute-start.28 = (bf16[128,896]{1,0:T(8,128)(2,1)S(1)}, bf16[128,896]{1,0:T(8,128)(2,1)S(1)}, u32[]{:S(2)}, u32[]{:S(2)}) collective-permute-start(bf16[128,896]{1,0:T(8,128)(2,1)S(1)} %get-tuple-element.162), channel_id=1, source_target_pairs={{0,6},{2,4},{4,2},{6,0},{1,7},{3,5},{5,3},{7,1},{8,14},{10,12},{12... | collective-permute-start | bytes 688136 | tf_op jit(solution)/shard_map/ppermute | solution.py:88
  130.2 1.4 add_convert_fusion.1
  131.6 4.4 %collective-permute-done.28 = bf16[128,896]{1,0:T(8,128)(2,1)S(1)} collective-permute-done((bf16[128,896]{1,0:T(8,128)(2,1)S(1)}, bf16[128,896]{1,0:T(8,128)(2,1)S(1)}, u32[]{:S(2)}, u32[]{:S(2)}) %collective-permute-start.28) | collective-permute-done | bytes 229408 | tf_op jit(solution)/shard_map/ppermute | solution.py:88
  136.1 4.3 %collective-permute-done.27 = bf16[128,896]{1,0:T(8,128)(2,1)S(1)} collective-permute-done((bf16[128,896]{1,0:T(8,128)(2,1)S(1)}, bf16[128,896]{1,0:T(8,128)(2,1)S(1)}, u32[]{:S(2)}, u32[]{:S(2)}) %collective-permute-start.27) | collective-permute-done | bytes 229408 | tf_op jit(solution)/shard_map/ppermute | solution.py:88
  140.8 1.7 collective-permute-start.32
  142.5 1.3 collective-permute-start.31
  146.2 1.5 collective-permute-start.34
  148.5 1.8 collective-permute-done.32
  150.2 1.6 collective-permute-start.36
  151.9 7.4 %attend_backward.1 = (bf16[256,448]{1,0:T(8,128)(2,1)S(1)}, bf16[256,128]{1,0:T(8,128)(2,1)S(1)}, bf16[256,128]{1,0:T(8,128)(2,1)S(1)}, bf16[256,128]{1,0:T(8,128)(2,1)S(1)}, bf16[256,128]{1,0:T(8,128)(2,1)S(1)}) custom-call(s32[1]{0:T(128)} %bitcast.1.own_ref, bf16[256,448]{1,0:T(8,128)(2,1)S(1)} %copy-done.7, s32[1,256]{1,0:T(1,128)S(1)} %get-tuple-element.86.start_ref, ...), custom_call_target="tpu_custom_call" | custom-call | tf_op jit(solution)/shard_map/attend_backward/pallas_call | solution.py:354
  159.3 1.4 collective-permute-start.37
  161.2 1.6 collective-permute-start.39
  162.9 2.2 %collective-permute-done.36.refs_7_ = bf16[224,448]{1,0:T(8,128)(2,1)S(1)} collective-permute-done((bf16[224,448]{1,0:T(8,128)(2,1)S(1)}, bf16[224,448]{1,0:T(8,128)(2,1)S(1)}, u32[]{:S(2)}, u32[]{:S(2)}) %collective-permute-start.36) | collective-permute-done | bytes 200736 | tf_op jit(solution)/shard_map/ppermute | solution.py:88
  165.0 1.4 collective-permute-done.37.refs_1_
  168.3 1.8 collective-permute-done.40.second_ref
  170.1 1.9 last_grads.1
  172.0 1.5 collective-permute-start.41
  174.2 1.3 collective-permute-start.43
  175.7 6.4 %collective-permute-done.41.refs_1_ = bf16[240,576]{1,0:T(8,128)(2,1)S(1)} collective-permute-done((bf16[240,576]{1,0:T(8,128)(2,1)S(1)}, bf16[240,576]{1,0:T(8,128)(2,1)S(1)}, u32[]{:S(2)}, u32[]{:S(2)}) %collective-permute-start.41) | collective-permute-done | bytes 276512 | tf_op jit(solution)/shard_map/ppermute | solution.py:88
  182.1 7.0 %collective-permute-done.42.refs_2_ = bf16[240,576]{1,0:T(8,128)(2,1)S(1)} collective-permute-done((bf16[240,576]{1,0:T(8,128)(2,1)S(1)}, bf16[240,576]{1,0:T(8,128)(2,1)S(1)}, u32[]{:S(2)}, u32[]{:S(2)}) %collective-permute-start.42) | collective-permute-done | bytes 276512 | tf_op jit(solution)/shard_map/ppermute | solution.py:88
  189.7 1.5 collective-permute-start.45
  191.2 2.5 %collective-permute-start.46 = (bf16[72,1024]{1,0:T(8,128)(2,1)S(1)}, bf16[72,1024]{1,0:T(8,128)(2,1)S(1)}, u32[]{:S(2)}, u32[]{:S(2)}) collective-permute-start(bf16[72,1024]{1,0:T(8,128)(2,1)S(1)} %get-tuple-element.133), channel_id=1, source_target_pairs={{0,24},{8,0},{16,8},{24,16},{1,25},{9,1},{17,9},{25,17},{2,26},{10... | collective-permute-start | bytes 442376 | tf_op jit(solution)/shard_map/ppermute | solution.py:126
  193.6 2.1 dynamic-slice_bitcast_fusion
  195.7 1.4 collective-permute-start.49
  199.3 2.1 fusion.14
  201.4 1.3 collective-permute-done.45.refs_2_
  204.7 2.2 %collective-permute-done.48.refs_2_ = bf16[56,1920]{1,0:T(8,128)(2,1)S(1)} collective-permute-done((bf16[56,1920]{1,0:T(8,128)(2,1)}, bf16[56,1920]{1,0:T(8,128)(2,1)S(1)}, u32[]{:S(2)}, u32[]{:S(2)}) %collective-permute-start.48) | collective-permute-done | bytes 215072 | tf_op jit(solution)/shard_map/ppermute | solution.py:88
  207.0 1.3 mlp_out.1
  (212 shorter events, 37.4 us)
Async XLA Ops:
  7.2 17.2 %copy-start.45 = (bf16[56,64]{1,0:T(8,128)(2,1)S(1)}, bf16[56,64]{1,0:T(8,128)(2,1)}, u32[]{:S(2)}) copy-start(bf16[56,64]{1,0:T(8,128)(2,1)} %param.24) | copy-start | bytes 21508
  7.2 17.2 %copy-start.46 = (bf16[56,64]{1,0:T(8,128)(2,1)S(1)}, bf16[56,64]{1,0:T(8,128)(2,1)}, u32[]{:S(2)}) copy-start(bf16[56,64]{1,0:T(8,128)(2,1)} %param.22) | copy-start | bytes 21508
  7.2 17.2 %copy-start.44 = (bf16[56,448]{1,0:T(8,128)(2,1)S(1)}, bf16[56,448]{1,0:T(8,128)(2,1)}, u32[]{:S(2)}) copy-start(bf16[56,448]{1,0:T(8,128)(2,1)} %param.20) | copy-start | bytes 150532
  7.2 17.2 %copy-start.43 = (bf16[448,56]{0,1:T(8,128)(2,1)S(1)}, bf16[448,56]{0,1:T(8,128)(2,1)}, u32[]{:S(2)}) copy-start(bf16[448,56]{0,1:T(8,128)(2,1)} %param.26) | copy-start | bytes 150532
  7.2 92.9 %all-gather.2.cloned.1.call-start = ((), (), s32[]{:S(2)}) async-start(), calls=%async_computation.1 | async-start | bytes 4300800 | tf_op jit(solution)/shard_map/all_gather | solution.py:798
  8.2 16.1 %collective-permute-start.2 = (bf16[56,1024]{1,0:T(8,128)(2,1)S(1)}, bf16[56,1024]{1,0:T(8,128)(2,1)S(1)}, u32[]{:S(2)}, u32[]{:S(2)}) collective-permute-start(bf16[56,1024]{1,0:T(8,128)(2,1)S(1)} %pad_maximum_fusion.7), channel_id=1, source_target_pairs={{0,8},{8,16},{16,24},{24,0},{1,9},{9,17},{17,25},{25,1},{2,10},{10... | collective-permute-start | bytes 344072 | tf_op jit(solution)/shard_map/ppermute | solution.py:116
  11.3 13.0 %collective-permute-start.1 = (bf16[56,1024]{1,0:T(8,128)(2,1)S(1)}, bf16[56,1024]{1,0:T(8,128)(2,1)S(1)}, u32[]{:S(2)}, u32[]{:S(2)}) collective-permute-start(bf16[56,1024]{1,0:T(8,128)(2,1)S(1)} %pad_maximum_fusion.7), channel_id=1, source_target_pairs={{0,16},{8,24},{16,0},{24,8},{1,17},{9,25},{17,1},{25,9},{2,18},{10... | collective-permute-start | bytes 344072 | tf_op jit(solution)/shard_map/ppermute | solution.py:116
  13.9 9.8 %collective-permute-start = (bf16[56,1024]{1,0:T(8,128)(2,1)S(1)}, bf16[56,1024]{1,0:T(8,128)(2,1)S(1)}, u32[]{:S(2)}, u32[]{:S(2)}) collective-permute-start(bf16[56,1024]{1,0:T(8,128)(2,1)S(1)} %pad_maximum_fusion.7), channel_id=1, source_target_pairs={{0,24},{8,0},{16,8},{24,16},{1,25},{9,1},{17,9},{25,17},{2,26},{10... | collective-permute-start | bytes 344072 | tf_op jit(solution)/shard_map/ppermute | solution.py:116
  18.3 6.3 %collective-permute-start.21 = (bf16[56,1920]{1,0:T(8,128)(2,1)S(1)}, bf16[56,1920]{1,0:T(8,128)(2,1)S(1)}, u32[]{:S(2)}, u32[]{:S(2)}) collective-permute-start(bf16[56,1920]{1,0:T(8,128)(2,1)S(1)} %get-tuple-element.91), channel_id=1, source_target_pairs={{0,2},{2,0},{4,6},{6,4},{1,3},{3,1},{5,7},{7,5},{8,10},{10,8},{12,... | collective-permute-start | bytes 645128 | tf_op jit(solution)/shard_map/ppermute | solution.py:88
  19.8 9.6 %collective-permute-start.22 = (bf16[56,1920]{1,0:T(8,128)(2,1)S(1)}, bf16[56,1920]{1,0:T(8,128)(2,1)S(1)}, u32[]{:S(2)}, u32[]{:S(2)}) collective-permute-start(bf16[56,1920]{1,0:T(8,128)(2,1)S(1)} %get-tuple-element.92), channel_id=1, source_target_pairs={{0,4},{2,6},{4,0},{6,2},{1,5},{3,7},{5,1},{7,3},{8,12},{10,14},{12... | collective-permute-start | bytes 645128 | tf_op jit(solution)/shard_map/ppermute | solution.py:88
  23.7 6.8 %collective-permute-start.23 = (bf16[56,1920]{1,0:T(8,128)(2,1)S(1)}, bf16[56,1920]{1,0:T(8,128)(2,1)S(1)}, u32[]{:S(2)}, u32[]{:S(2)}) collective-permute-start(bf16[56,1920]{1,0:T(8,128)(2,1)S(1)} %get-tuple-element.93), channel_id=1, source_target_pairs={{0,6},{2,4},{4,2},{6,0},{1,7},{3,5},{5,3},{7,1},{8,14},{10,12},{12... | collective-permute-start | bytes 645128 | tf_op jit(solution)/shard_map/ppermute | solution.py:88
  31.9 161.7 %reduce-scatter.2.cloned.1.call-start = ((), (), s32[]{:S(2)}) async-start(), calls=%async_computation.2 | async-start | bytes 4300800 | tf_op jit(solution)/shard_map/reduce_scatter | solution.py:902
  32.1 11.9 %collective-permute-start.4 = (bf16[4,56,576]{2,1,0:T(8,128)(2,1)S(1)}, bf16[4,56,576]{2,1,0:T(8,128)(2,1)S(1)}, u32[]{:S(2)}, u32[]{:S(2)}) collective-permute-start(bf16[4,56,576]{2,1,0:T(8,128)(2,1)S(1)} %constant_dynamic-slice_fusion), channel_id=1, source_target_pairs={{0,4},{2,6},{4,0},{6,2},{1,5},{3,7},{5,1},{7,3},{8,12},{10,14},{12... | collective-permute-start | bytes 774152 | tf_op jit(solution)/shard_map/ppermute | solution.py:80
  33.4 13.3 %collective-permute-start.3 = (bf16[4,56,576]{2,1,0:T(8,128)(2,1)S(1)}, bf16[4,56,576]{2,1,0:T(8,128)(2,1)S(1)}, u32[]{:S(2)}, u32[]{:S(2)}) collective-permute-start(bf16[4,56,576]{2,1,0:T(8,128)(2,1)S(1)} %constant_dynamic-slice_fusion), channel_id=1, source_target_pairs={{0,2},{2,0},{4,6},{6,4},{1,3},{3,1},{5,7},{7,5},{8,10},{10,8},{12,... | collective-permute-start | bytes 774152 | tf_op jit(solution)/shard_map/ppermute | solution.py:80
  34.0 15.7 %collective-permute-start.5 = (bf16[4,56,576]{2,1,0:T(8,128)(2,1)S(1)}, bf16[4,56,576]{2,1,0:T(8,128)(2,1)S(1)}, u32[]{:S(2)}, u32[]{:S(2)}) collective-permute-start(bf16[4,56,576]{2,1,0:T(8,128)(2,1)S(1)} %constant_dynamic-slice_fusion), channel_id=1, source_target_pairs={{0,6},{2,4},{4,2},{6,0},{1,7},{3,5},{5,3},{7,1},{8,14},{10,12},{12... | collective-permute-start | bytes 774152 | tf_op jit(solution)/shard_map/ppermute | solution.py:80
  35.8 18.6 %collective-permute-start.13 = (bf16[4,56,448]{2,1,0:T(8,128)(2,1)S(1)}, bf16[4,56,448]{2,1,0:T(8,128)(2,1)S(1)}, u32[]{:S(2)}, u32[]{:S(2)}) collective-permute-start(bf16[4,56,448]{2,1,0:T(8,128)(2,1)S(1)} %constant_dynamic-slice_fusion.14), channel_id=1, source_target_pairs={{0,4},{2,6},{4,0},{6,2},{1,5},{3,7},{5,1},{7,3},{8,12},{10,14},{12... | collective-permute-start | bytes 602120 | tf_op jit(solution)/shard_map/ppermute | solution.py:80
  37.1 18.3 %collective-permute-start.12 = (bf16[4,56,448]{2,1,0:T(8,128)(2,1)S(1)}, bf16[4,56,448]{2,1,0:T(8,128)(2,1)S(1)}, u32[]{:S(2)}, u32[]{:S(2)}) collective-permute-start(bf16[4,56,448]{2,1,0:T(8,128)(2,1)S(1)} %constant_dynamic-slice_fusion.14), channel_id=1, source_target_pairs={{0,2},{2,0},{4,6},{6,4},{1,3},{3,1},{5,7},{7,5},{8,10},{10,8},{12,... | collective-permute-start | bytes 602120 | tf_op jit(solution)/shard_map/ppermute | solution.py:80
  44.0 13.1 %collective-permute-start.14 = (bf16[4,56,448]{2,1,0:T(8,128)(2,1)S(1)}, bf16[4,56,448]{2,1,0:T(8,128)(2,1)S(1)}, u32[]{:S(2)}, u32[]{:S(2)}) collective-permute-start(bf16[4,56,448]{2,1,0:T(8,128)(2,1)S(1)} %constant_dynamic-slice_fusion.14), channel_id=1, source_target_pairs={{0,6},{2,4},{4,2},{6,0},{1,7},{3,5},{5,3},{7,1},{8,14},{10,12},{12... | collective-permute-start | bytes 602120 | tf_op jit(solution)/shard_map/ppermute | solution.py:80
  50.3 9.1 %copy-start.35 = (bf16[1,256,896]{2,1,0:T(8,128)(2,1)S(1)}, bf16[1,256,896]{2,1,0:T(8,128)(2,1)}, u32[]{:S(2)}) copy-start(bf16[1,256,896]{2,1,0:T(8,128)(2,1)} %param.31) | copy-start | bytes 1376260
  51.9 13.4 %copy-start.6 = (bf16[256,448]{1,0:T(8,128)(2,1)}, bf16[256,448]{1,0:T(8,128)(2,1)S(1)}, u32[]{:S(2)}) copy-start(bf16[256,448]{1,0:T(8,128)(2,1)S(1)} %get-tuple-element.81.q_ref) | copy-start | bytes 688132
  51.9 13.4 %copy-start.14 = (bf16[272,128]{1,0:T(8,128)(2,1)}, bf16[272,128]{1,0:T(8,128)(2,1)S(1)}, u32[]{:S(2)}) copy-start(bf16[272,128]{1,0:T(8,128)(2,1)S(1)} %get-tuple-element.82.refs_0_) | copy-start | bytes 208900
  51.9 6.0 %collective-permute-start.8 = (bf16[272,128]{1,0:T(8,128)(2,1)S(1)}, bf16[272,128]{1,0:T(8,128)(2,1)S(1)}, u32[]{:S(2)}, u32[]{:S(2)}) collective-permute-start(bf16[272,128]{1,0:T(8,128)(2,1)S(1)} %get-tuple-element.82.refs_0_), channel_id=1, source_target_pairs={{0,6},{2,4},{4,2},{6,0},{1,7},{3,5},{5,3},{7,1},{8,14},{10,12},{12... | collective-permute-start | bytes 208904 | tf_op jit(solution)/shard_map/ppermute | solution.py:80
  53.2 5.6 %collective-permute-start.7 = (bf16[272,128]{1,0:T(8,128)(2,1)S(1)}, bf16[272,128]{1,0:T(8,128)(2,1)S(1)}, u32[]{:S(2)}, u32[]{:S(2)}) collective-permute-start(bf16[272,128]{1,0:T(8,128)(2,1)S(1)} %get-tuple-element.82.refs_0_), channel_id=1, source_target_pairs={{0,4},{2,6},{4,0},{6,2},{1,5},{3,7},{5,1},{7,3},{8,12},{10,14},{12... | collective-permute-start | bytes 208904 | tf_op jit(solution)/shard_map/ppermute | solution.py:80
  54.4 5.1 %collective-permute-start.6 = (bf16[272,128]{1,0:T(8,128)(2,1)S(1)}, bf16[272,128]{1,0:T(8,128)(2,1)S(1)}, u32[]{:S(2)}, u32[]{:S(2)}) collective-permute-start(bf16[272,128]{1,0:T(8,128)(2,1)S(1)} %get-tuple-element.82.refs_0_), channel_id=1, source_target_pairs={{0,2},{2,0},{4,6},{6,4},{1,3},{3,1},{5,7},{7,5},{8,10},{10,8},{12,... | collective-permute-start | bytes 208904 | tf_op jit(solution)/shard_map/ppermute | solution.py:80
  59.5 10.8 %collective-permute-start.11 = (bf16[128,896]{1,0:T(8,128)(2,1)S(1)}, bf16[128,896]{1,0:T(8,128)(2,1)S(1)}, u32[]{:S(2)}, u32[]{:S(2)}) collective-permute-start(bf16[128,896]{1,0:T(8,128)(2,1)S(1)} %constant_dynamic-slice_fusion.9), channel_id=1, source_target_pairs={{0,6},{2,4},{4,2},{6,0},{1,7},{3,5},{5,3},{7,1},{8,14},{10,12},{12... | collective-permute-start | bytes 688136 | tf_op jit(solution)/shard_map/ppermute | solution.py:80
  62.3 7.9 %collective-permute-start.10 = (bf16[128,896]{1,0:T(8,128)(2,1)S(1)}, bf16[128,896]{1,0:T(8,128)(2,1)S(1)}, u32[]{:S(2)}, u32[]{:S(2)}) collective-permute-start(bf16[128,896]{1,0:T(8,128)(2,1)S(1)} %constant_dynamic-slice_fusion.9), channel_id=1, source_target_pairs={{0,4},{2,6},{4,0},{6,2},{1,5},{3,7},{5,1},{7,3},{8,12},{10,14},{12... | collective-permute-start | bytes 688136 | tf_op jit(solution)/shard_map/ppermute | solution.py:80
  65.0 6.0 %collective-permute-start.9 = (bf16[128,896]{1,0:T(8,128)(2,1)S(1)}, bf16[128,896]{1,0:T(8,128)(2,1)S(1)}, u32[]{:S(2)}, u32[]{:S(2)}) collective-permute-start(bf16[128,896]{1,0:T(8,128)(2,1)S(1)} %constant_dynamic-slice_fusion.9), channel_id=1, source_target_pairs={{0,2},{2,0},{4,6},{6,4},{1,3},{3,1},{5,7},{7,5},{8,10},{10,8},{12,... | collective-permute-start | bytes 688136 | tf_op jit(solution)/shard_map/ppermute | solution.py:80
  71.6 1.9 collective-permute-start.15
  74.2 14.3 %copy-start.27 = (f32[256,896]{1,0:T(8,128)}, f32[256,896]{1,0:T(8,128)S(1)}, u32[]{:S(2)}) copy-start(f32[256,896]{1,0:T(8,128)S(1)} %broadcast_multiply_fusion) | copy-start | bytes 2752516
  75.0 9.4 %collective-permute-start.18 = (bf16[128,896]{1,0:T(8,128)(2,1)S(1)}, bf16[128,896]{1,0:T(8,128)(2,1)S(1)}, u32[]{:S(2)}, u32[]{:S(2)}) collective-permute-start(bf16[128,896]{1,0:T(8,128)(2,1)S(1)} %get-tuple-element.151), channel_id=1, source_target_pairs={{0,6},{2,4},{4,2},{6,0},{1,7},{3,5},{5,3},{7,1},{8,14},{10,12},{12... | collective-permute-start | bytes 688136 | tf_op jit(solution)/shard_map/ppermute | solution.py:80
  76.9 11.5 %collective-permute-start.17 = (bf16[128,896]{1,0:T(8,128)(2,1)S(1)}, bf16[128,896]{1,0:T(8,128)(2,1)S(1)}, u32[]{:S(2)}, u32[]{:S(2)}) collective-permute-start(bf16[128,896]{1,0:T(8,128)(2,1)S(1)} %get-tuple-element.151), channel_id=1, source_target_pairs={{0,4},{2,6},{4,0},{6,2},{1,5},{3,7},{5,1},{7,3},{8,12},{10,14},{12... | collective-permute-start | bytes 688136 | tf_op jit(solution)/shard_map/ppermute | solution.py:80
  77.8 10.7 %collective-permute-start.16 = (bf16[128,896]{1,0:T(8,128)(2,1)S(1)}, bf16[128,896]{1,0:T(8,128)(2,1)S(1)}, u32[]{:S(2)}, u32[]{:S(2)}) collective-permute-start(bf16[128,896]{1,0:T(8,128)(2,1)S(1)} %get-tuple-element.151), channel_id=1, source_target_pairs={{0,2},{2,0},{4,6},{6,4},{1,3},{3,1},{5,7},{7,5},{8,10},{10,8},{12,... | collective-permute-start | bytes 688136 | tf_op jit(solution)/shard_map/ppermute | solution.py:80
  78.5 11.2 %collective-permute-start.20 = (bf16[512,896]{1,0:T(8,128)(2,1)S(1)}, bf16[512,896]{1,0:T(8,128)(2,1)S(1)}, u32[]{:S(2)}, u32[]{:S(2)}) collective-permute-start(bf16[512,896]{1,0:T(8,128)(2,1)S(1)} %pad_maximum_fusion.2.top_one_ref), channel_id=1, source_target_pairs={{0,1},{1,0},{2,3},{3,2},{4,5},{5,4},{6,7},{7,6},{8,9},{9,8},{10,11... | collective-permute-start | bytes 2752520 | tf_op jit(solution)/shard_map/ppermute | solution.py:62
  88.6 2.5 %collective-permute-start.19 = (bf16[512,896]{1,0:T(8,128)(2,1)S(1)}, bf16[512,896]{1,0:T(8,128)(2,1)S(1)}, u32[]{:S(2)}, u32[]{:S(2)}) collective-permute-start(bf16[512,896]{1,0:T(8,128)(2,1)S(1)} %pad_maximum_fusion.4.first_ref), channel_id=1, source_target_pairs={{0,1},{1,0},{2,3},{3,2},{4,5},{5,4},{6,7},{7,6},{8,9},{9,8},{10,11... | collective-permute-start | bytes 2752520 | tf_op jit(solution)/shard_map/ppermute | solution.py:62
  105.6 7.9 %copy-start.38 = (bf16[128,896]{1,0:T(8,128)(2,1)S(1)}, bf16[128,896]{1,0:T(8,128)(2,1)}, u32[]{:S(2)}) copy-start(bf16[128,896]{1,0:T(8,128)(2,1)} %copy-done.37) | copy-start | bytes 688132
  113.4 2.5 %collective-permute-start.25 = (bf16[512,896]{1,0:T(8,128)(2,1)S(1)}, bf16[512,896]{1,0:T(8,128)(2,1)S(1)}, u32[]{:S(2)}, u32[]{:S(2)}) collective-permute-start(bf16[512,896]{1,0:T(8,128)(2,1)S(1)} %get-tuple-element.96), channel_id=1, source_target_pairs={{0,1},{1,0},{2,3},{3,2},{4,5},{5,4},{6,7},{7,6},{8,9},{9,8},{10,11... | collective-permute-start | bytes 2752520 | tf_op jit(solution)/shard_map/ppermute | solution.py:62
  126.4 3.8 %collective-permute-start.24 = (bf16[512,896]{1,0:T(8,128)(2,1)}, bf16[512,896]{1,0:T(8,128)(2,1)}, u32[]{:S(2)}, u32[]{:S(2)}) collective-permute-start(bf16[512,896]{1,0:T(8,128)(2,1)} %split.41), channel_id=1, source_target_pairs={{0,1},{1,0},{2,3},{3,2},{4,5},{5,4},{6,7},{7,6},{8,9},{9,8},{10,11... | collective-permute-start | bytes 2752520 | tf_op jit(solution)/shard_map/ppermute | solution.py:62
  126.7 9.4 %collective-permute-start.28 = (bf16[128,896]{1,0:T(8,128)(2,1)S(1)}, bf16[128,896]{1,0:T(8,128)(2,1)S(1)}, u32[]{:S(2)}, u32[]{:S(2)}) collective-permute-start(bf16[128,896]{1,0:T(8,128)(2,1)S(1)} %get-tuple-element.162), channel_id=1, source_target_pairs={{0,6},{2,4},{4,2},{6,0},{1,7},{3,5},{5,3},{7,1},{8,14},{10,12},{12... | collective-permute-start | bytes 688136 | tf_op jit(solution)/shard_map/ppermute | solution.py:88
  129.1 11.3 %collective-permute-start.27 = (bf16[128,896]{1,0:T(8,128)(2,1)S(1)}, bf16[128,896]{1,0:T(8,128)(2,1)S(1)}, u32[]{:S(2)}, u32[]{:S(2)}) collective-permute-start(bf16[128,896]{1,0:T(8,128)(2,1)S(1)} %get-tuple-element.163), channel_id=1, source_target_pairs={{0,4},{2,6},{4,0},{6,2},{1,5},{3,7},{5,1},{7,3},{8,12},{10,14},{12... | collective-permute-start | bytes 688136 | tf_op jit(solution)/shard_map/ppermute | solution.py:88
  129.7 10.8 %collective-permute-start.26 = (bf16[128,896]{1,0:T(8,128)(2,1)S(1)}, bf16[128,896]{1,0:T(8,128)(2,1)S(1)}, u32[]{:S(2)}, u32[]{:S(2)}) collective-permute-start(bf16[128,896]{1,0:T(8,128)(2,1)S(1)} %get-tuple-element.164), channel_id=1, source_target_pairs={{0,2},{2,0},{4,6},{6,4},{1,3},{3,1},{5,7},{7,5},{8,10},{10,8},{12,... | collective-permute-start | bytes 688136 | tf_op jit(solution)/shard_map/ppermute | solution.py:88
  131.6 12.8 %copy-start.28 = (f32[256,896]{1,0:T(8,128)S(1)}, f32[256,896]{1,0:T(8,128)}, u32[]{:S(2)}) copy-start(f32[256,896]{1,0:T(8,128)} %copy-done.27) | copy-start | bytes 2752516
  140.6 3.8 %collective-permute-start.29 = (bf16[128,896]{1,0:T(8,128)(2,1)S(1)}, bf16[128,896]{1,0:T(8,128)(2,1)S(1)}, u32[]{:S(2)}, u32[]{:S(2)}) collective-permute-start(bf16[128,896]{1,0:T(8,128)(2,1)S(1)} %add_convert_fusion.4), channel_id=1, source_target_pairs={{0,1},{1,0},{2,3},{3,2},{4,5},{5,4},{6,7},{7,6},{8,9},{9,8},{10,11... | collective-permute-start | bytes 688136 | tf_op jit(solution)/shard_map/ppermute | solution.py:62
  140.8 9.4 %collective-permute-start.32 = (bf16[128,896]{1,0:T(8,128)(2,1)S(1)}, bf16[128,896]{1,0:T(8,128)(2,1)S(1)}, u32[]{:S(2)}, u32[]{:S(2)}) collective-permute-start(bf16[128,896]{1,0:T(8,128)(2,1)S(1)} %get-tuple-element.158), channel_id=1, source_target_pairs={{0,6},{2,4},{4,2},{6,0},{1,7},{3,5},{5,3},{7,1},{8,14},{10,12},{12... | collective-permute-start | bytes 688136 | tf_op jit(solution)/shard_map/ppermute | solution.py:88
  142.5 16.8 %collective-permute-start.31 = (bf16[128,896]{1,0:T(8,128)(2,1)S(1)}, bf16[128,896]{1,0:T(8,128)(2,1)S(1)}, u32[]{:S(2)}, u32[]{:S(2)}) collective-permute-start(bf16[128,896]{1,0:T(8,128)(2,1)S(1)} %get-tuple-element.159), channel_id=1, source_target_pairs={{0,4},{2,6},{4,0},{6,2},{1,5},{3,7},{5,1},{7,3},{8,12},{10,14},{12... | collective-permute-start | bytes 688136 | tf_op jit(solution)/shard_map/ppermute | solution.py:88
  143.8 16.9 %collective-permute-start.30 = (bf16[128,896]{1,0:T(8,128)(2,1)S(1)}, bf16[128,896]{1,0:T(8,128)(2,1)S(1)}, u32[]{:S(2)}, u32[]{:S(2)}) collective-permute-start(bf16[128,896]{1,0:T(8,128)(2,1)S(1)} %get-tuple-element.160), channel_id=1, source_target_pairs={{0,2},{2,0},{4,6},{6,4},{1,3},{3,1},{5,7},{7,5},{8,10},{10,8},{12,... | collective-permute-start | bytes 688136 | tf_op jit(solution)/shard_map/ppermute | solution.py:88
  146.2 15.0 %collective-permute-start.34 = (bf16[224,448]{1,0:T(8,128)(2,1)S(1)}, bf16[224,448]{1,0:T(8,128)(2,1)S(1)}, u32[]{:S(2)}, u32[]{:S(2)}) collective-permute-start(bf16[224,448]{1,0:T(8,128)(2,1)S(1)} %get-tuple-element.109), channel_id=1, source_target_pairs={{0,2},{2,0},{4,6},{6,4},{1,3},{3,1},{5,7},{7,5},{8,10},{10,8},{12,... | collective-permute-start | bytes 602120 | tf_op jit(solution)/shard_map/ppermute | solution.py:88
  147.7 15.1 %collective-permute-start.35 = (bf16[224,448]{1,0:T(8,128)(2,1)S(1)}, bf16[224,448]{1,0:T(8,128)(2,1)S(1)}, u32[]{:S(2)}, u32[]{:S(2)}) collective-permute-start(bf16[224,448]{1,0:T(8,128)(2,1)S(1)} %get-tuple-element.113), channel_id=1, source_target_pairs={{0,4},{2,6},{4,0},{6,2},{1,5},{3,7},{5,1},{7,3},{8,12},{10,14},{12... | collective-permute-start | bytes 602120 | tf_op jit(solution)/shard_map/ppermute | solution.py:88
  150.2 14.8 %collective-permute-start.36 = (bf16[224,448]{1,0:T(8,128)(2,1)S(1)}, bf16[224,448]{1,0:T(8,128)(2,1)S(1)}, u32[]{:S(2)}, u32[]{:S(2)}) collective-permute-start(bf16[224,448]{1,0:T(8,128)(2,1)S(1)} %get-tuple-element.114), channel_id=1, source_target_pairs={{0,6},{2,4},{4,2},{6,0},{1,7},{3,5},{5,3},{7,1},{8,14},{10,12},{12... | collective-permute-start | bytes 602120 | tf_op jit(solution)/shard_map/ppermute | solution.py:88
  159.3 7.2 %collective-permute-start.37 = (bf16[256,128]{1,0:T(8,128)(2,1)S(1)}, bf16[256,128]{1,0:T(8,128)(2,1)S(1)}, u32[]{:S(2)}, u32[]{:S(2)}) collective-permute-start(bf16[256,128]{1,0:T(8,128)(2,1)S(1)} %get-tuple-element.116), channel_id=1, source_target_pairs={{0,2},{2,0},{4,6},{6,4},{1,3},{3,1},{5,7},{7,5},{8,10},{10,8},{12,... | collective-permute-start | bytes 196616 | tf_op jit(solution)/shard_map/ppermute | solution.py:88
  160.7 5.8 %collective-permute-start.38 = (bf16[256,128]{1,0:T(8,128)(2,1)S(1)}, bf16[256,128]{1,0:T(8,128)(2,1)S(1)}, u32[]{:S(2)}, u32[]{:S(2)}) collective-permute-start(bf16[256,128]{1,0:T(8,128)(2,1)S(1)} %get-tuple-element.117), channel_id=1, source_target_pairs={{0,4},{2,6},{4,0},{6,2},{1,5},{3,7},{5,1},{7,3},{8,12},{10,14},{12... | collective-permute-start | bytes 196616 | tf_op jit(solution)/shard_map/ppermute | solution.py:88
  161.2 6.1 %collective-permute-start.39 = (bf16[256,128]{1,0:T(8,128)(2,1)S(1)}, bf16[256,128]{1,0:T(8,128)(2,1)S(1)}, u32[]{:S(2)}, u32[]{:S(2)}) collective-permute-start(bf16[256,128]{1,0:T(8,128)(2,1)S(1)} %get-tuple-element.118), channel_id=1, source_target_pairs={{0,6},{2,4},{4,2},{6,0},{1,7},{3,5},{5,3},{7,1},{8,14},{10,12},{12... | collective-permute-start | bytes 196616 | tf_op jit(solution)/shard_map/ppermute | solution.py:88
  168.2 1.9 collective-permute-start.40
  172.0 10.1 %collective-permute-start.41 = (bf16[240,576]{1,0:T(8,128)(2,1)S(1)}, bf16[240,576]{1,0:T(8,128)(2,1)S(1)}, u32[]{:S(2)}, u32[]{:S(2)}) collective-permute-start(bf16[240,576]{1,0:T(8,128)(2,1)S(1)} %get-tuple-element.123), channel_id=1, source_target_pairs={{0,2},{2,0},{4,6},{6,4},{1,3},{3,1},{5,7},{7,5},{8,10},{10,8},{12,... | collective-permute-start | bytes 829448 | tf_op jit(solution)/shard_map/ppermute | solution.py:88
  173.5 15.6 %collective-permute-start.42 = (bf16[240,576]{1,0:T(8,128)(2,1)S(1)}, bf16[240,576]{1,0:T(8,128)(2,1)S(1)}, u32[]{:S(2)}, u32[]{:S(2)}) collective-permute-start(bf16[240,576]{1,0:T(8,128)(2,1)S(1)} %get-tuple-element.124), channel_id=1, source_target_pairs={{0,4},{2,6},{4,0},{6,2},{1,5},{3,7},{5,1},{7,3},{8,12},{10,14},{12... | collective-permute-start | bytes 829448 | tf_op jit(solution)/shard_map/ppermute | solution.py:88
  174.2 14.8 %collective-permute-start.43 = (bf16[240,576]{1,0:T(8,128)(2,1)S(1)}, bf16[240,576]{1,0:T(8,128)(2,1)S(1)}, u32[]{:S(2)}, u32[]{:S(2)}) collective-permute-start(bf16[240,576]{1,0:T(8,128)(2,1)S(1)} %get-tuple-element.125), channel_id=1, source_target_pairs={{0,6},{2,4},{4,2},{6,0},{1,7},{3,5},{5,3},{7,1},{8,14},{10,12},{12... | collective-permute-start | bytes 829448 | tf_op jit(solution)/shard_map/ppermute | solution.py:88
  175.6 21.6 %collective-permute-start.33 = (bf16[128,896]{1,0:T(8,128)(2,1)S(1)}, bf16[128,896]{1,0:T(8,128)(2,1)}, u32[]{:S(2)}, u32[]{:S(2)}) collective-permute-start(bf16[128,896]{1,0:T(8,128)(2,1)S(1)} %add_convert_fusion.3), channel_id=1, source_target_pairs={{0,1},{1,0},{2,3},{3,2},{4,5},{5,4},{6,7},{7,6},{8,9},{9,8},{10,11... | collective-permute-start | bytes 688136 | tf_op jit(solution)/shard_map/ppermute | solution.py:62
  189.1 10.2 %copy-start.30 = (bf16[256,896]{1,0:T(8,128)(2,1)S(1)}, bf16[256,896]{1,0:T(8,128)(2,1)}, u32[]{:S(2)}) copy-start(bf16[256,896]{1,0:T(8,128)(2,1)} %copy-done.29) | copy-start | bytes 1376260
  189.1 10.2 %copy-start.32 = (bf16[256,896]{1,0:T(8,128)(2,1)S(1)}, bf16[256,896]{1,0:T(8,128)(2,1)}, u32[]{:S(2)}) copy-start(bf16[256,896]{1,0:T(8,128)(2,1)} %copy-done.31) | copy-start | bytes 1376260
  189.6 8.7 %collective-permute-start.44 = (bf16[72,1024]{1,0:T(8,128)(2,1)S(1)}, bf16[72,1024]{1,0:T(8,128)(2,1)S(1)}, u32[]{:S(2)}, u32[]{:S(2)}) collective-permute-start(bf16[72,1024]{1,0:T(8,128)(2,1)S(1)} %get-tuple-element.131), channel_id=1, source_target_pairs={{0,8},{8,16},{16,24},{24,0},{1,9},{9,17},{17,25},{25,1},{2,10},{10... | collective-permute-start | bytes 442376 | tf_op jit(solution)/shard_map/ppermute | solution.py:126
  189.7 13.0 %collective-permute-start.45 = (bf16[72,1024]{1,0:T(8,128)(2,1)S(1)}, bf16[72,1024]{1,0:T(8,128)(2,1)S(1)}, u32[]{:S(2)}, u32[]{:S(2)}) collective-permute-start(bf16[72,1024]{1,0:T(8,128)(2,1)S(1)} %get-tuple-element.132), channel_id=1, source_target_pairs={{0,16},{8,24},{16,0},{24,8},{1,17},{9,25},{17,1},{25,9},{2,18},{10... | collective-permute-start | bytes 442376 | tf_op jit(solution)/shard_map/ppermute | solution.py:126
  191.2 11.5 %collective-permute-start.46 = (bf16[72,1024]{1,0:T(8,128)(2,1)S(1)}, bf16[72,1024]{1,0:T(8,128)(2,1)S(1)}, u32[]{:S(2)}, u32[]{:S(2)}) collective-permute-start(bf16[72,1024]{1,0:T(8,128)(2,1)S(1)} %get-tuple-element.133), channel_id=1, source_target_pairs={{0,24},{8,0},{16,8},{24,16},{1,25},{9,1},{17,9},{25,17},{2,26},{10... | collective-permute-start | bytes 442376 | tf_op jit(solution)/shard_map/ppermute | solution.py:126
  195.7 9.0 %collective-permute-start.49 = (bf16[56,1920]{1,0:T(8,128)(2,1)}, bf16[56,1920]{1,0:T(8,128)(2,1)S(1)}, u32[]{:S(2)}, u32[]{:S(2)}) collective-permute-start(bf16[56,1920]{1,0:T(8,128)(2,1)} %get-tuple-element.170), channel_id=1, source_target_pairs={{0,6},{2,4},{4,2},{6,0},{1,7},{3,5},{5,3},{7,1},{8,14},{10,12},{12... | collective-permute-start | bytes 645128 | tf_op jit(solution)/shard_map/ppermute | solution.py:88
  197.2 9.8 %collective-permute-start.48 = (bf16[56,1920]{1,0:T(8,128)(2,1)}, bf16[56,1920]{1,0:T(8,128)(2,1)S(1)}, u32[]{:S(2)}, u32[]{:S(2)}) collective-permute-start(bf16[56,1920]{1,0:T(8,128)(2,1)} %get-tuple-element.171), channel_id=1, source_target_pairs={{0,4},{2,6},{4,0},{6,2},{1,5},{3,7},{5,1},{7,3},{8,12},{10,14},{12... | collective-permute-start | bytes 645128 | tf_op jit(solution)/shard_map/ppermute | solution.py:88
  198.3 8.6 %collective-permute-start.47 = (bf16[56,1920]{1,0:T(8,128)(2,1)}, bf16[56,1920]{1,0:T(8,128)(2,1)S(1)}, u32[]{:S(2)}, u32[]{:S(2)}) collective-permute-start(bf16[56,1920]{1,0:T(8,128)(2,1)} %get-tuple-element.172), channel_id=1, source_target_pairs={{0,2},{2,0},{4,6},{6,4},{1,3},{3,1},{5,7},{7,5},{8,10},{10,8},{12,... | collective-permute-start | bytes 645128 | tf_op jit(solution)/shard_map/ppermute | solution.py:88
  (37 other events, 128.9 us)
Sparse Core Ops, SparseCore 0:
  32.0 68.0 all-gather.1
  120.9 63.4 reduce-scatter.1

commit v2 on v1

--- a/solution.py
+++ b/solution.py
@@ -508,48 +508,37 @@
 
 
 def pack_kernel(count, lines, own_ref, *refs):
-    qkv_refs, o_refs = refs[:count], refs[count : 2 * count]
-    outs = refs[2 * count : 2 * count + lines]
-    qkv_sum, o_sum, block = refs[2 * count + lines :]
+    qkv_refs, outs = refs[:count], refs[count : count + lines]
+    qkv_sum, block = refs[count + lines :]
     qkv_sum[...] = sum(ref[...].astype(F32) for ref in qkv_refs)
-    o_sum[...] = sum(ref[...].astype(F32) for ref in o_refs)
-    rows = o_sum.shape[0] // lines
-    width = qkv_sum.shape[1]
-    block[rows:, :] = jnp.zeros((SMALL_ROWS, block.shape[1]), F32)
-    block[rows:, :width] = qkv_sum[lines * rows :, :]
+    rows = block.shape[0] - SMALL_ROWS
+    block[rows:, :] = qkv_sum[lines * rows :, :]
     for step in range(lines):
         begin = pl.multiple_of(lax.rem(own_ref[0] + step, lines) * rows, 8)
-        block[:rows, :width] = qkv_sum[pl.ds(begin, rows), :]
-        block[:rows, width:] = o_sum[pl.ds(begin, rows), :]
+        block[:rows, :] = qkv_sum[pl.ds(begin, rows), :]
         outs[step][...] = block[...].astype(BF)
 
 
-def pack(own_line, qkv_parts, o_parts, lines):
-    count = len(qkv_parts)
-    width, width_o = qkv_parts[0].shape[1], o_parts[0].shape[1]
-    rows = o_parts[0].shape[0] // lines
-    shape = (rows + SMALL_ROWS, width + width_o)
+def pack(own_line, qkv_parts, lines):
+    height, width = qkv_parts[0].shape
+    shape = ((height - SMALL_ROWS) // lines + SMALL_ROWS, width)
     return list(
         pl.pallas_call(
-            functools.partial(pack_kernel, count, lines),
+            functools.partial(pack_kernel, len(qkv_parts), lines),
             out_shape=(jax.ShapeDtypeStruct(shape, BF),) * lines,
-            in_specs=[IN_SMEM] + [IN_VMEM] * (2 * count),
+            in_specs=[IN_SMEM] + [IN_VMEM] * len(qkv_parts),
             out_specs=(IN_VMEM,) * lines,
-            scratch_shapes=[
-                pltpu.VMEM(qkv_parts[0].shape, F32),
-                pltpu.VMEM(o_parts[0].shape, F32),
-                pltpu.VMEM(shape, F32),
-            ],
+            scratch_shapes=[pltpu.VMEM((height, width), F32), pltpu.VMEM(shape, F32)],
             compiler_params=pltpu.CompilerParams(vmem_limit_bytes=VMEM_BYTES),
             cost_estimate=FREE,
             name="pack",
-        )(own_line, *qkv_parts, *o_parts)
+        )(own_line, *qkv_parts)
     )
 
 
 def unpack_kernel(lines, widths, *refs):
-    parts = refs[:lines]
-    q_ref, k_ref, v_ref, o_ref, bq_ref, bk_ref, bv_ref, attn_ref, mlp_ref, total = refs[lines:]
+    parts, o_parts = refs[:lines], refs[lines : 2 * lines]
+    q_ref, k_ref, v_ref, o_ref, bq_ref, bk_ref, bv_ref, attn_ref, mlp_ref, total = refs[2 * lines :]
     total[...] = sum(ref[...].astype(F32) for ref in parts)
     rows = q_ref.shape[0]
     first, second = widths[0], widths[0] + widths[1]
@@ -557,7 +546,7 @@
     q_ref[...] = total[:rows, :first]
     k_ref[...] = total[:rows, first:second]
     v_ref[...] = total[:rows, second:third]
-    o_ref[...] = total[:rows, third:]
+    o_ref[...] = sum(ref[...].astype(F32) for ref in o_parts)
     bq_ref[...] = total[rows : rows + 1, :first]
     bk_ref[...] = total[rows : rows + 1, first:second]
     bv_ref[...] = total[rows : rows + 1, second:third]
@@ -566,10 +555,10 @@
         ref[:, SPLIT:] = total[row + 1 : row + 2, : ref.shape[1] - SPLIT]
 
 
-def unpack(parts, features, width_q, width_k):
+def unpack(parts, o_parts, features, width_q, width_k):
     rows, width = parts[0].shape
     rows -= SMALL_ROWS
-    width_o = width - width_q - 2 * width_k
+    width_o = o_parts[0].shape[1]
     shapes = [
         (rows, width_q), (rows, width_k), (rows, width_k), (rows, width_o),
         (1, width_q), (1, width_k), (1, width_k), (1, features), (1, features),
@@ -577,13 +566,13 @@
     return pl.pallas_call(
         functools.partial(unpack_kernel, len(parts), (width_q, width_k)),
         out_shape=tuple(jax.ShapeDtypeStruct(shape, F32) for shape in shapes),
-        in_specs=[IN_VMEM] * len(parts),
+        in_specs=[IN_VMEM] * (2 * len(parts)),
         out_specs=(IN_VMEM,) * len(shapes),
         scratch_shapes=[pltpu.VMEM(parts[0].shape, F32)],
         compiler_params=pltpu.CompilerParams(vmem_limit_bytes=VMEM_BYTES),
         cost_estimate=FREE,
         name="unpack",
-    )(*parts)
+    )(*parts, *o_parts)
 
 
 def mlp_out_kernel(count, chunk, own_ref, *refs):
@@ -1009,29 +998,38 @@
         small = small.astype(jnp.bfloat16)
         qkv_pieces = [jnp.concatenate([part, small]) for part in owners(normed, grad_qkv)]
     qkv_parts = trade(qkv_pieces)
+    o_sum = sum(part.astype(F32) for part in o_parts).astype(jnp.bfloat16)
+    o_sum = o_sum.reshape(fsdp_size, rows, o_sum.shape[-1])
+    o_lines = [
+        lax.dynamic_index_in_dim(o_sum, (fsdp_own[0] + step) % fsdp_size, 0, keepdims=False)
+        for step in range(fsdp_size)
+    ]
+    o_lines = o_lines[:1] + [send_up(o_lines[step], step) for step in range(1, fsdp_size)]
+    mlp_mine = mlp_mine.reshape(ctx_size, rows, 3 * chunk)
+    mlp_chosen = choose(mlp_mine)
+    qkv_parts[0], o_lines, mlp_chosen = lax.optimization_barrier(
+        (qkv_parts[0], o_lines, mlp_chosen)
+    )
     if few():
-        packed = pack(fsdp_own, qkv_parts, o_parts, fsdp_size)
+        packed = pack(fsdp_own, qkv_parts, fsdp_size)
     else:
         qkv_sum = sum(part.astype(F32) for part in qkv_parts)
-        o_sum = sum(part.astype(F32) for part in o_parts)
-        small = jnp.pad(qkv_sum[fsdp_size * rows :], ((0, 0), (0, w_o.shape[0])))
-        both = jnp.concatenate([qkv_sum[: fsdp_size * rows], o_sum], axis=-1)
-        both = both.reshape(fsdp_size, rows, both.shape[-1])
+        small = qkv_sum[fsdp_size * rows :]
+        both = qkv_sum[: fsdp_size * rows].reshape(fsdp_size, rows, width_qkv)
         packed = [
             jnp.concatenate([both[(fsdp_own[0] + step) % fsdp_size], small]).astype(jnp.bfloat16)
             for step in range(fsdp_size)
         ]
-    mlp_mine = mlp_mine.reshape(ctx_size, rows, 3 * chunk)
     packed = packed[:1] + [send_up(packed[step], step) for step in range(1, fsdp_size)]
-    mlp_pieces = trade(choose(mlp_mine))
+    mlp_pieces = trade(mlp_chosen)
     if few():
-        w_grads = unpack(packed, features, width_q, width_k)
+        w_grads = unpack(packed, o_lines, features, width_q, width_k)
         mlp_grads = mlp_out(own, mlp_pieces, hidden_count)
     else:
         total = sum(part.astype(F32) for part in packed)
         tops = [0, width_q, width_q + width_k, width_qkv]
         w_grads = [total[:rows, tops[k] : tops[k + 1]] for k in range(3)]
-        w_grads.append(total[:rows, width_qkv:])
+        w_grads.append(sum(part.astype(F32) for part in o_lines))
         w_grads += [total[rows, tops[k] : tops[k + 1]] for k in range(3)]
         for row in (rows + 1, rows + 3):
             w_grads.append(

time: 216 us -> 214 us (level)
  waiting for transfers between devices: 75.1 us -> 67.8 us
  starting transfers between devices: 57.1 us -> 60.2 us
    ppermute x21, waiting for transfers between devices: 36.9 us -> 23.4 us  [trade(): lax.ppermute(parts[step], 'ctx', flips(size, step))]
    reduce_scatter x1, waiting for transfers between devices: 0.01 us -> 4.54 us  [body(): lax.psum_scatter(mlp_grad, 'fsdp', scatter_dimension=0, tiled=False)]
    ppermute x3 -> x6, waiting for transfers between devices: 1.92 us -> 5.55 us  [send_up(): lax.ppermute(values, 'fsdp', [(index, (index + step) % size) for index in...]
    ppermute x3 -> x6, starting transfers between devices: 4 us -> 6.59 us  [send_up(): lax.ppermute(values, 'fsdp', [(index, (index + step) % size) for index in...]
    unnamed x106 -> x128, local copies, waits for them, and re-layouts: 14.8 us -> 15.1 us
  transfers between devices with their start and end apart: 52 -> 55, of which waited for: 29 -> 26; matrix products, arithmetic and copies ran while one was open for 9% -> 10% of each run, Pallas kernels for 8% -> 8%
where the time goes in v2:
time: 214 us
  waiting for transfers between devices  67.8 us (32%)
  starting transfers between devices  60.2 us (28%)
  Pallas kernels  26.1 us (12%)
  local copies, waits for them, and re-layouts  20.7 us (10%)
  other arithmetic  15.4 us (7%)
  between operations  15 us (7%)
  matrix products  8.14 us (4%)
    ppermute x21, starting transfers between devices, trade(): lax.ppermute(parts[step], 'ctx', flips(size, step))  25.1 us
    ppermute x15, waiting for transfers between devices, spread(): lax.ppermute(values, 'ctx', flips(size, step))  23.5 us
    ppermute x21, waiting for transfers between devices, trade(): lax.ppermute(parts[step], 'ctx', flips(size, step))  23.4 us
    ppermute x15, starting transfers between devices, spread(): lax.ppermute(values, 'ctx', flips(size, step))  20.7 us
    unnamed x128, local copies, waits for them, and re-layouts  15.1 us
    all_gather x1, waiting for transfers between devices, body(): mlp_rows = lax.all_gather(recut, 'fsdp', axis=0, tiled=True)  8.03 us
    pallas_call x1, Pallas kernels, mlp(): pl.pallas_call(functools.partial(mlp_kernel, chunk), out_shape=(jax.Shape...  7.95 us
    pallas_call x1, Pallas kernels, attend_bwd(): pl.pallas_call(functools.partial(bwd_kernel, n), out_shape=(jax.ShapeDtyp...  7.39 us
  transfers between devices with their start and end apart: 55, of which 26 were waited for; matrix products, arithmetic and copies ran while one was open for 10% of the time, Pallas kernels for 8%

profile of v2, /device:TPU:0, one launch (start us, length us, event | category | flops | bytes accessed | tf_op | source)
XLA Modules:
  0.0 213.5 jit_solution(18370924564423304529)
XLA Ops:
  8.2 3.1 %collective-permute-start.2 = (bf16[56,1024]{1,0:T(8,128)(2,1)S(1)}, bf16[56,1024]{1,0:T(8,128)(2,1)S(1)}, u32[]{:S(2)}, u32[]{:S(2)}) collective-permute-start(bf16[56,1024]{1,0:T(8,128)(2,1)S(1)} %pad_maximum_fusion.7), channel_id=1, source_target_pairs={{0,8},{8,16},{16,24},{24,0},{1,9},{9,17},{17,25},{25,1},{2,10},{10... | collective-permute-start | bytes 344072 | tf_op jit(solution)/shard_map/ppermute | solution.py:116
  11.3 2.6 %collective-permute-start.1 = (bf16[56,1024]{1,0:T(8,128)(2,1)S(1)}, bf16[56,1024]{1,0:T(8,128)(2,1)S(1)}, u32[]{:S(2)}, u32[]{:S(2)}) collective-permute-start(bf16[56,1024]{1,0:T(8,128)(2,1)S(1)} %pad_maximum_fusion.7), channel_id=1, source_target_pairs={{0,16},{8,24},{16,0},{24,8},{1,17},{9,25},{17,1},{25,9},{2,18},{10... | collective-permute-start | bytes 344072 | tf_op jit(solution)/shard_map/ppermute | solution.py:116
  13.9 1.3 collective-permute-start
  18.3 1.6 collective-permute-start.21
  19.8 1.5 collective-permute-start.22
  24.5 4.9 %collective-permute-done.22 = bf16[56,1920]{1,0:T(8,128)(2,1)S(1)} collective-permute-done((bf16[56,1920]{1,0:T(8,128)(2,1)S(1)}, bf16[56,1920]{1,0:T(8,128)(2,1)S(1)}, u32[]{:S(2)}, u32[]{:S(2)}) %collective-permute-start.22) | collective-permute-done | bytes 215072 | tf_op jit(solution)/shard_map/ppermute | solution.py:88
  29.4 1.2 collective-permute-done.23
  32.0 1.4 collective-permute-start.4
  33.9 1.7 collective-permute-start.5
  35.8 1.4 collective-permute-start.13
  37.8 6.1 %collective-permute-done.4 = bf16[4,56,576]{2,1,0:T(8,128)(2,1)S(1)} collective-permute-done((bf16[4,56,576]{2,1,0:T(8,128)(2,1)S(1)}, bf16[4,56,576]{2,1,0:T(8,128)(2,1)S(1)}, u32[]{:S(2)}, u32[]{:S(2)}) %collective-permute-start.4) | collective-permute-done | bytes 258080 | tf_op jit(solution)/shard_map/ppermute | solution.py:80
  44.0 2.7 %collective-permute-start.14 = (bf16[4,56,448]{2,1,0:T(8,128)(2,1)S(1)}, bf16[4,56,448]{2,1,0:T(8,128)(2,1)S(1)}, u32[]{:S(2)}, u32[]{:S(2)}) collective-permute-start(bf16[4,56,448]{2,1,0:T(8,128)(2,1)S(1)} %constant_dynamic-slice_fusion.14), channel_id=1, source_target_pairs={{0,6},{2,4},{4,2},{6,0},{1,7},{3,5},{5,3},{7,1},{8,14},{10,12},{12... | collective-permute-start | bytes 602120 | tf_op jit(solution)/shard_map/ppermute | solution.py:80
  46.7 2.9 %collective-permute-done.5 = bf16[4,56,576]{2,1,0:T(8,128)(2,1)S(1)} collective-permute-done((bf16[4,56,576]{2,1,0:T(8,128)(2,1)S(1)}, bf16[4,56,576]{2,1,0:T(8,128)(2,1)S(1)}, u32[]{:S(2)}, u32[]{:S(2)}) %collective-permute-start.5) | collective-permute-done | bytes 258080 | tf_op jit(solution)/shard_map/ppermute | solution.py:80
  51.9 1.3 collective-permute-start.8
  53.2 1.2 collective-permute-start.7
  54.4 1.1 collective-permute-start.6
  55.4 1.6 collective-permute-done.14
  59.4 2.9 %collective-permute-start.11 = (bf16[128,896]{1,0:T(8,128)(2,1)S(1)}, bf16[128,896]{1,0:T(8,128)(2,1)S(1)}, u32[]{:S(2)}, u32[]{:S(2)}) collective-permute-start(bf16[128,896]{1,0:T(8,128)(2,1)S(1)} %constant_dynamic-slice_fusion.9), channel_id=1, source_target_pairs={{0,6},{2,4},{4,2},{6,0},{1,7},{3,5},{5,3},{7,1},{8,14},{10,12},{12... | collective-permute-start | bytes 688136 | tf_op jit(solution)/shard_map/ppermute | solution.py:80
  62.3 2.6 %collective-permute-start.10 = (bf16[128,896]{1,0:T(8,128)(2,1)S(1)}, bf16[128,896]{1,0:T(8,128)(2,1)S(1)}, u32[]{:S(2)}, u32[]{:S(2)}) collective-permute-start(bf16[128,896]{1,0:T(8,128)(2,1)S(1)} %constant_dynamic-slice_fusion.9), channel_id=1, source_target_pairs={{0,4},{2,6},{4,0},{6,2},{1,5},{3,7},{5,1},{7,3},{8,12},{10,14},{12... | collective-permute-start | bytes 688136 | tf_op jit(solution)/shard_map/ppermute | solution.py:80
  65.3 4.2 %attend_forward.1 = (bf16[256,448]{1,0:T(8,128)(2,1)S(1)}, f32[448,256]{1,0:T(8,128)S(1)}, f32[7,256]{1,0:T(8,128)S(1)}, s32[1,256]{1,0:T(1,128)S(1)}) custom-call(s32[1]{0:T(128)} %bitcast.1.own_ref, bf16[256,448]{1,0:T(8,128)(2,1)S(1)} %get-tuple-element.90.q_ref, s32[1,256]{1,0:T(1,128)S(1)} %copy-done.26, ...), custom_call_target="tpu_custom_call" | custom-call | tf_op jit(solution)/shard_map/attend_forward/pallas_call | solution.py:308
  71.6 1.8 collective-permute-done.15
  75.0 1.9 collective-permute-start.18
  78.5 5.9 %collective-permute-done.18 = bf16[128,896]{1,0:T(8,128)(2,1)S(1)} collective-permute-done((bf16[128,896]{1,0:T(8,128)(2,1)S(1)}, bf16[128,896]{1,0:T(8,128)(2,1)S(1)}, u32[]{:S(2)}, u32[]{:S(2)}) %collective-permute-start.18) | collective-permute-done | bytes 229408 | tf_op jit(solution)/shard_map/ppermute | solution.py:80
  84.4 4.1 %collective-permute-done.17 = bf16[128,896]{1,0:T(8,128)(2,1)S(1)} collective-permute-done((bf16[128,896]{1,0:T(8,128)(2,1)S(1)}, bf16[128,896]{1,0:T(8,128)(2,1)S(1)}, u32[]{:S(2)}, u32[]{:S(2)}) %collective-permute-start.17) | collective-permute-done | bytes 229408 | tf_op jit(solution)/shard_map/ppermute | solution.py:80
  92.1 8.0 %all-gather.2.cloned.1.call-done.weights = bf16[896,1920]{1,0:T(8,128)(2,1)} async-done(((bf16[224,1920]{1,0:T(8,128)(2,1)}), bf16[896,1920]{1,0:T(8,128)(2,1)}) %all-gather.2.cloned.1.call-update) | async-done | bytes 3440656 | tf_op jit(solution)/shard_map/all_gather | solution.py:787
  100.1 1.2 copy-done.2
  101.3 1.2 copy-done.4
  102.4 2.0 copy-done.5
  104.4 1.2 copy-done.11
  105.6 8.0 %mlp.1 = (bf16[512,896]{1,0:T(8,128)(2,1)S(1)}, bf16[512,896]{1,0:T(8,128)(2,1)S(1)}, bf16[1024,640]{1,0:T(8,128)(2,1)S(1)}, bf16[1024,1280]{1,0:T(8,128)(2,1)S(1)}) custom-call(bf16[512,896]{1,0:T(8,128)(2,1)S(1)} %copy-done.4, bf16[512,896]{1,0:T(8,128)(2,1)S(1)} %copy-done.2, bf16[512,896]{1,0:T(8,128)(2,1)S(1)} %pad_maximum_fusion.2.top_one_ref, ...), custom_call_target="tpu_custom_call" | custom-call | tf_op jit(solution)/shard_map/mlp/pallas_call | solution.py:418
  113.9 1.7 fusion.4
  116.3 2.6 %convolution_convert_fusion = bf16[896,1280]{1,0:T(8,128)(2,1)S(1)} fusion(bf16[1024,896]{1,0:T(8,128)(2,1)S(1)} %constant_dynamic-update-slice_fusion, bf16[1024,1280]{1,0:T(8,128)(2,1)S(1)} %get-tuple-element.137), kind=kOutput, calls=%fused_computation | convolution fusion | flops 2349957120 | bytes 6750208 | tf_op jit(solution)/shard_map/dot_general | solution.py:40
  119.0 2.0 pad_maximum_fusion
  121.0 3.4 %convolution_convert_fusion.1 = bf16[1024,896]{1,0:T(8,128)(2,1)S(1)} fusion(bf16[1024,640]{1,0:T(8,128)(2,1)} %copy-done.27, bf16[896,1920]{1,0:T(8,128)(2,1)} %all-gather.2.cloned.1.call-done.weights), kind=kOutput, calls=%fused_computation.8 | convolution fusion | flops 1175322624 | bytes 4292608 | tf_op jit(solution)/shard_map/dot_general | solution.py:36
  124.4 1.3 copy-done.34
  127.0 2.5 %collective-permute-start.28 = (bf16[128,896]{1,0:T(8,128)(2,1)S(1)}, bf16[128,896]{1,0:T(8,128)(2,1)S(1)}, u32[]{:S(2)}, u32[]{:S(2)}) collective-permute-start(bf16[128,896]{1,0:T(8,128)(2,1)S(1)} %get-tuple-element.180), channel_id=1, source_target_pairs={{0,6},{2,4},{4,2},{6,0},{1,7},{3,5},{5,3},{7,1},{8,14},{10,12},{12... | collective-permute-start | bytes 688136 | tf_op jit(solution)/shard_map/ppermute | solution.py:88
  130.5 1.4 add_convert_fusion.1
  131.9 4.5 %collective-permute-done.28 = bf16[128,896]{1,0:T(8,128)(2,1)S(1)} collective-permute-done((bf16[128,896]{1,0:T(8,128)(2,1)S(1)}, bf16[128,896]{1,0:T(8,128)(2,1)S(1)}, u32[]{:S(2)}, u32[]{:S(2)}) %collective-permute-start.28) | collective-permute-done | bytes 229408 | tf_op jit(solution)/shard_map/ppermute | solution.py:88
  136.4 4.3 %collective-permute-done.27 = bf16[128,896]{1,0:T(8,128)(2,1)S(1)} collective-permute-done((bf16[128,896]{1,0:T(8,128)(2,1)S(1)}, bf16[128,896]{1,0:T(8,128)(2,1)S(1)}, u32[]{:S(2)}, u32[]{:S(2)}) %collective-permute-start.27) | collective-permute-done | bytes 229408 | tf_op jit(solution)/shard_map/ppermute | solution.py:88
  141.8 1.6 collective-permute-start.32
  143.4 1.3 collective-permute-start.31
  147.1 1.5 collective-permute-start.34
  149.4 1.8 collective-permute-done.32
  151.2 1.6 collective-permute-start.36
  152.8 7.4 %attend_backward.1 = (bf16[256,448]{1,0:T(8,128)(2,1)S(1)}, bf16[256,128]{1,0:T(8,128)(2,1)S(1)}, bf16[256,128]{1,0:T(8,128)(2,1)S(1)}, bf16[256,128]{1,0:T(8,128)(2,1)S(1)}, bf16[256,128]{1,0:T(8,128)(2,1)S(1)}) custom-call(s32[1]{0:T(128)} %bitcast.1.own_ref, bf16[256,448]{1,0:T(8,128)(2,1)S(1)} %copy-done.7, s32[1,256]{1,0:T(1,128)S(1)} %get-tuple-element.95.start_ref, ...), custom_call_target="tpu_custom_call" | custom-call | tf_op jit(solution)/shard_map/attend_backward/pallas_call | solution.py:354
  160.2 1.4 collective-permute-start.37
  162.2 1.6 collective-permute-start.39
  163.8 2.2 %collective-permute-done.36 = bf16[224,448]{1,0:T(8,128)(2,1)S(1)} collective-permute-done((bf16[224,448]{1,0:T(8,128)(2,1)S(1)}, bf16[224,448]{1,0:T(8,128)(2,1)S(1)}, u32[]{:S(2)}, u32[]{:S(2)}) %collective-permute-start.36) | collective-permute-done | bytes 200736 | tf_op jit(solution)/shard_map/ppermute | solution.py:88
  166.0 1.4 collective-permute-done.37.refs_1_
  169.4 1.4 add_convert_fusion.3
  172.0 1.9 last_grads.1
  174.0 1.5 collective-permute-start.44
  176.2 1.2 collective-permute-start.46
  177.7 4.8 %collective-permute-done.42.refs_6_ = bf16[56,448]{1,0:T(8,128)(2,1)S(1)} collective-permute-done((bf16[56,448]{1,0:T(8,128)(2,1)S(1)}, bf16[56,448]{1,0:T(8,128)(2,1)S(1)}, u32[]{:S(2)}, u32[]{:S(2)}) %collective-permute-start.42) | collective-permute-done | bytes 50208 | tf_op jit(solution)/shard_map/ppermute | solution.py:126
  182.5 4.5 %reduce-scatter.2.cloned.1.call-done = bf16[1,224,1920]{2,1,0:T(8,128)(2,1)} async-done(((bf16[4,224,1920]{2,1,0:T(8,128)(2,1)}), bf16[1,224,1920]{2,1,0:T(8,128)(2,1)}) %reduce-scatter.2.cloned.1.call-update) | async-done | bytes 860176 | tf_op jit(solution)/shard_map/reduce_scatter | solution.py:891
  187.0 2.1 dynamic-slice_bitcast_fusion
  189.2 2.1 collective-permute-done.45.refs_2_
  191.6 1.7 collective-permute-start.47
  193.9 1.4 collective-permute-start.51
  195.3 1.5 collective-permute-start.52
  196.8 1.9 collective-permute-start.48
  198.7 1.8 collective-permute-start.49
  200.5 2.1 fusion.14
  205.4 1.3 mlp_out.1
  (242 shorter events, 39.2 us)
Async XLA Ops:
  7.2 17.2 %copy-start.56 = (bf16[56,64]{1,0:T(8,128)(2,1)S(1)}, bf16[56,64]{1,0:T(8,128)(2,1)}, u32[]{:S(2)}) copy-start(bf16[56,64]{1,0:T(8,128)(2,1)} %param.24) | copy-start | bytes 21508
  7.2 17.2 %copy-start.57 = (bf16[56,64]{1,0:T(8,128)(2,1)S(1)}, bf16[56,64]{1,0:T(8,128)(2,1)}, u32[]{:S(2)}) copy-start(bf16[56,64]{1,0:T(8,128)(2,1)} %param.22) | copy-start | bytes 21508
  7.2 17.2 %copy-start.55 = (bf16[56,448]{1,0:T(8,128)(2,1)S(1)}, bf16[56,448]{1,0:T(8,128)(2,1)}, u32[]{:S(2)}) copy-start(bf16[56,448]{1,0:T(8,128)(2,1)} %param.20) | copy-start | bytes 150532
  7.2 17.2 %copy-start.54 = (bf16[448,56]{0,1:T(8,128)(2,1)S(1)}, bf16[448,56]{0,1:T(8,128)(2,1)}, u32[]{:S(2)}) copy-start(bf16[448,56]{0,1:T(8,128)(2,1)} %param.26) | copy-start | bytes 150532
  7.2 92.9 %all-gather.2.cloned.1.call-start = ((), (), s32[]{:S(2)}) async-start(), calls=%async_computation.1 | async-start | bytes 4300800 | tf_op jit(solution)/shard_map/all_gather | solution.py:787
  8.2 16.1 %collective-permute-start.2 = (bf16[56,1024]{1,0:T(8,128)(2,1)S(1)}, bf16[56,1024]{1,0:T(8,128)(2,1)S(1)}, u32[]{:S(2)}, u32[]{:S(2)}) collective-permute-start(bf16[56,1024]{1,0:T(8,128)(2,1)S(1)} %pad_maximum_fusion.7), channel_id=1, source_target_pairs={{0,8},{8,16},{16,24},{24,0},{1,9},{9,17},{17,25},{25,1},{2,10},{10... | collective-permute-start | bytes 344072 | tf_op jit(solution)/shard_map/ppermute | solution.py:116
  11.3 13.0 %collective-permute-start.1 = (bf16[56,1024]{1,0:T(8,128)(2,1)S(1)}, bf16[56,1024]{1,0:T(8,128)(2,1)S(1)}, u32[]{:S(2)}, u32[]{:S(2)}) collective-permute-start(bf16[56,1024]{1,0:T(8,128)(2,1)S(1)} %pad_maximum_fusion.7), channel_id=1, source_target_pairs={{0,16},{8,24},{16,0},{24,8},{1,17},{9,25},{17,1},{25,9},{2,18},{10... | collective-permute-start | bytes 344072 | tf_op jit(solution)/shard_map/ppermute | solution.py:116
  13.9 9.8 %collective-permute-start = (bf16[56,1024]{1,0:T(8,128)(2,1)S(1)}, bf16[56,1024]{1,0:T(8,128)(2,1)S(1)}, u32[]{:S(2)}, u32[]{:S(2)}) collective-permute-start(bf16[56,1024]{1,0:T(8,128)(2,1)S(1)} %pad_maximum_fusion.7), channel_id=1, source_target_pairs={{0,24},{8,0},{16,8},{24,16},{1,25},{9,1},{17,9},{25,17},{2,26},{10... | collective-permute-start | bytes 344072 | tf_op jit(solution)/shard_map/ppermute | solution.py:116
  18.3 6.3 %collective-permute-start.21 = (bf16[56,1920]{1,0:T(8,128)(2,1)S(1)}, bf16[56,1920]{1,0:T(8,128)(2,1)S(1)}, u32[]{:S(2)}, u32[]{:S(2)}) collective-permute-start(bf16[56,1920]{1,0:T(8,128)(2,1)S(1)} %get-tuple-element.100), channel_id=1, source_target_pairs={{0,2},{2,0},{4,6},{6,4},{1,3},{3,1},{5,7},{7,5},{8,10},{10,8},{12,... | collective-permute-start | bytes 645128 | tf_op jit(solution)/shard_map/ppermute | solution.py:88
  19.8 9.6 %collective-permute-start.22 = (bf16[56,1920]{1,0:T(8,128)(2,1)S(1)}, bf16[56,1920]{1,0:T(8,128)(2,1)S(1)}, u32[]{:S(2)}, u32[]{:S(2)}) collective-permute-start(bf16[56,1920]{1,0:T(8,128)(2,1)S(1)} %get-tuple-element.101), channel_id=1, source_target_pairs={{0,4},{2,6},{4,0},{6,2},{1,5},{3,7},{5,1},{7,3},{8,12},{10,14},{12... | collective-permute-start | bytes 645128 | tf_op jit(solution)/shard_map/ppermute | solution.py:88
  23.7 6.8 %collective-permute-start.23 = (bf16[56,1920]{1,0:T(8,128)(2,1)S(1)}, bf16[56,1920]{1,0:T(8,128)(2,1)S(1)}, u32[]{:S(2)}, u32[]{:S(2)}) collective-permute-start(bf16[56,1920]{1,0:T(8,128)(2,1)S(1)} %get-tuple-element.102), channel_id=1, source_target_pairs={{0,6},{2,4},{4,2},{6,0},{1,7},{3,5},{5,3},{7,1},{8,14},{10,12},{12... | collective-permute-start | bytes 645128 | tf_op jit(solution)/shard_map/ppermute | solution.py:88
  31.9 155.1 %reduce-scatter.2.cloned.1.call-start = ((), (), s32[]{:S(2)}) async-start(), calls=%async_computation.2 | async-start | bytes 4300800 | tf_op jit(solution)/shard_map/reduce_scatter | solution.py:891
  32.0 11.9 %collective-permute-start.4 = (bf16[4,56,576]{2,1,0:T(8,128)(2,1)S(1)}, bf16[4,56,576]{2,1,0:T(8,128)(2,1)S(1)}, u32[]{:S(2)}, u32[]{:S(2)}) collective-permute-start(bf16[4,56,576]{2,1,0:T(8,128)(2,1)S(1)} %constant_dynamic-slice_fusion), channel_id=1, source_target_pairs={{0,4},{2,6},{4,0},{6,2},{1,5},{3,7},{5,1},{7,3},{8,12},{10,14},{12... | collective-permute-start | bytes 774152 | tf_op jit(solution)/shard_map/ppermute | solution.py:80
  33.4 13.3 %collective-permute-start.3 = (bf16[4,56,576]{2,1,0:T(8,128)(2,1)S(1)}, bf16[4,56,576]{2,1,0:T(8,128)(2,1)S(1)}, u32[]{:S(2)}, u32[]{:S(2)}) collective-permute-start(bf16[4,56,576]{2,1,0:T(8,128)(2,1)S(1)} %constant_dynamic-slice_fusion), channel_id=1, source_target_pairs={{0,2},{2,0},{4,6},{6,4},{1,3},{3,1},{5,7},{7,5},{8,10},{10,8},{12,... | collective-permute-start | bytes 774152 | tf_op jit(solution)/shard_map/ppermute | solution.py:80
  33.9 15.7 %collective-permute-start.5 = (bf16[4,56,576]{2,1,0:T(8,128)(2,1)S(1)}, bf16[4,56,576]{2,1,0:T(8,128)(2,1)S(1)}, u32[]{:S(2)}, u32[]{:S(2)}) collective-permute-start(bf16[4,56,576]{2,1,0:T(8,128)(2,1)S(1)} %constant_dynamic-slice_fusion), channel_id=1, source_target_pairs={{0,6},{2,4},{4,2},{6,0},{1,7},{3,5},{5,3},{7,1},{8,14},{10,12},{12... | collective-permute-start | bytes 774152 | tf_op jit(solution)/shard_map/ppermute | solution.py:80
  35.8 18.6 %collective-permute-start.13 = (bf16[4,56,448]{2,1,0:T(8,128)(2,1)S(1)}, bf16[4,56,448]{2,1,0:T(8,128)(2,1)S(1)}, u32[]{:S(2)}, u32[]{:S(2)}) collective-permute-start(bf16[4,56,448]{2,1,0:T(8,128)(2,1)S(1)} %constant_dynamic-slice_fusion.14), channel_id=1, source_target_pairs={{0,4},{2,6},{4,0},{6,2},{1,5},{3,7},{5,1},{7,3},{8,12},{10,14},{12... | collective-permute-start | bytes 602120 | tf_op jit(solution)/shard_map/ppermute | solution.py:80
  37.1 18.3 %collective-permute-start.12 = (bf16[4,56,448]{2,1,0:T(8,128)(2,1)S(1)}, bf16[4,56,448]{2,1,0:T(8,128)(2,1)S(1)}, u32[]{:S(2)}, u32[]{:S(2)}) collective-permute-start(bf16[4,56,448]{2,1,0:T(8,128)(2,1)S(1)} %constant_dynamic-slice_fusion.14), channel_id=1, source_target_pairs={{0,2},{2,0},{4,6},{6,4},{1,3},{3,1},{5,7},{7,5},{8,10},{10,8},{12,... | collective-permute-start | bytes 602120 | tf_op jit(solution)/shard_map/ppermute | solution.py:80
  44.0 13.1 %collective-permute-start.14 = (bf16[4,56,448]{2,1,0:T(8,128)(2,1)S(1)}, bf16[4,56,448]{2,1,0:T(8,128)(2,1)S(1)}, u32[]{:S(2)}, u32[]{:S(2)}) collective-permute-start(bf16[4,56,448]{2,1,0:T(8,128)(2,1)S(1)} %constant_dynamic-slice_fusion.14), channel_id=1, source_target_pairs={{0,6},{2,4},{4,2},{6,0},{1,7},{3,5},{5,3},{7,1},{8,14},{10,12},{12... | collective-permute-start | bytes 602120 | tf_op jit(solution)/shard_map/ppermute | solution.py:80
  51.9 6.0 %collective-permute-start.8 = (bf16[272,128]{1,0:T(8,128)(2,1)S(1)}, bf16[272,128]{1,0:T(8,128)(2,1)S(1)}, u32[]{:S(2)}, u32[]{:S(2)}) collective-permute-start(bf16[272,128]{1,0:T(8,128)(2,1)S(1)} %get-tuple-element.91.refs_0_), channel_id=1, source_target_pairs={{0,6},{2,4},{4,2},{6,0},{1,7},{3,5},{5,3},{7,1},{8,14},{10,12},{12... | collective-permute-start | bytes 208904 | tf_op jit(solution)/shard_map/ppermute | solution.py:80
  53.2 5.5 %collective-permute-start.7 = (bf16[272,128]{1,0:T(8,128)(2,1)S(1)}, bf16[272,128]{1,0:T(8,128)(2,1)S(1)}, u32[]{:S(2)}, u32[]{:S(2)}) collective-permute-start(bf16[272,128]{1,0:T(8,128)(2,1)S(1)} %get-tuple-element.91.refs_0_), channel_id=1, source_target_pairs={{0,4},{2,6},{4,0},{6,2},{1,5},{3,7},{5,1},{7,3},{8,12},{10,14},{12... | collective-permute-start | bytes 208904 | tf_op jit(solution)/shard_map/ppermute | solution.py:80
  54.4 5.1 %collective-permute-start.6 = (bf16[272,128]{1,0:T(8,128)(2,1)S(1)}, bf16[272,128]{1,0:T(8,128)(2,1)S(1)}, u32[]{:S(2)}, u32[]{:S(2)}) collective-permute-start(bf16[272,128]{1,0:T(8,128)(2,1)S(1)} %get-tuple-element.91.refs_0_), channel_id=1, source_target_pairs={{0,2},{2,0},{4,6},{6,4},{1,3},{3,1},{5,7},{7,5},{8,10},{10,8},{12,... | collective-permute-start | bytes 208904 | tf_op jit(solution)/shard_map/ppermute | solution.py:80
  59.4 10.8 %collective-permute-start.11 = (bf16[128,896]{1,0:T(8,128)(2,1)S(1)}, bf16[128,896]{1,0:T(8,128)(2,1)S(1)}, u32[]{:S(2)}, u32[]{:S(2)}) collective-permute-start(bf16[128,896]{1,0:T(8,128)(2,1)S(1)} %constant_dynamic-slice_fusion.9), channel_id=1, source_target_pairs={{0,6},{2,4},{4,2},{6,0},{1,7},{3,5},{5,3},{7,1},{8,14},{10,12},{12... | collective-permute-start | bytes 688136 | tf_op jit(solution)/shard_map/ppermute | solution.py:80
  62.3 7.9 %collective-permute-start.10 = (bf16[128,896]{1,0:T(8,128)(2,1)S(1)}, bf16[128,896]{1,0:T(8,128)(2,1)S(1)}, u32[]{:S(2)}, u32[]{:S(2)}) collective-permute-start(bf16[128,896]{1,0:T(8,128)(2,1)S(1)} %constant_dynamic-slice_fusion.9), channel_id=1, source_target_pairs={{0,4},{2,6},{4,0},{6,2},{1,5},{3,7},{5,1},{7,3},{8,12},{10,14},{12... | collective-permute-start | bytes 688136 | tf_op jit(solution)/shard_map/ppermute | solution.py:80
  64.9 6.0 %collective-permute-start.9 = (bf16[128,896]{1,0:T(8,128)(2,1)S(1)}, bf16[128,896]{1,0:T(8,128)(2,1)S(1)}, u32[]{:S(2)}, u32[]{:S(2)}) collective-permute-start(bf16[128,896]{1,0:T(8,128)(2,1)S(1)} %constant_dynamic-slice_fusion.9), channel_id=1, source_target_pairs={{0,2},{2,0},{4,6},{6,4},{1,3},{3,1},{5,7},{7,5},{8,10},{10,8},{12,... | collective-permute-start | bytes 688136 | tf_op jit(solution)/shard_map/ppermute | solution.py:80
  71.6 1.9 collective-permute-start.15
  74.2 14.2 %copy-start.28 = (f32[256,896]{1,0:T(8,128)}, f32[256,896]{1,0:T(8,128)S(1)}, u32[]{:S(2)}) copy-start(f32[256,896]{1,0:T(8,128)S(1)} %broadcast_multiply_fusion) | copy-start | bytes 2752516
  75.0 9.4 %collective-permute-start.18 = (bf16[128,896]{1,0:T(8,128)(2,1)S(1)}, bf16[128,896]{1,0:T(8,128)(2,1)S(1)}, u32[]{:S(2)}, u32[]{:S(2)}) collective-permute-start(bf16[128,896]{1,0:T(8,128)(2,1)S(1)} %get-tuple-element.169), channel_id=1, source_target_pairs={{0,6},{2,4},{4,2},{6,0},{1,7},{3,5},{5,3},{7,1},{8,14},{10,12},{12... | collective-permute-start | bytes 688136 | tf_op jit(solution)/shard_map/ppermute | solution.py:80
  76.9 11.5 %collective-permute-start.17 = (bf16[128,896]{1,0:T(8,128)(2,1)S(1)}, bf16[128,896]{1,0:T(8,128)(2,1)S(1)}, u32[]{:S(2)}, u32[]{:S(2)}) collective-permute-start(bf16[128,896]{1,0:T(8,128)(2,1)S(1)} %get-tuple-element.169), channel_id=1, source_target_pairs={{0,4},{2,6},{4,0},{6,2},{1,5},{3,7},{5,1},{7,3},{8,12},{10,14},{12... | collective-permute-start | bytes 688136 | tf_op jit(solution)/shard_map/ppermute | solution.py:80
  77.8 10.7 %collective-permute-start.16 = (bf16[128,896]{1,0:T(8,128)(2,1)S(1)}, bf16[128,896]{1,0:T(8,128)(2,1)S(1)}, u32[]{:S(2)}, u32[]{:S(2)}) collective-permute-start(bf16[128,896]{1,0:T(8,128)(2,1)S(1)} %get-tuple-element.169), channel_id=1, source_target_pairs={{0,2},{2,0},{4,6},{6,4},{1,3},{3,1},{5,7},{7,5},{8,10},{10,8},{12,... | collective-permute-start | bytes 688136 | tf_op jit(solution)/shard_map/ppermute | solution.py:80
  78.5 11.2 %collective-permute-start.20 = (bf16[512,896]{1,0:T(8,128)(2,1)S(1)}, bf16[512,896]{1,0:T(8,128)(2,1)S(1)}, u32[]{:S(2)}, u32[]{:S(2)}) collective-permute-start(bf16[512,896]{1,0:T(8,128)(2,1)S(1)} %pad_maximum_fusion.2.top_one_ref), channel_id=1, source_target_pairs={{0,1},{1,0},{2,3},{3,2},{4,5},{5,4},{6,7},{7,6},{8,9},{9,8},{10,11... | collective-permute-start | bytes 2752520 | tf_op jit(solution)/shard_map/ppermute | solution.py:62
  88.6 2.5 %collective-permute-start.19 = (bf16[512,896]{1,0:T(8,128)(2,1)S(1)}, bf16[512,896]{1,0:T(8,128)(2,1)S(1)}, u32[]{:S(2)}, u32[]{:S(2)}) collective-permute-start(bf16[512,896]{1,0:T(8,128)(2,1)S(1)} %pad_maximum_fusion.4.first_ref), channel_id=1, source_target_pairs={{0,1},{1,0},{2,3},{3,2},{4,5},{5,4},{6,7},{7,6},{8,9},{9,8},{10,11... | collective-permute-start | bytes 2752520 | tf_op jit(solution)/shard_map/ppermute | solution.py:62
  113.6 2.5 %collective-permute-start.25 = (bf16[512,896]{1,0:T(8,128)(2,1)S(1)}, bf16[512,896]{1,0:T(8,128)(2,1)S(1)}, u32[]{:S(2)}, u32[]{:S(2)}) collective-permute-start(bf16[512,896]{1,0:T(8,128)(2,1)S(1)} %get-tuple-element.105), channel_id=1, source_target_pairs={{0,1},{1,0},{2,3},{3,2},{4,5},{5,4},{6,7},{7,6},{8,9},{9,8},{10,11... | collective-permute-start | bytes 2752520 | tf_op jit(solution)/shard_map/ppermute | solution.py:62
  126.7 3.8 %collective-permute-start.24 = (bf16[512,896]{1,0:T(8,128)(2,1)}, bf16[512,896]{1,0:T(8,128)(2,1)}, u32[]{:S(2)}, u32[]{:S(2)}) collective-permute-start(bf16[512,896]{1,0:T(8,128)(2,1)} %split.41), channel_id=1, source_target_pairs={{0,1},{1,0},{2,3},{3,2},{4,5},{5,4},{6,7},{7,6},{8,9},{9,8},{10,11... | collective-permute-start | bytes 2752520 | tf_op jit(solution)/shard_map/ppermute | solution.py:62
  127.0 9.4 %collective-permute-start.28 = (bf16[128,896]{1,0:T(8,128)(2,1)S(1)}, bf16[128,896]{1,0:T(8,128)(2,1)S(1)}, u32[]{:S(2)}, u32[]{:S(2)}) collective-permute-start(bf16[128,896]{1,0:T(8,128)(2,1)S(1)} %get-tuple-element.180), channel_id=1, source_target_pairs={{0,6},{2,4},{4,2},{6,0},{1,7},{3,5},{5,3},{7,1},{8,14},{10,12},{12... | collective-permute-start | bytes 688136 | tf_op jit(solution)/shard_map/ppermute | solution.py:88
  129.4 11.3 %collective-permute-start.27 = (bf16[128,896]{1,0:T(8,128)(2,1)S(1)}, bf16[128,896]{1,0:T(8,128)(2,1)S(1)}, u32[]{:S(2)}, u32[]{:S(2)}) collective-permute-start(bf16[128,896]{1,0:T(8,128)(2,1)S(1)} %get-tuple-element.181), channel_id=1, source_target_pairs={{0,4},{2,6},{4,0},{6,2},{1,5},{3,7},{5,1},{7,3},{8,12},{10,14},{12... | collective-permute-start | bytes 688136 | tf_op jit(solution)/shard_map/ppermute | solution.py:88
  130.0 10.8 %collective-permute-start.26 = (bf16[128,896]{1,0:T(8,128)(2,1)S(1)}, bf16[128,896]{1,0:T(8,128)(2,1)S(1)}, u32[]{:S(2)}, u32[]{:S(2)}) collective-permute-start(bf16[128,896]{1,0:T(8,128)(2,1)S(1)} %get-tuple-element.182), channel_id=1, source_target_pairs={{0,2},{2,0},{4,6},{6,4},{1,3},{3,1},{5,7},{7,5},{8,10},{10,8},{12,... | collective-permute-start | bytes 688136 | tf_op jit(solution)/shard_map/ppermute | solution.py:88
  140.9 4.4 %collective-permute-start.29 = (bf16[128,896]{1,0:T(8,128)(2,1)S(1)}, bf16[128,896]{1,0:T(8,128)(2,1)S(1)}, u32[]{:S(2)}, u32[]{:S(2)}) collective-permute-start(bf16[128,896]{1,0:T(8,128)(2,1)S(1)} %add_convert_fusion.5), channel_id=1, source_target_pairs={{0,1},{1,0},{2,3},{3,2},{4,5},{5,4},{6,7},{7,6},{8,9},{9,8},{10,11... | collective-permute-start | bytes 688136 | tf_op jit(solution)/shard_map/ppermute | solution.py:62
  141.8 9.3 %collective-permute-start.32 = (bf16[128,896]{1,0:T(8,128)(2,1)S(1)}, bf16[128,896]{1,0:T(8,128)(2,1)S(1)}, u32[]{:S(2)}, u32[]{:S(2)}) collective-permute-start(bf16[128,896]{1,0:T(8,128)(2,1)S(1)} %get-tuple-element.176), channel_id=1, source_target_pairs={{0,6},{2,4},{4,2},{6,0},{1,7},{3,5},{5,3},{7,1},{8,14},{10,12},{12... | collective-permute-start | bytes 688136 | tf_op jit(solution)/shard_map/ppermute | solution.py:88
  143.4 16.8 %collective-permute-start.31 = (bf16[128,896]{1,0:T(8,128)(2,1)S(1)}, bf16[128,896]{1,0:T(8,128)(2,1)S(1)}, u32[]{:S(2)}, u32[]{:S(2)}) collective-permute-start(bf16[128,896]{1,0:T(8,128)(2,1)S(1)} %get-tuple-element.177), channel_id=1, source_target_pairs={{0,4},{2,6},{4,0},{6,2},{1,5},{3,7},{5,1},{7,3},{8,12},{10,14},{12... | collective-permute-start | bytes 688136 | tf_op jit(solution)/shard_map/ppermute | solution.py:88
  144.8 16.9 %collective-permute-start.30 = (bf16[128,896]{1,0:T(8,128)(2,1)S(1)}, bf16[128,896]{1,0:T(8,128)(2,1)S(1)}, u32[]{:S(2)}, u32[]{:S(2)}) collective-permute-start(bf16[128,896]{1,0:T(8,128)(2,1)S(1)} %get-tuple-element.178), channel_id=1, source_target_pairs={{0,2},{2,0},{4,6},{6,4},{1,3},{3,1},{5,7},{7,5},{8,10},{10,8},{12,... | collective-permute-start | bytes 688136 | tf_op jit(solution)/shard_map/ppermute | solution.py:88
  147.1 22.0 %copy-start.25 = (bf16[224,448]{1,0:T(8,128)(2,1)}, bf16[224,448]{1,0:T(8,128)(2,1)S(1)}, u32[]{:S(2)}) copy-start(bf16[224,448]{1,0:T(8,128)(2,1)S(1)} %get-tuple-element.132) | copy-start | bytes 602116
  147.1 15.1 %collective-permute-start.34 = (bf16[224,448]{1,0:T(8,128)(2,1)S(1)}, bf16[224,448]{1,0:T(8,128)(2,1)S(1)}, u32[]{:S(2)}, u32[]{:S(2)}) collective-permute-start(bf16[224,448]{1,0:T(8,128)(2,1)S(1)} %get-tuple-element.118), channel_id=1, source_target_pairs={{0,2},{2,0},{4,6},{6,4},{1,3},{3,1},{5,7},{7,5},{8,10},{10,8},{12,... | collective-permute-start | bytes 602120 | tf_op jit(solution)/shard_map/ppermute | solution.py:88
  148.7 15.1 %collective-permute-start.35 = (bf16[224,448]{1,0:T(8,128)(2,1)S(1)}, bf16[224,448]{1,0:T(8,128)(2,1)S(1)}, u32[]{:S(2)}, u32[]{:S(2)}) collective-permute-start(bf16[224,448]{1,0:T(8,128)(2,1)S(1)} %get-tuple-element.122), channel_id=1, source_target_pairs={{0,4},{2,6},{4,0},{6,2},{1,5},{3,7},{5,1},{7,3},{8,12},{10,14},{12... | collective-permute-start | bytes 602120 | tf_op jit(solution)/shard_map/ppermute | solution.py:88
  151.2 18.0 %copy-start.45 = (bf16[128,896]{1,0:T(8,128)(2,1)}, bf16[128,896]{1,0:T(8,128)(2,1)S(1)}, u32[]{:S(2)}) copy-start(bf16[128,896]{1,0:T(8,128)(2,1)S(1)} %collective-permute-done.32) | copy-start | bytes 688132
  151.2 14.8 %collective-permute-start.36 = (bf16[224,448]{1,0:T(8,128)(2,1)S(1)}, bf16[224,448]{1,0:T(8,128)(2,1)S(1)}, u32[]{:S(2)}, u32[]{:S(2)}) collective-permute-start(bf16[224,448]{1,0:T(8,128)(2,1)S(1)} %get-tuple-element.123), channel_id=1, source_target_pairs={{0,6},{2,4},{4,2},{6,0},{1,7},{3,5},{5,3},{7,1},{8,14},{10,12},{12... | collective-permute-start | bytes 602120 | tf_op jit(solution)/shard_map/ppermute | solution.py:88
  160.2 7.2 %collective-permute-start.37 = (bf16[256,128]{1,0:T(8,128)(2,1)S(1)}, bf16[256,128]{1,0:T(8,128)(2,1)S(1)}, u32[]{:S(2)}, u32[]{:S(2)}) collective-permute-start(bf16[256,128]{1,0:T(8,128)(2,1)S(1)} %get-tuple-element.125), channel_id=1, source_target_pairs={{0,2},{2,0},{4,6},{6,4},{1,3},{3,1},{5,7},{7,5},{8,10},{10,8},{12,... | collective-permute-start | bytes 196616 | tf_op jit(solution)/shard_map/ppermute | solution.py:88
  161.7 5.7 %collective-permute-start.38 = (bf16[256,128]{1,0:T(8,128)(2,1)S(1)}, bf16[256,128]{1,0:T(8,128)(2,1)S(1)}, u32[]{:S(2)}, u32[]{:S(2)}) collective-permute-start(bf16[256,128]{1,0:T(8,128)(2,1)S(1)} %get-tuple-element.126), channel_id=1, source_target_pairs={{0,4},{2,6},{4,0},{6,2},{1,5},{3,7},{5,1},{7,3},{8,12},{10,14},{12... | collective-permute-start | bytes 196616 | tf_op jit(solution)/shard_map/ppermute | solution.py:88
  162.2 6.1 %collective-permute-start.39 = (bf16[256,128]{1,0:T(8,128)(2,1)S(1)}, bf16[256,128]{1,0:T(8,128)(2,1)S(1)}, u32[]{:S(2)}, u32[]{:S(2)}) collective-permute-start(bf16[256,128]{1,0:T(8,128)(2,1)S(1)} %get-tuple-element.127), channel_id=1, source_target_pairs={{0,6},{2,4},{4,2},{6,0},{1,7},{3,5},{5,3},{7,1},{8,14},{10,12},{12... | collective-permute-start | bytes 196616 | tf_op jit(solution)/shard_map/ppermute | solution.py:88
  169.2 2.8 %collective-permute-start.40 = (bf16[256,896]{1,0:T(8,128)(2,1)S(1)}, bf16[256,896]{1,0:T(8,128)(2,1)S(1)}, u32[]{:S(2)}, u32[]{:S(2)}) collective-permute-start(bf16[256,896]{1,0:T(8,128)(2,1)S(1)} %get-tuple-element.129.first_ref), channel_id=1, source_target_pairs={{0,1},{1,0},{2,3},{3,2},{4,5},{5,4},{6,7},{7,6},{8,9},{9,8},{10,11... | collective-permute-start | bytes 1376264 | tf_op jit(solution)/shard_map/ppermute | solution.py:62
  170.8 6.7 %collective-permute-start.43 = (bf16[56,448]{1,0:T(8,128)(2,1)S(1)}, bf16[56,448]{1,0:T(8,128)(2,1)S(1)}, u32[]{:S(2)}, u32[]{:S(2)}) collective-permute-start(bf16[56,448]{1,0:T(8,128)(2,1)S(1)} %get-tuple-element.196), channel_id=1, source_target_pairs={{0,24},{8,0},{16,8},{24,16},{1,25},{9,1},{17,9},{25,17},{2,26},{10... | collective-permute-start | bytes 150536 | tf_op jit(solution)/shard_map/ppermute | solution.py:126
  171.8 10.7 %collective-permute-start.42 = (bf16[56,448]{1,0:T(8,128)(2,1)S(1)}, bf16[56,448]{1,0:T(8,128)(2,1)S(1)}, u32[]{:S(2)}, u32[]{:S(2)}) collective-permute-start(bf16[56,448]{1,0:T(8,128)(2,1)S(1)} %get-tuple-element.197), channel_id=1, source_target_pairs={{0,16},{8,24},{16,0},{24,8},{1,17},{9,25},{17,1},{25,9},{2,18},{10... | collective-permute-start | bytes 150536 | tf_op jit(solution)/shard_map/ppermute | solution.py:126
  174.0 15.2 %collective-permute-start.44 = (bf16[240,576]{1,0:T(8,128)(2,1)}, bf16[240,576]{1,0:T(8,128)(2,1)S(1)}, u32[]{:S(2)}, u32[]{:S(2)}) collective-permute-start(bf16[240,576]{1,0:T(8,128)(2,1)} %get-tuple-element.139), channel_id=1, source_target_pairs={{0,2},{2,0},{4,6},{6,4},{1,3},{3,1},{5,7},{7,5},{8,10},{10,8},{12,... | collective-permute-start | bytes 829448 | tf_op jit(solution)/shard_map/ppermute | solution.py:88
  175.4 15.9 %collective-permute-start.45 = (bf16[240,576]{1,0:T(8,128)(2,1)}, bf16[240,576]{1,0:T(8,128)(2,1)S(1)}, u32[]{:S(2)}, u32[]{:S(2)}) collective-permute-start(bf16[240,576]{1,0:T(8,128)(2,1)} %get-tuple-element.140), channel_id=1, source_target_pairs={{0,4},{2,6},{4,0},{6,2},{1,5},{3,7},{5,1},{7,3},{8,12},{10,14},{12... | collective-permute-start | bytes 829448 | tf_op jit(solution)/shard_map/ppermute | solution.py:88
  176.2 24.3 %copy-start.31 = (bf16[256,896]{1,0:T(8,128)(2,1)S(1)}, bf16[256,896]{1,0:T(8,128)(2,1)}, u32[]{:S(2)}) copy-start(bf16[256,896]{1,0:T(8,128)(2,1)} %copy-done.30) | copy-start | bytes 1376260
  176.2 24.3 %copy-start.33 = (bf16[256,896]{1,0:T(8,128)(2,1)S(1)}, bf16[256,896]{1,0:T(8,128)(2,1)}, u32[]{:S(2)}) copy-start(bf16[256,896]{1,0:T(8,128)(2,1)} %copy-done.32) | copy-start | bytes 1376260
  176.2 15.1 %collective-permute-start.46 = (bf16[240,576]{1,0:T(8,128)(2,1)}, bf16[240,576]{1,0:T(8,128)(2,1)S(1)}, u32[]{:S(2)}, u32[]{:S(2)}) collective-permute-start(bf16[240,576]{1,0:T(8,128)(2,1)} %get-tuple-element.141), channel_id=1, source_target_pairs={{0,6},{2,4},{4,2},{6,0},{1,7},{3,5},{5,3},{7,1},{8,14},{10,12},{12... | collective-permute-start | bytes 829448 | tf_op jit(solution)/shard_map/ppermute | solution.py:88
  177.6 19.2 %collective-permute-start.33 = (bf16[128,896]{1,0:T(8,128)(2,1)S(1)}, bf16[128,896]{1,0:T(8,128)(2,1)}, u32[]{:S(2)}, u32[]{:S(2)}) collective-permute-start(bf16[128,896]{1,0:T(8,128)(2,1)S(1)} %add_convert_fusion.4), channel_id=1, source_target_pairs={{0,1},{1,0},{2,3},{3,2},{4,5},{5,4},{6,7},{7,6},{8,9},{9,8},{10,11... | collective-permute-start | bytes 688136 | tf_op jit(solution)/shard_map/ppermute | solution.py:62
  182.5 6.7 %collective-permute-start.41 = (bf16[56,448]{1,0:T(8,128)(2,1)S(1)}, bf16[56,448]{1,0:T(8,128)(2,1)S(1)}, u32[]{:S(2)}, u32[]{:S(2)}) collective-permute-start(bf16[56,448]{1,0:T(8,128)(2,1)S(1)} %get-tuple-element.198), channel_id=1, source_target_pairs={{0,8},{8,16},{16,24},{24,0},{1,9},{9,17},{17,25},{25,1},{2,10},{10... | collective-permute-start | bytes 150536 | tf_op jit(solution)/shard_map/ppermute | solution.py:126
  191.6 7.1 %collective-permute-start.47 = (bf16[72,576]{1,0:T(8,128)(2,1)S(1)}, bf16[72,576]{1,0:T(8,128)(2,1)S(1)}, u32[]{:S(2)}, u32[]{:S(2)}) collective-permute-start(bf16[72,576]{1,0:T(8,128)(2,1)S(1)} %get-tuple-element.143), channel_id=1, source_target_pairs={{0,8},{8,16},{16,24},{24,0},{1,9},{9,17},{17,25},{25,1},{2,10},{10... | collective-permute-start | bytes 248840 | tf_op jit(solution)/shard_map/ppermute | solution.py:126
  193.3 12.0 %collective-permute-start.50 = (bf16[56,1920]{1,0:T(8,128)(2,1)}, bf16[56,1920]{1,0:T(8,128)(2,1)S(1)}, u32[]{:S(2)}, u32[]{:S(2)}) collective-permute-start(bf16[56,1920]{1,0:T(8,128)(2,1)} %get-tuple-element.160), channel_id=1, source_target_pairs={{0,2},{2,0},{4,6},{6,4},{1,3},{3,1},{5,7},{7,5},{8,10},{10,8},{12,... | collective-permute-start | bytes 645128 | tf_op jit(solution)/shard_map/ppermute | solution.py:88
  193.9 11.5 %collective-permute-start.51 = (bf16[56,1920]{1,0:T(8,128)(2,1)}, bf16[56,1920]{1,0:T(8,128)(2,1)S(1)}, u32[]{:S(2)}, u32[]{:S(2)}) collective-permute-start(bf16[56,1920]{1,0:T(8,128)(2,1)} %get-tuple-element.161), channel_id=1, source_target_pairs={{0,4},{2,6},{4,0},{6,2},{1,5},{3,7},{5,1},{7,3},{8,12},{10,14},{12... | collective-permute-start | bytes 645128 | tf_op jit(solution)/shard_map/ppermute | solution.py:88
  195.3 10.1 %collective-permute-start.52 = (bf16[56,1920]{1,0:T(8,128)(2,1)}, bf16[56,1920]{1,0:T(8,128)(2,1)S(1)}, u32[]{:S(2)}, u32[]{:S(2)}) collective-permute-start(bf16[56,1920]{1,0:T(8,128)(2,1)} %get-tuple-element.162), channel_id=1, source_target_pairs={{0,6},{2,4},{4,2},{6,0},{1,7},{3,5},{5,3},{7,1},{8,14},{10,12},{12... | collective-permute-start | bytes 645128 | tf_op jit(solution)/shard_map/ppermute | solution.py:88
  196.8 6.5 %collective-permute-start.48 = (bf16[72,576]{1,0:T(8,128)(2,1)S(1)}, bf16[72,576]{1,0:T(8,128)(2,1)S(1)}, u32[]{:S(2)}, u32[]{:S(2)}) collective-permute-start(bf16[72,576]{1,0:T(8,128)(2,1)S(1)} %get-tuple-element.144), channel_id=1, source_target_pairs={{0,16},{8,24},{16,0},{24,8},{1,17},{9,25},{17,1},{25,9},{2,18},{10... | collective-permute-start | bytes 248840 | tf_op jit(solution)/shard_map/ppermute | solution.py:126
  198.7 4.7 %collective-permute-start.49 = (bf16[72,576]{1,0:T(8,128)(2,1)S(1)}, bf16[72,576]{1,0:T(8,128)(2,1)S(1)}, u32[]{:S(2)}, u32[]{:S(2)}) collective-permute-start(bf16[72,576]{1,0:T(8,128)(2,1)S(1)} %get-tuple-element.145), channel_id=1, source_target_pairs={{0,24},{8,0},{16,8},{24,16},{1,25},{9,1},{17,9},{25,17},{2,26},{10... | collective-permute-start | bytes 248840 | tf_op jit(solution)/shard_map/ppermute | solution.py:126
  (51 other events, 246.9 us)
Sparse Core Ops, SparseCore 0:
  32.0 68.0 all-gather.1
  121.1 65.8 reduce-scatter.1
